TPU v7x, 128 devices: a whole 4x4x4 slice. The times are simulated.
128 devices in a mesh: dp: 16 (over z, y_lo, core), tensor: 8 (over x, y_hi).
Axes of the slice: x: 4, y: 4 (y_hi: 2, y_lo: 2; y = y_hi * 2 + y_lo), z: 4, core: 2. Of those that a mesh axis runs over, the one named last changes fastest.
Arguments:
- text_rows: bfloat16 [28672, 8192], P('dp', 'tensor'), may hold values from -6 to 6
- vis_rows: bfloat16 [24576, 8192], P('dp', 'tensor'), may hold values from -6 to 6
- q_weight: bfloat16 [8192, 4096], P('dp', 'tensor'), may hold values from -40 to 40
- kv_weight: bfloat16 [8192, 2, 1024], P(None, None, 'tensor'), may hold values from -40 to 40
- q_bias: float32 [4096], P('tensor'), may hold values from -3 to 3
- kv_bias: float32 [2, 1024], P(None, 'tensor'), may hold values from -3 to 3
- norm_gain: float32 [8192], replicated, may hold values from 0.1 to 1.9
- tile_dest: int32 [16, 6], replicated, may hold values from 0 to 15, as said below
- tile_block: int32 [16, 6], P('dp'), may hold values from 0 to 6, as said below
- doc_lens: int32 [16, 4], P('dp'), may hold values from 1 to 896, 1792 in all within a row
Outputs:
- context: bfloat16 [28672, 4096], P('dp', 'tensor')
Inputs may be any that keep to these rules, and one draw needn't show every extreme that they name: `tile_dest`: each column j names every sequence once, and the 6 tiles of one vision shard go to different sequences. `tile_block`: the 6 blocks of one sequence are different.
All inputs are finite; a program needn't handle non-finite values.
Results may differ from a plain program's by a relative error of at most 0.0048.
Values may be sent and summed in bfloat16 or wider, within the bound.
No kernel may reach another device: no remote copies, remote signals or barrier semaphores. Data moves between devices by JAX's collectives and lax.ppermute only.
A program may use at most 256 MiB of HBM per device.

v0:
```python
import math

import jax
import jax.numpy as jnp
from jax import lax
from jax.sharding import PartitionSpec as P

HD = 128


rope_base = 1000000.0
eps = 1e-06
masked_score = -1e30


def rope_tables(length, width):
    half_width = width // 2
    inverse = rope_base ** (-(jnp.arange(half_width, dtype=jnp.float32) * 2.0) / width)
    angles = jnp.arange(length, dtype=jnp.float32)[:, None] * inverse[None, :]
    return (jnp.cos(angles), jnp.sin(angles))


def rotate(values, cosine_table, sine_table):
    half_width = values.shape[-1] // 2
    front = values[..., :half_width]
    back = values[..., half_width:]
    cosine = cosine_table[:, None, :]
    sine_part = sine_table[:, None, :]
    return jnp.concatenate(
        [front * cosine - back * sine_part, back * cosine + front * sine_part], axis=-1
    )


def normalize(rows, gain):
    floats = rows.astype(jnp.float32)
    spread = jnp.mean(floats * floats, axis=-1, keepdims=True)
    return (floats * lax.rsqrt(spread + eps) * gain).astype(jnp.bfloat16)


def place_tiles(rows, tiles, blocks):
    tile_len = tiles.shape[1]
    for slot_index in range(tiles.shape[0]):
        start_row = blocks[slot_index] * tile_len
        rows = lax.dynamic_update_slice_in_dim(rows, tiles[slot_index], start_row, 0)
    return rows


def local(
    text_rows,
    vis_rows,
    q_weight,
    kv_weight,
    q_bias,
    kv_bias,
    norm_gain,
    tile_dest,
    tile_block,
    doc_lens,
):
    seq_len = text_rows.shape[0]
    width = norm_gain.shape[0]
    shards = lax.axis_size("dp")
    my_index = lax.axis_index("dp")
    tile_dev = tile_dest.shape[1]
    tile_len = vis_rows.shape[0] // tile_dev
    feature_part = vis_rows.shape[1]
    own_tiles = vis_rows.reshape(tile_dev, tile_len, feature_part)
    owner_ids = jnp.arange(shards, dtype=jnp.int32)
    source_of = jnp.sum(jnp.where(tile_dest == my_index, owner_ids[:, None], 0), axis=0)
    my_dest = lax.dynamic_slice_in_dim(tile_dest, my_index, 1, 0)[0]
    send_pick = (owner_ids[:, None] == my_dest[None, :]).astype(jnp.bfloat16)
    flat_tiles = own_tiles.reshape(tile_dev, tile_len * feature_part)
    outgoing = jnp.dot(send_pick, flat_tiles, preferred_element_type=jnp.float32).astype(
        jnp.bfloat16
    )
    incoming = lax.all_to_all(
        outgoing.reshape(shards, tile_len, feature_part),
        "dp",
        split_axis=0,
        concat_axis=0,
        tiled=True,
    )
    receive_pick = (source_of[:, None] == owner_ids[None, :]).astype(jnp.bfloat16)
    chosen = jnp.dot(receive_pick, incoming.reshape(shards, -1), preferred_element_type=jnp.float32)
    my_tiles = chosen.astype(jnp.bfloat16).reshape(tile_dev, tile_len, feature_part)
    blocks = tile_block[0]
    positions = jnp.arange(seq_len, dtype=jnp.int32)
    full_text = lax.all_gather(text_rows, "tensor", axis=1, tiled=True)
    full_tiles = lax.all_gather(my_tiles, "tensor", axis=2, tiled=True)
    normed = normalize(place_tiles(full_text, full_tiles, blocks), norm_gain)
    query_width = q_weight.shape[1]
    query_sum = (
        jnp.dot(
            normed,
            lax.all_gather(q_weight, "dp", axis=0, tiled=True),
            preferred_element_type=jnp.float32,
        )
        + q_bias
    )
    key_width = kv_weight.shape[2]
    pair_sum = jnp.dot(
        normed, kv_weight.reshape(width, 2 * key_width), preferred_element_type=jnp.float32
    )
    pair_sum = pair_sum.reshape(seq_len, 2, key_width) + kv_bias
    cosine_table, sine_table = rope_tables(seq_len, HD)
    query_heads = query_width // HD
    key_heads = key_width // HD
    group_size = query_heads // key_heads
    query_rows = rotate(
        query_sum.reshape(seq_len, query_heads, HD), cosine_table, sine_table
    ).astype(jnp.bfloat16)
    key_rows = rotate(
        pair_sum[:, 0].reshape(seq_len, key_heads, HD), cosine_table, sine_table
    ).astype(jnp.bfloat16)
    value_rows = pair_sum[:, 1].reshape(seq_len, key_heads, HD).astype(jnp.bfloat16)
    grouped = query_rows.reshape(seq_len, key_heads, group_size, HD)
    ends = jnp.cumsum(doc_lens[0])
    documents = jnp.sum((positions[:, None] >= ends[None, :]).astype(jnp.int32), axis=1)
    score_scale = 1.0 / math.sqrt(HD)
    block_rows = min(896, seq_len)
    results = []
    for offset_row in range(0, seq_len, block_rows):
        query_block = grouped[offset_row : offset_row + block_rows]
        scores = (
            jnp.einsum("qhgd,khd->hgqk", query_block, key_rows, preferred_element_type=jnp.float32)
            * score_scale
        )
        block_docs = documents[offset_row : offset_row + block_rows]
        block_positions = positions[offset_row : offset_row + block_rows]
        allowed = (block_docs[:, None] == documents[None, :]) & (
            positions[None, :] <= block_positions[:, None]
        )
        scores = jnp.where(allowed[None, None], scores, masked_score)
        row_top = jnp.max(scores, axis=-1, keepdims=True)
        weights = jnp.exp(scores - row_top)
        probs = (weights / jnp.sum(weights, axis=-1, keepdims=True)).astype(jnp.bfloat16)
        mixed = jnp.einsum("hgqk,khd->qhgd", probs, value_rows, preferred_element_type=jnp.float32)
        results.append(mixed.astype(jnp.bfloat16).reshape(block_rows, query_width))
    return jnp.concatenate(results, axis=0)


def solution(mesh):
    in_specs = (
        P("dp", "tensor"),
        P("dp", "tensor"),
        P("dp", "tensor"),
        P(None, None, "tensor"),
        P("tensor"),
        P(None, "tensor"),
        P(),
        P(),
        P("dp", None),
        P("dp", None),
    )
    out_specs = P("dp", "tensor")
    return jax.shard_map(local, mesh=mesh, in_specs=in_specs, out_specs=out_specs, check_vma=False)
```

profile of v0, /device:TPU:1, one launch (start us, length us, event | category | flops | bytes accessed | tf_op | source)
XLA Modules:
  0.0 805.4 jit_solution(4240236037600504697)
XLA Ops:
  6.5 0.7 all-gather.4.cloned.1.call-update
  7.3 7.7 reshape_reshape.3
  15.0 0.2 dynamic-slice_reduce_fusion
  15.2 8.1 %convolution_convert_fusion = bf16[16,262144]{1,0:T(8,128)(2,1)} fusion(bf16[6,262144]{1,0:T(8,128)(2,1)} %reshape_reshape.3, s32[6]{0:T(128)S(1)} %dynamic-slice_reduce_fusion), kind=kOutput, calls=%fused_computation | convolution fusion | flops 54526048 | bytes 11534360 | tf_op jit(solution)/shard_map/dot_general | solution.py:73
  23.3 12.9 %copy.37 = bf16[2,8,256,1024]{3,2,1,0:T(8,128)(2,1)} copy(bf16[2,8,256,1024]{3,1,2,0:T(8,128)(2,1)} %bitcast.128) | data formatting | bytes 16777216
  36.1 8.8 %all-to-all-start = ((bf16[16,256,1024]{2,1,0:T(8,128)(2,1)}), bf16[16,256,1024]{2,1,0:T(8,128)(2,1)}, u32[]{:S(2)}, u32[]{:S(2)}) async-start(bf16[16,256,1024]{2,1,0:T(8,128)(2,1)} %bitcast.127), calls=%async_computation | async-start | bytes 16777216 | tf_op jit(solution)/shard_map/all_to_all | solution.py:76
  44.9 0.6 all-gather.6.cloned.1.call-start
  45.5 0.1 select_reduce_fusion
  45.6 151.2 %all-to-all-done = bf16[16,256,1024]{2,1,0:T(8,128)(2,1)} async-done(((bf16[16,256,1024]{2,1,0:T(8,128)(2,1)}), bf16[16,256,1024]{2,1,0:T(8,128)(2,1)}, u32[]{:S(2)}, u32[]{:S(2)}) %all-to-all-start) | async-done | bytes 8388640 | tf_op jit(solution)/shard_map/all_to_all | solution.py:76
  196.8 11.3 %copy.38 = bf16[2,8,256,1024]{3,1,2,0:T(8,128)(2,1)} copy(bf16[2,8,256,1024]{3,2,1,0:T(8,128)(2,1)} %bitcast.44) | data formatting | bytes 16777216
  208.1 4.7 convolution_convert_fusion.1
  212.8 0.0 copy-start.6
  212.8 3.4 copy.44
  216.2 0.0 all-gather.6.cloned.1.call-update
  216.2 0.2 all-gather.8.cloned.1.call-start
  216.4 0.5 all-gather.8.cloned.1.call-update
  216.9 0.7 fusion.60
  221.4 4.7 copy.43
  226.1 6.4 copy.20
  232.5 4.2 fusion.42
  236.8 0.2 reduce-window.8
  237.0 0.1 convert_reduce_fusion
  237.1 3.8 fusion.16
  240.9 131.2 %all-gather.4.cloned.1.call-done = bf16[1792,8192]{1,0:T(8,128)(2,1)} async-done(((bf16[1792,1024]{1,0:T(8,128)(2,1)}), bf16[1792,8192]{1,0:T(8,128)(2,1)}) %all-gather.4.cloned.1.call-update) | async-done | bytes 29360144 | tf_op jit(solution)/shard_map/all_gather | solution.py:88
  372.0 262.1 %all-gather.6.cloned.1.call-done = bf16[6,256,8192]{2,1,0:T(8,128)(2,1)} async-done(((bf16[6,256,1024]{2,1,0:T(8,128)(2,1)}), bf16[6,256,8192]{2,1,0:T(8,128)(2,1)}) %all-gather.6.cloned.1.call-update) | async-done | bytes 25165840 | tf_op jit(solution)/shard_map/all_gather | solution.py:89
  634.2 4.9 fusion.23
  639.1 5.6 fusion.22
  644.6 5.3 fusion.21
  650.0 2.2 fusion.20
  652.2 2.2 fusion.19
  654.4 2.2 fusion.18
  656.7 10.8 %fusion = f32[1792]{0:T(1024)S(1)} fusion(bf16[1792,8192]{1,0:T(8,128)(2,1)} %fusion.18), kind=kLoop, calls=%fused_computation.4 | loop fusion | flops 44038400 | bytes 29367296 | tf_op jit(solution)/shard_map/reduce_sum | solution.py:36
  667.5 16.4 %fusion.27 = f32[1792,2,128]{0,2,1:T(8,128)S(1)} fusion(bf16[2,128,8192]{2,1,0:T(8,128)(2,1)} %bitcast.133, f32[8192]{0:T(1024)S(1)} %copy-done.8, f32[1792]{0:T(1024)S(1)} %add_rsqrt_fusion, bf16[1792,8192]{1,0:T(8,128)(2,1)} %fusion.18, f32[2,128]{1,0:T(2,128)S(1)} %copy-done.10), kind=kOutput, calls=%fused_computation.45 | convolution fusion | flops 7575371776 | bytes 35430400 | tf_op jit(solution)/shard_map/dot_general | solution.py:101
  684.0 2.6 fusion.46
  686.6 0.3 all-gather.8.cloned.1.call-done
  686.8 25.9 %fusion.24 = f32[1792,512]{0,1:T(8,128)} fusion(bf16[8192,512]{1,0:T(8,128)(2,1)} %all-gather.8.cloned.1.call-done, bf16[1792,8192]{1,0:T(8,128)(2,1)} %fusion.18, f32[8192]{0:T(1024)S(1)} %copy-done.8, f32[1792]{0:T(1024)S(1)} %add_rsqrt_fusion, f32[512]{0:T(512)S(1)} %copy-done.9), kind=kOutput, calls=%fused_computation.43 | convolution fusion | flops 15092023296 | bytes 41460736 | tf_op jit(solution)/shard_map/dot_general | solution.py:93
  712.8 3.6 fusion.58
  716.4 3.6 copy.35
  719.9 2.5 copy.36
  722.4 4.6 subtract_convert_fusion
  727.1 11.6 %fusion.8 = (f32[4,896]{1,0:T(4,128)S(1)}, f32[1792,896,4]{1,0,2:T(8,128)}) fusion(pred[896,1792]{0,1:T(8,128)(4,1)S(1)} %get-tuple-element.12, bf16[1792,4,64]{2,0,1:T(8,128)(2,1)S(1)} %get-tuple-element.6, bf16[1792,4,64]{2,0,1:T(8,128)(2,1)S(1)} %get-tuple-element.5, bf16[1792,64]{0,1:T(8,128)(2,1)S(1)} %copy-done.3, bf16[1792,64]{0,1:T(8,128)(2,1)S(1)} %copy-done.2), kind=kOutput, calls=%fused_computation.18 | convolution fusion | flops 1666183680 | bytes 29603840 | tf_op jit(solution)/shard_map/qhgd,khd->hgqk/dot_general | solution.py:125
  738.7 11.9 %fusion.7 = (f32[4,896]{1,0:T(4,128)S(1)}, f32[1792,896,4]{1,0,2:T(8,128)}) fusion(pred[896,1792]{0,1:T(8,128)(4,1)S(1)} %copy-done.1, bf16[1792,4,64]{2,0,1:T(8,128)(2,1)S(1)} %get-tuple-element.5, bf16[1792,4,64]{2,0,1:T(8,128)(2,1)S(1)} %get-tuple-element.6, bf16[1792,64]{0,1:T(8,128)(2,1)S(1)} %copy-done.3, bf16[1792,64]{0,1:T(8,128)(2,1)S(1)} %copy-done.2), kind=kOutput, calls=%fused_computation.17 | convolution fusion | flops 1666183680 | bytes 29603840 | tf_op jit(solution)/shard_map/qhgd,khd->hgqk/dot_general | solution.py:125
  750.5 19.4 %fusion.5 = (f32[4,896]{1,0:T(4,128)S(1)}, f32[4,896]{1,0:T(4,128)S(1)}) fusion(f32[1792,896,4]{1,0,2:T(8,128)} %get-tuple-element.26, f32[4,896]{1,0:T(4,128)S(1)} %get-tuple-element.25, pred[896,1792]{0,1:T(8,128)(4,1)S(1)} %copy-done.1, f32[4,896]{1,0:T(4,128)S(1)} %get-tuple-element.23, f32[1792,896,4]{1,0,2:T(8,128)} %get-tuple-element.24, ...), kind=kLoop, calls=%fused_computation.15 | loop fusion | flops 51373056 | bytes 54648832 | tf_op jit(solution)/shard_map/reduce_sum | solution.py:136
  770.0 12.8 %fusion.30 = bf16[128,4,896]{2,0,1:T(8,128)(2,1)S(1)} fusion(f32[4,896]{1,0:T(4,128)S(1)} %get-tuple-element.27, f32[4,896]{1,0:T(4,128)S(1)} %get-tuple-element.25, f32[1792,896,4]{1,0,2:T(8,128)} %get-tuple-element.26, pred[896,1792]{0,1:T(8,128)(4,1)S(1)} %copy-done.1, f32[1792,2,128]{0,2,1:T(8,128)S(1)} %copy-done.5), kind=kOutput, calls=%fused_computation.49 | convolution fusion | flops 1676738560 | bytes 28700672 | tf_op jit(solution)/shard_map/hgqk,khd->qhgd/dot_general | solution.py:137
  782.8 0.5 copy.27
  783.3 13.2 %fusion.33 = bf16[128,4,896]{2,0,1:T(8,128)(2,1)S(1)} fusion(f32[4,896]{1,0:T(4,128)S(1)} %get-tuple-element.28, f32[4,896]{1,0:T(4,128)S(1)} %get-tuple-element.23, f32[1792,896,4]{1,0,2:T(8,128)} %get-tuple-element.24, pred[896,1792]{0,1:T(8,128)(4,1)S(1)} %get-tuple-element.12, f32[1792,2,128]{0,2,1:T(8,128)} %copy-done.4), kind=kOutput, calls=%fused_computation.50 | convolution fusion | flops 1676738560 | bytes 28700672 | tf_op jit(solution)/shard_map/hgqk,khd->qhgd/dot_general | solution.py:137
  796.5 0.5 copy.28
  797.0 1.3 pad_maximum_fusion
  (29 shorter events, 0.1 us)
Async XLA Ops:
  6.5 8.5 %copy-start.7 = (s32[16,6]{0,1:T(8,128)S(1)}, s32[16,6]{0,1:T(8,128)}, u32[]{:S(2)}) copy-start(s32[16,6]{0,1:T(8,128)} %param.17) | copy-start | bytes 1156
  6.5 365.5 %all-gather.4.cloned.1.call-start = ((), (), s32[]{:S(2)}) async-start(), calls=%async_computation.1 | async-start | bytes 33030144 | tf_op jit(solution)/shard_map/all_gather | solution.py:88
  36.1 160.7 %all-to-all-start = ((bf16[16,256,1024]{2,1,0:T(8,128)(2,1)}), bf16[16,256,1024]{2,1,0:T(8,128)(2,1)}, u32[]{:S(2)}, u32[]{:S(2)}) async-start(bf16[16,256,1024]{2,1,0:T(8,128)(2,1)} %bitcast.127), calls=%async_computation | async-start | bytes 16777216 | tf_op jit(solution)/shard_map/all_to_all | solution.py:76
  44.9 589.3 %all-gather.6.cloned.1.call-start = ((), (), s32[]{:S(2)}) async-start(), calls=%async_computation.2 | async-start | bytes 28311552 | tf_op jit(solution)/shard_map/all_gather | solution.py:89
  212.8 4.2 copy-start.6
  216.2 470.6 %all-gather.8.cloned.1.call-start = ((), (), s32[]{:S(2)}) async-start(), calls=%async_computation.3 | async-start | bytes 8912896 | tf_op jit(solution)/shard_map/all_gather | solution.py:95
  221.4 15.4 %copy-start.11 = (s32[1,4]{1,0:T(1,128)S(1)}, s32[1,4]{1,0:T(1,128)}, u32[]{:S(2)}) copy-start(s32[1,4]{1,0:T(1,128)} %param.19) | copy-start | bytes 52
  634.2 15.8 %copy-start = (bf16[6,256,8192]{2,1,0:T(8,128)(2,1)S(1)}, bf16[6,256,8192]{2,1,0:T(8,128)(2,1)}, u32[]{:S(2)}) copy-start(bf16[6,256,8192]{2,1,0:T(8,128)(2,1)} %all-gather.6.cloned.1.call-done) | copy-start | bytes 75497472
  656.7 10.8 %copy-start.8 = (f32[8192]{0:T(1024)S(1)}, f32[8192]{0:T(1024)}, u32[]{:S(2)}) copy-start(f32[8192]{0:T(1024)} %param.16) | copy-start | bytes 98308
  656.7 10.8 %copy-start.10 = (f32[2,128]{1,0:T(2,128)S(1)}, f32[2,128]{1,0:T(2,128)}, u32[]{:S(2)}) copy-start(f32[2,128]{1,0:T(2,128)} %param.15) | copy-start | bytes 3076
  667.5 19.4 %copy-start.9 = (f32[512]{0:T(512)S(1)}, f32[512]{0:T(512)}, u32[]{:S(2)}) copy-start(f32[512]{0:T(512)} %param.14) | copy-start | bytes 6148
  683.9 28.8 %copy-start.4 = (f32[1792,2,128]{0,2,1:T(8,128)}, f32[1792,2,128]{0,2,1:T(8,128)S(1)}, u32[]{:S(2)}) copy-start(f32[1792,2,128]{0,2,1:T(8,128)S(1)} %fusion.27) | copy-start | bytes 5505028
  722.4 4.6 copy-start.2
  722.4 4.6 copy-start.3
  727.0 11.6 %copy-start.1 = (pred[896,1792]{0,1:T(8,128)(4,1)S(1)}, pred[896,1792]{0,1:T(8,128)(4,1)}, u32[]{:S(2)}) copy-start(pred[896,1792]{0,1:T(8,128)(4,1)} %get-tuple-element.11) | copy-start | bytes 4816900
  750.5 19.4 %copy-start.5 = (f32[1792,2,128]{0,2,1:T(8,128)S(1)}, f32[1792,2,128]{0,2,1:T(8,128)}, u32[]{:S(2)}) copy-start(f32[1792,2,128]{0,2,1:T(8,128)} %copy-done.4) | copy-start | bytes 5505028
Sparse Core Ops, SparseCore 0:
  9.7 362.2 all-gather.3
  374.4 259.7 all-gather.5
  635.9 50.9 all-gather.7
where the time goes:
time: 814 us; the launch traced here: 805 us
  waiting for transfers between devices  546 us (67%)
  matrix products  105 us (13%)
  local copies, waits for them, and re-layouts  80.5 us (10%)
  other arithmetic  47.2 us (6%)
  between operations  17.6 us (2%)
  starting transfers between devices  9.55 us (1%)
    all_gather x1, waiting for transfers between devices, local(): full_tiles = lax.all_gather(my_tiles, 'tensor', axis=2, tiled=True)  262 us
    all_to_all x1, waiting for transfers between devices, local(): lax.all_to_all(outgoing.reshape(shards, tile_len, feature_part), 'dp', sp...  151 us
    all_gather x1, waiting for transfers between devices, local(): full_text = lax.all_gather(text_rows, 'tensor', axis=1, tiled=True)  131 us
    unnamed x30, local copies, waits for them, and re-layouts  38.3 us
    dot_general x2, matrix products, local(): jnp.einsum('hgqk,khd->qhgd', probs, value_rows, preferred_element_type=jn...  26 us
    dot_general x1, matrix products, local(): jnp.dot(normed, lax.all_gather(q_weight, 'dp', axis=0, tiled=True), prefe...  25.9 us
    dot_general x2, matrix products, local(): jnp.einsum('qhgd,khd->hgqk', query_block, key_rows, preferred_element_typ...  23.5 us
    dynamic_update_slice x6, local copies, waits for them, and re-layouts, place_tiles(): lax.dynamic_update_slice_in_dim(rows, tiles[slot_index], start_row, 0)  22.5 us
  transfers between devices with their start and end apart: 4, of which 4 were waited for; matrix products, arithmetic and copies ran while one was open for 15% of the time, Pallas kernels for 0%

commit v1 on v0

v1 whole, which is shorter than its diff:
```python
import math

import jax
import jax.numpy as jnp
from jax import lax
from jax.experimental import pallas as pl
from jax.experimental.pallas import tpu as pltpu
from jax.sharding import PartitionSpec as P

HD = 128
TILE = 256
BLOCKS = 7
SEQ = BLOCKS * TILE
HALF = SEQ // 2
PART = 1024
SLICE = 2 * PART
WIDE = 2 * HD
QUARTER = HALF // 2
VMEM = 48 * 1024 * 1024

rope_base = 1000000.0
eps = 1e-06
masked_score = -1e30


def params():
    return pltpu.CompilerParams(vmem_limit_bytes=VMEM)


def cost(flops, moved, transcendentals=0):
    return pl.CostEstimate(flops=flops, bytes_accessed=moved, transcendentals=transcendentals)


def rope_tables(length, width):
    half_width = width // 2
    inverse = rope_base ** (-(jnp.arange(half_width, dtype=jnp.float32) * 2.0) / width)
    angles = jnp.arange(length, dtype=jnp.float32)[:, None] * inverse[None, :]
    cosine, sine = jnp.cos(angles), jnp.sin(angles)
    return (
        jnp.concatenate([cosine, cosine], axis=1),
        jnp.concatenate([-sine, sine], axis=1),
    )


def shift_x(value, step):
    pairs = [
        (2 * x + high, 2 * ((x + step) % 4) + high) for x in range(4) for high in range(2)
    ]
    return lax.ppermute(value, "tensor", pairs)


def swap_high(value):
    return lax.ppermute(value, "tensor", [(t, t ^ 1) for t in range(8)])


def transpose_weight(value):
    pairs = []
    for z in range(4):
        for low in range(2):
            for core in range(2):
                for x in range(4):
                    for high in range(2):
                        source = ((z * 2 + low) * 2 + core) * 8 + x * 2 + high
                        there = (((x - z) % 4 * 2 + (low ^ high)) * 2 + core) * 8 + z * 2 + high
                        pairs.append((source, there))
    return lax.ppermute(value, ("dp", "tensor"), pairs)


def norm_kernel(picks, tiles, text, scale, gain, out):
    step = pl.program_id(0)

    def put(rows):
        out[...] = (rows[...].astype(jnp.float32) * scale[...] * gain[...]).astype(jnp.bfloat16)

    @pl.when(step < BLOCKS - 1)
    def _():
        put(tiles)

    @pl.when(step == BLOCKS - 1)
    def _():
        put(text)


def norm_rows(pick, tiles, text, scale, gain):
    grid_spec = pltpu.PrefetchScalarGridSpec(
        num_scalar_prefetch=1,
        grid=(BLOCKS,),
        in_specs=[
            pl.BlockSpec((TILE, PART), lambda i, s: (jnp.minimum(i, BLOCKS - 2), 0)),
            pl.BlockSpec((TILE, PART), lambda i, s: (s[0], 0)),
            pl.BlockSpec((TILE, 1), lambda i, s: (i, 0)),
            pl.BlockSpec((1, PART), lambda i, s: (0, 0)),
        ],
        out_specs=pl.BlockSpec((TILE, PART), lambda i, s: (i, 0)),
    )
    return pl.pallas_call(
        norm_kernel,
        grid_spec=grid_spec,
        out_shape=jax.ShapeDtypeStruct((SEQ, PART), jnp.bfloat16),
        compiler_params=params(),
        cost_estimate=cost(3 * SEQ * PART, 4 * SEQ * PART),
        name="norm_rows",
    )(pick, tiles, text, scale, gain)


def product(own, other, weight):
    both = jnp.dot(own[...], weight[0, :PART], preferred_element_type=jnp.float32)
    return both + jnp.dot(other[...], weight[0, PART:], preferred_element_type=jnp.float32)


def far_kernel(own, other, weight, first, second):
    step = pl.program_id(0)
    result = product(own, other, weight).astype(jnp.bfloat16)

    @pl.when(step < 2)
    def _():
        first[...] = result

    @pl.when(step >= 2)
    def _():
        second[...] = result


def far_parts(own, other, weight, place):
    half = jax.ShapeDtypeStruct((HALF, WIDE), jnp.bfloat16)
    return pl.pallas_call(
        far_kernel,
        grid=(4,),
        in_specs=[
            pl.BlockSpec((QUARTER, PART), lambda i: (i, 0)),
            pl.BlockSpec((QUARTER, PART), lambda i: (i, 0)),
            pl.BlockSpec((1, SLICE, WIDE), lambda i: place),
        ],
        out_specs=[
            pl.BlockSpec((QUARTER, WIDE), lambda i: (jnp.minimum(i, 1), 0)),
            pl.BlockSpec((QUARTER, WIDE), lambda i: (jnp.maximum(i - 2, 0), 0)),
        ],
        out_shape=[half, half],
        compiler_params=params(),
        cost_estimate=cost(2 * SEQ * SLICE * WIDE, 2 * SEQ * SLICE),
        name="far_parts",
    )(own, other, weight)


def near_kernel(own, other, weight_up, weight_down, got_up, got_down, up, down):
    step = pl.program_id(0)
    upward = product(own, other, weight_up)
    downward = product(own, other, weight_down)

    @pl.when(step < 2)
    def _():
        up[...] = (upward + got_up[...].astype(jnp.float32)).astype(jnp.bfloat16)
        down[...] = downward.astype(jnp.bfloat16)

    @pl.when(step >= 2)
    def _():
        up[...] = upward.astype(jnp.bfloat16)
        down[...] = (downward + got_down[...].astype(jnp.float32)).astype(jnp.bfloat16)


def near_parts(own, other, weight_up, place_up, weight_down, place_down, got_up, got_down):
    whole = jax.ShapeDtypeStruct((SEQ, WIDE), jnp.bfloat16)
    return pl.pallas_call(
        near_kernel,
        grid=(4,),
        in_specs=[
            pl.BlockSpec((QUARTER, PART), lambda i: (i, 0)),
            pl.BlockSpec((QUARTER, PART), lambda i: (i, 0)),
            pl.BlockSpec((1, SLICE, WIDE), lambda i: place_up),
            pl.BlockSpec((1, SLICE, WIDE), lambda i: place_down),
            pl.BlockSpec((QUARTER, WIDE), lambda i: (jnp.minimum(i, 1), 0)),
            pl.BlockSpec((QUARTER, WIDE), lambda i: (jnp.maximum(i - 2, 0), 0)),
        ],
        out_specs=[
            pl.BlockSpec((QUARTER, WIDE), lambda i: (i, 0)),
            pl.BlockSpec((QUARTER, WIDE), lambda i: (i, 0)),
        ],
        out_shape=[whole, whole],
        compiler_params=params(),
        cost_estimate=cost(4 * SEQ * SLICE * WIDE, 2 * SEQ * SLICE),
        name="near_parts",
    )(own, other, weight_up, weight_down, got_up, got_down)


def finish_kernel(
    rotated, dest, spots, own, other, weight, left, right, bias, cosine, sine, slots, text
):
    step = pl.program_id(0)
    total = product(own, other, weight)
    total = total + left[...].astype(jnp.float32) + right[...].astype(jnp.float32) + bias[...]
    heads = []
    for head in range(2):
        values = total[:, head * HD : (head + 1) * HD]
        if head < rotated:
            values = values * cosine[...] + pltpu.roll(values, HD // 2, 1) * sine[...]
        heads.append(values.astype(jnp.bfloat16))

    @pl.when(step < BLOCKS - 1)
    def _():
        for head in range(2):
            slots[0, :, head * HD : (head + 1) * HD] = heads[head]

    @pl.when(step == BLOCKS - 1)
    def _():
        for head in range(2):
            text[:, head * HD : (head + 1) * HD] = heads[head]


def finish(rotated, dest, spots, own, other, weight, place, left, right, bias, cosine, sine, shards):
    def row(i, d, s):
        return (i, 0)

    def spot(i, d, s):
        return (s[i], 0)

    def none(i, d, s):
        return (0, 0)

    grid_spec = pltpu.PrefetchScalarGridSpec(
        num_scalar_prefetch=2,
        grid=(BLOCKS,),
        in_specs=[
            pl.BlockSpec((TILE, PART), row),
            pl.BlockSpec((TILE, PART), row),
            pl.BlockSpec((1, SLICE, WIDE), lambda i, d, s: place),
            pl.BlockSpec((TILE, WIDE), row),
            pl.BlockSpec((TILE, WIDE), row),
            pl.BlockSpec((1, WIDE), none),
            pl.BlockSpec((TILE, HD), spot),
            pl.BlockSpec((TILE, HD), spot),
        ],
        out_specs=[
            pl.BlockSpec((1, TILE, WIDE), lambda i, d, s: (d[i], 0, 0)),
            pl.BlockSpec((TILE, WIDE), none),
        ],
    )

    def body(*refs):
        finish_kernel(rotated, *refs)

    return pl.pallas_call(
        body,
        grid_spec=grid_spec,
        out_shape=[
            jax.ShapeDtypeStruct((shards, TILE, WIDE), jnp.bfloat16),
            jax.ShapeDtypeStruct((TILE, WIDE), jnp.bfloat16),
        ],
        compiler_params=params(),
        cost_estimate=cost(2 * SEQ * SLICE * WIDE, 2 * SEQ * SLICE),
        name="finish_rows",
    )(dest, spots, own, other, weight, left, right, bias, cosine, sine)


def attend_kernel(
    has_base, source, text_at, ends, slots, text, pair_slots, pair_text, *rest
):
    base, out, keys, values = rest if has_base else (None,) + rest
    block = pl.program_id(0)

    @pl.when(block == 0)
    def _():
        for at in range(BLOCKS):
            rows = slice(at * TILE, (at + 1) * TILE)

            @pl.when(text_at[0] == at)
            def _():
                keys[rows] = pair_text[:, :HD]
                values[rows] = pair_text[:, HD:]

            @pl.when(text_at[0] != at)
            def _():
                keys[rows] = pair_slots[source[at], :, :HD]
                values[rows] = pair_slots[source[at], :, HD:]

    queries = jnp.where(block == text_at[0], text[...], slots[0])
    queries = jnp.concatenate([queries[:, :HD], queries[:, HD:]], axis=0)
    score_scale = 1.0 / math.sqrt(HD)
    first = block * TILE
    index = lax.broadcasted_iota(jnp.int32, (2 * TILE, 1), 0)
    position = first + jnp.where(index >= TILE, index - TILE, index)
    start = jnp.zeros_like(position)
    low = jnp.int32(0)
    for at in range(4):
        end = ends[at]
        start = jnp.where(position >= end, end, start)
        low = jnp.where(first >= end, end, low)
    column = lax.broadcasted_iota(jnp.int32, (2 * TILE, TILE), 1)

    def scores_of(at):
        offset = pl.multiple_of(at * TILE, TILE)
        key_block = keys[pl.ds(offset, TILE), :]
        return (
            lax.dot_general(
                queries, key_block, (((1,), (1,)), ((), ())), preferred_element_type=jnp.float32
            )
            * score_scale
        )

    def mix(weights, at):
        offset = pl.multiple_of(at * TILE, TILE)
        return jnp.dot(
            weights.astype(jnp.bfloat16),
            values[pl.ds(offset, TILE), :],
            preferred_element_type=jnp.float32,
        )

    allowed = (column + first <= position) & (column + first >= start)
    scores = jnp.where(allowed, scores_of(block), masked_score)
    top = jnp.max(scores, axis=1, keepdims=True)
    weights = jnp.exp(scores - top)
    total = jnp.sum(weights, axis=1, keepdims=True)
    mixed = mix(weights, block)

    def body(at, carry):
        top, total, mixed = carry
        scores = jnp.where(column + at * TILE >= start, scores_of(at), masked_score)
        higher = jnp.maximum(top, jnp.max(scores, axis=1, keepdims=True))
        fade = jnp.exp(top - higher)
        weights = jnp.exp(scores - higher)
        total = total * fade + jnp.sum(weights, axis=1, keepdims=True)
        return higher, total, mixed * fade + mix(weights, at)

    top, total, mixed = lax.fori_loop(low // TILE, block, body, (top, total, mixed))
    result = (mixed / total).astype(jnp.bfloat16)
    out[:, :HD] = result[:TILE]
    out[:, HD:] = result[TILE:]


def attend(source, text_at, ends, slots, text, pair_slots, pair_text, base, half):
    shards = pair_slots.shape[0]
    in_specs = [
        pl.BlockSpec((1, TILE, WIDE), lambda i, s, t, e: (s[i], 0, 0)),
        pl.BlockSpec((TILE, WIDE), lambda i, s, t, e: (0, 0)),
        pl.BlockSpec((shards, TILE, WIDE), lambda i, s, t, e: (0, 0, 0)),
        pl.BlockSpec((TILE, WIDE), lambda i, s, t, e: (0, 0)),
    ]
    operands = [source, text_at, ends, slots, text, pair_slots, pair_text]
    aliases = {}
    if base is not None:
        in_specs.append(pl.BlockSpec(memory_space=pl.ANY))
        operands.append(base)
        aliases = {7: 0}
    grid_spec = pltpu.PrefetchScalarGridSpec(
        num_scalar_prefetch=3,
        grid=(BLOCKS,),
        in_specs=in_specs,
        out_specs=pl.BlockSpec((TILE, WIDE), lambda i, s, t, e: (i, half)),
        scratch_shapes=[
            pltpu.VMEM((SEQ, HD), jnp.bfloat16),
            pltpu.VMEM((SEQ, HD), jnp.bfloat16),
        ],
    )

    def body(*refs):
        attend_kernel(base is not None, *refs)

    return pl.pallas_call(
        body,
        grid_spec=grid_spec,
        out_shape=jax.ShapeDtypeStruct((SEQ, 2 * WIDE), jnp.bfloat16),
        input_output_aliases=aliases,
        compiler_params=params(),
        cost_estimate=cost(4 * SEQ * SEQ * WIDE, 6 * SEQ * WIDE, SEQ * SEQ),
        name="attend",
    )(*operands)


def local(
    text_rows,
    vis_rows,
    q_weight,
    kv_weight,
    q_bias,
    kv_bias,
    norm_gain,
    tile_dest,
    tile_block,
    doc_lens,
):
    width = norm_gain.shape[0]
    shards = lax.axis_size("dp")
    me = lax.axis_index("dp")
    tensor_at = lax.axis_index("tensor")
    x_at, high = tensor_at // 2, tensor_at % 2

    owner_ids = jnp.arange(shards, dtype=jnp.int32)
    source_of = jnp.sum(jnp.where(tile_dest == me, owner_ids[:, None], 0), axis=0)
    my_dest = lax.dynamic_slice_in_dim(tile_dest, me, 1, 0)[0]
    blocks = tile_block[0]
    text_block = sum(range(BLOCKS)) - jnp.sum(blocks)
    all_blocks = lax.all_gather(tile_block, "dp", axis=0, tiled=True)
    sent = (owner_ids[:, None] == my_dest[None, :]).astype(jnp.int32)
    spots = jnp.concatenate([jnp.sum(sent * all_blocks, axis=0), text_block[None]])
    dest = jnp.concatenate([my_dest, my_dest[-1:]])
    at_block = blocks[None, :] == jnp.arange(BLOCKS, dtype=jnp.int32)[:, None]
    source = jnp.sum(jnp.where(at_block, source_of[None, :], 0), axis=1)
    text_at = text_block[None]
    ends = jnp.cumsum(doc_lens[0])

    text_own = lax.dynamic_slice_in_dim(text_rows, text_block * TILE, TILE, 0)
    vis_other = swap_high(vis_rows)
    text_other = swap_high(text_own)

    q_all = lax.all_gather(transpose_weight(q_weight), "dp", axis=0, tiled=True)
    q_all = q_all.reshape(4, SLICE, q_weight.shape[1])
    pairs = kv_weight.reshape(4, 2, PART, WIDE)

    def pair_slice(step):
        rows = lax.dynamic_index_in_dim(pairs, (x_at + step) % 4, 0, keepdims=False)
        first = lax.dynamic_index_in_dim(rows, high, 0, keepdims=False)
        second = lax.dynamic_index_in_dim(rows, 1 - high, 0, keepdims=False)
        return jnp.concatenate([first, second], axis=0)

    pair_weights = [pair_slice(0)] + [shift_x(pair_slice(4 - r), 4 - r) for r in range(1, 4)]
    pair_weights = [weight[None] for weight in pair_weights]

    def squares(rows):
        floats = rows.astype(jnp.float32)
        return jnp.sum(floats * floats, axis=1)

    spread = jnp.concatenate([squares(vis_rows), squares(text_own)])
    spread = lax.psum(spread, "tensor") / width
    scale = lax.rsqrt(spread + eps)[:, None]
    gains = norm_gain.reshape(8, 1, PART)
    gain_own = lax.dynamic_index_in_dim(gains, tensor_at, 0, keepdims=False)
    gain_other = lax.dynamic_index_in_dim(gains, tensor_at ^ 1, 0, keepdims=False)
    own = norm_rows(text_at, vis_rows, text_rows, scale, gain_own)
    other = norm_rows(jnp.zeros((1,), jnp.int32), vis_other, text_other, scale, gain_other)

    cosine, sine = rope_tables(SEQ, HD)
    chunks = [
        (1, [(weight, (0, 0, 0)) for weight in pair_weights], kv_bias.reshape(1, WIDE)),
        (2, [(q_all, (r, 0, 0)) for r in range(4)], q_bias[None, :WIDE]),
        (2, [(q_all, (r, 0, 1)) for r in range(4)], q_bias[None, WIDE:]),
    ]
    routed = []
    for rotated, weights, bias in chunks:
        far_up, far_down = far_parts(own, other, *weights[2])
        got_up, got_down = shift_x(far_up, 1), shift_x(far_down, 3)
        up, down = near_parts(own, other, *weights[1], *weights[3], got_up, got_down)
        left, right = shift_x(up, 1), shift_x(down, 3)
        slots, text = finish(
            rotated, dest, spots, own, other, *weights[0], left, right, bias, cosine, sine, shards
        )
        routed.append((lax.all_to_all(slots, "dp", split_axis=0, concat_axis=0, tiled=True), text))
    context = None
    for half in range(2):
        context = attend(source, text_at, ends, *routed[1 + half], *routed[0], context, half)
    return context


def solution(mesh):
    in_specs = (
        P("dp", "tensor"),
        P("dp", "tensor"),
        P("dp", "tensor"),
        P(None, None, "tensor"),
        P("tensor"),
        P(None, "tensor"),
        P(),
        P(),
        P("dp", None),
        P("dp", None),
    )
    out_specs = P("dp", "tensor")
    return jax.shard_map(local, mesh=mesh, in_specs=in_specs, out_specs=out_specs, check_vma=False)
```

time: 814 us -> 469 us (0.58)
  waiting for transfers between devices: 546 us -> 88.3 us
  blocking collectives: 0 us -> 128 us
  matrix products: 105 us -> 0 us
  Pallas kernels: 0 us -> 101 us
  starting transfers between devices: 9.55 us -> 100 us
  local copies, waits for them, and re-layouts: 80.5 us -> 22.7 us
  other arithmetic: 47.2 us -> 12.5 us
    all_gather x3 -> x1, waiting for transfers between devices: 394 us -> 0.01 us  [local(): q_all = lax.all_gather(transpose_weight(q_weight), 'dp', axis=0, tiled=True)]
    all_to_all x1 -> x3, waiting for transfers between devices: 151 us -> 12.1 us  [local(): lax.all_to_all(slots, 'dp', split_axis=0, concat_axis=0, tiled=True)]
    all_gather x0 -> x1, blocking collectives: none -> 107 us  [local(): all_blocks = lax.all_gather(tile_block, 'dp', axis=0, tiled=True)]
    dot_general x8 -> x0, matrix products: 105 us -> none  [the longest x2 26 us: local(): jnp.einsum('hgqk,khd->qhgd', probs, value_rows, preferred_element_type=jn...]
    pallas_call x0 -> x13, Pallas kernels: none -> 101 us  [the longest x2 29.1 us: attend(): pl.pallas_call(body, grid_spec=grid_spec, out_shape=jax.ShapeDtypeStruct(...]
    ppermute x0 -> x18, starting transfers between devices: none -> 76.5 us  [the longest x2 50.7 us: swap_high(): return lax.ppermute(value, 'tensor', [(t, t ^ 1) for t in range(8)])]
    ppermute x0 -> x18, waiting for transfers between devices: none -> 76.2 us  [the longest x15 76.2 us: shift_x(): return lax.ppermute(value, 'tensor', pairs)]
    unnamed x30 -> x32, local copies, waits for them, and re-layouts: 38.3 us -> 8.75 us
  transfers between devices with their start and end apart: 4 -> 22, of which waited for: 4 -> 7; matrix products, arithmetic and copies ran while one was open for 15% -> 6% of each run, Pallas kernels for 0% -> 19%
where the time goes in v1:
time: 469 us; the launch traced here: 467 us
  blocking collectives  128 us (27%)
  Pallas kernels  101 us (22%)
  starting transfers between devices  100 us (21%)
  waiting for transfers between devices  88.3 us (19%)
  local copies, waits for them, and re-layouts  22.7 us (5%)
  between operations  14.3 us (3%)
  other arithmetic  12.5 us (3%)
    all_gather x1, blocking collectives, local(): all_blocks = lax.all_gather(tile_block, 'dp', axis=0, tiled=True)  107 us
    ppermute x15, waiting for transfers between devices, shift_x(): return lax.ppermute(value, 'tensor', pairs)  76.2 us
    ppermute x2, starting transfers between devices, swap_high(): return lax.ppermute(value, 'tensor', [(t, t ^ 1) for t in range(8)])  50.7 us
    pallas_call x2, Pallas kernels, attend(): pl.pallas_call(body, grid_spec=grid_spec, out_shape=jax.ShapeDtypeStruct(...  29.1 us
    pallas_call x3, Pallas kernels, finish(): pl.pallas_call(body, grid_spec=grid_spec, out_shape=[jax.ShapeDtypeStruct...  24.3 us
    ppermute x15, starting transfers between devices, shift_x(): return lax.ppermute(value, 'tensor', pairs)  24.1 us
    all_to_all x3, starting transfers between devices, local(): lax.all_to_all(slots, 'dp', split_axis=0, concat_axis=0, tiled=True)  24 us
    pallas_call x3, Pallas kernels, near_parts(): pl.pallas_call(near_kernel, grid=(4,), in_specs=[pl.BlockSpec((QUARTER, P...  21.6 us
  transfers between devices with their start and end apart: 22, of which 7 were waited for; matrix products, arithmetic and copies ran while one was open for 6% of the time, Pallas kernels for 19%

profile of v1, /device:TPU:1, one launch (start us, length us, event | category | flops | bytes accessed | tf_op | source)
XLA Modules:
  0.0 467.1 jit_solution(17509013542866816832)
XLA Ops:
  6.5 1.7 collective-permute-start.2
  9.1 50.7 %collective-permute-start = (bf16[1536,1024]{1,0:T(8,128)(2,1)}, bf16[1536,1024]{1,0:T(8,128)(2,1)}, u32[]{:S(2)}, u32[]{:S(2)}) collective-permute-start(bf16[1536,1024]{1,0:T(8,128)(2,1)} %tiles.1), channel_id=1, source_target_pairs={{0,1},{1,0},{2,3},{3,2},{4,5},{5,4},{6,7},{7,6},{8,9},{9,8},{10,11... | collective-permute-start | bytes 9437192 | tf_op jit(solution)/shard_map/ppermute | solution.py:53
  59.8 1.3 reduce_sum.56
  61.7 1.9 multiply_reduce_fusion.1
  63.7 7.7 %reshape.68 = bf16[4,2,1024,256]{3,2,1,0:T(8,128)(2,1)} reshape(bf16[8192,2,128]{2,1,0:T(2,128)(2,1)} %param.13) | data formatting | bytes 8388608 | tf_op jit(solution)/shard_map/reshape | solution.py:406
  71.4 3.5 dynamic-slice_bitcast_fusion.1
  74.9 1.1 pad_maximum_fusion.2
  76.0 6.0 %collective-permute-start.9 = (bf16[2048,256]{1,0:T(8,128)(2,1)}, bf16[2048,256]{1,0:T(8,128)(2,1)}, u32[]{:S(2)}, u32[]{:S(2)}) collective-permute-start(bf16[2048,256]{1,0:T(8,128)(2,1)} %pad_maximum_fusion.2), channel_id=1, source_target_pairs={{0,4},{1,5},{2,6},{3,7},{4,0},{5,1},{6,2},{7,3},{8,12},{9,13},{10,... | collective-permute-start | bytes 3145736 | tf_op jit(solution)/shard_map/ppermute | solution.py:49
  83.0 1.1 pad_maximum_fusion.1
  84.1 1.5 collective-permute-start.8
  86.2 106.5 %all-gather = s32[16,1,6]{2,1,0:T(1,128)S(1)} all-gather(s32[1,1,6]{2,1,0:T(1,128)S(1)} %bitcast.54), channel_id=1, replica_groups=mesh['dp'=16,'tensor'=8] {'dp'}, dimensions={0}, use_global_device_ids=true | all-gather | bytes 408 | tf_op jit(solution)/shard_map/all_gather | solution.py:391
  192.9 21.2 %psum.7 = f32[1792]{0:T(1024)S(1)} all-reduce(f32[1792]{0:T(1024)S(1)} %pad_maximum_fusion.5), channel_id=1, replica_groups=mesh['dp'=16,'tensor'=8] {'tensor'}, use_global_device_ids=true, to_apply=%region_7.8 | all-reduce | flops 1792 | bytes 14336 | tf_op jit(solution)/shard_map/psum | solution.py:422
  214.1 1.3 broadcast_in_dim.70.scale
  216.1 1.2 copy-done.4
  217.3 5.1 %norm_rows.2.own.refs_2_ = bf16[1792,1024]{1,0:T(8,128)(2,1)} custom-call(s32[1]{0:T(128)} %bitcast.1.picks.refs_1_, bf16[1536,1024]{1,0:T(8,128)(2,1)S(1)} %copy-done.3, bf16[1792,1024]{1,0:T(8,128)(2,1)} %text.1, f32[1792,1]{1,0:T(8,128)S(1)} %copy-done.4, f32[1,1024]{1,0:T(1,128)S(1)} %get-tuple-element.54.gain), custom_call_target="tpu_custom_call" | custom-call | flops 5505024 | bytes 7340032 | tf_op jit(solution)/shard_map/norm_rows/pallas_call | solution.py:96
  222.4 6.5 %norm_rows.3.other.refs_3_ = bf16[1792,1024]{1,0:T(8,128)(2,1)} custom-call(s32[1]{0:T(128)} %constant.273.clone.1.picks, bf16[1536,1024]{1,0:T(8,128)(2,1)} %collective-permute-done.tiles, bf16[256,1024]{1,0:T(8,128)(2,1)} %collective-permute-done.1.text, f32[1792,1]{1,0:T(8,128)S(1)} %copy-done.5, f32[1,1024]{1,0:T(1,128)S(1)} %get-tuple-element.53.gain), custom_call_target="tpu_custom_call" | custom-call | flops 5505024 | bytes 7340032 | tf_op jit(solution)/shard_map/norm_rows/pallas_call | solution.py:96
  228.9 4.9 %far_parts.4 = (bf16[896,256]{1,0:T(8,128)(2,1)S(1)}, bf16[896,256]{1,0:T(8,128)(2,1)S(1)}) custom-call(bf16[1792,1024]{1,0:T(8,128)(2,1)S(1)} %copy-done, bf16[1792,1024]{1,0:T(8,128)(2,1)} %norm_rows.3.other.refs_3_, bf16[1,2048,256]{2,1,0:T(8,128)(2,1)} %bitcast.23.weight), custom_call_target="tpu_custom_call" | custom-call | flops 1879048192 | bytes 7340032 | tf_op jit(solution)/shard_map/far_parts/pallas_call | solution.py:126
  233.9 2.7 collective-permute-start.11
  237.0 6.1 %collective-permute-done.10.got_up = bf16[896,256]{1,0:T(8,128)(2,1)S(1)} collective-permute-done((bf16[896,256]{1,0:T(8,128)(2,1)S(1)}, bf16[896,256]{1,0:T(8,128)(2,1)S(1)}, u32[]{:S(2)}, u32[]{:S(2)}) %collective-permute-start.10) | collective-permute-done | bytes 458784 | tf_op jit(solution)/shard_map/ppermute | solution.py:49
  243.1 7.2 %near_parts.4 = (bf16[1792,256]{1,0:T(8,128)(2,1)S(1)}, bf16[1792,256]{1,0:T(8,128)(2,1)S(1)}) custom-call(bf16[1792,1024]{1,0:T(8,128)(2,1)} %norm_rows.2.own.refs_2_, bf16[1792,1024]{1,0:T(8,128)(2,1)} %norm_rows.3.other.refs_3_, bf16[1,2048,256]{2,1,0:T(8,128)(2,1)} %bitcast.17.weight_up, bf16[1,2048,256]{2,1,0:T(8,128)(2,1)} %bitcast.20.weight_down, ...), custom_call_target="tpu_custom_call" | custom-call | flops 3758096384 | bytes 7340032 | tf_op jit(solution)/shard_map/near_parts/pallas_call | solution.py:163
  250.4 2.7 collective-permute-start.13
  254.3 3.4 fusion.2
  258.3 10.3 %collective-permute-done.12.refs_5_ = bf16[1792,256]{1,0:T(8,128)(2,1)S(1)} collective-permute-done((bf16[1792,256]{1,0:T(8,128)(2,1)S(1)}, bf16[1792,256]{1,0:T(8,128)(2,1)S(1)}, u32[]{:S(2)}, u32[]{:S(2)}) %collective-permute-start.12) | collective-permute-done | bytes 917536 | tf_op jit(solution)/shard_map/ppermute | solution.py:49
  268.6 8.4 %finish_rows.4 = (bf16[16,256,256]{2,1,0:T(8,128)(2,1)}, bf16[256,256]{1,0:T(8,128)(2,1)S(1)}) custom-call(s32[7]{0:T(128)S(1)} %get-tuple-element.60.refs_0_, s32[7]{0:T(128)S(1)} %get-tuple-element.61.refs_1_, bf16[1792,1024]{1,0:T(8,128)(2,1)} %norm_rows.2.own.refs_2_, bf16[1792,1024]{1,0:T(8,128)(2,1)} %norm_rows.3.other.refs_3_, ...), custom_call_target="tpu_custom_call" | custom-call | flops 1879048192 | bytes 7340032 | tf_op jit(solution)/shard_map/finish_rows/pallas_call | solution.py:241
  277.0 9.9 %all-to-all-start.1 = ((bf16[16,256,256]{2,1,0:T(8,128)(2,1)}), bf16[16,256,256]{2,1,0:T(8,128)(2,1)}, u32[]{:S(2)}, u32[]{:S(2)}) async-start(bf16[16,256,256]{2,1,0:T(8,128)(2,1)} %get-tuple-element.33), calls=%async_computation.1 | async-start | bytes 4194304 | tf_op jit(solution)/shard_map/all_to_all | solution.py:445
  286.9 2.0 copy-done.1
  289.0 4.8 %far_parts.5 = (bf16[896,256]{1,0:T(8,128)(2,1)S(1)}, bf16[896,256]{1,0:T(8,128)(2,1)S(1)}) custom-call(bf16[1792,1024]{1,0:T(8,128)(2,1)S(1)} %copy-done.1, bf16[1792,1024]{1,0:T(8,128)(2,1)} %norm_rows.3.other.refs_3_, bf16[4,2048,512]{2,1,0:T(8,128)(2,1)} %bitcast.45), custom_call_target="tpu_custom_call" | custom-call | flops 1879048192 | bytes 7340032 | tf_op jit(solution)/shard_map/far_parts/pallas_call | solution.py:126
  294.4 2.2 collective-permute-start.15
  296.6 10.4 %collective-permute-done.14.got_up = bf16[896,256]{1,0:T(8,128)(2,1)S(1)} collective-permute-done((bf16[896,256]{1,0:T(8,128)(2,1)S(1)}, bf16[896,256]{1,0:T(8,128)(2,1)S(1)}, u32[]{:S(2)}, u32[]{:S(2)}) %collective-permute-start.14) | collective-permute-done | bytes 458784 | tf_op jit(solution)/shard_map/ppermute | solution.py:49
  307.0 7.2 %near_parts.5 = (bf16[1792,256]{1,0:T(8,128)(2,1)S(1)}, bf16[1792,256]{1,0:T(8,128)(2,1)S(1)}) custom-call(bf16[1792,1024]{1,0:T(8,128)(2,1)} %norm_rows.2.own.refs_2_, bf16[1792,1024]{1,0:T(8,128)(2,1)} %norm_rows.3.other.refs_3_, bf16[4,2048,512]{2,1,0:T(8,128)(2,1)} %bitcast.46, bf16[4,2048,512]{2,1,0:T(8,128)(2,1)} %bitcast.47, ...), custom_call_target="tpu_custom_call" | custom-call | flops 3758096384 | bytes 7340032 | tf_op jit(solution)/shard_map/near_parts/pallas_call | solution.py:163
  314.8 2.1 collective-permute-start.17
  316.9 19.4 %collective-permute-done.16.refs_5_ = bf16[1792,256]{1,0:T(8,128)(2,1)S(1)} collective-permute-done((bf16[1792,256]{1,0:T(8,128)(2,1)S(1)}, bf16[1792,256]{1,0:T(8,128)(2,1)S(1)}, u32[]{:S(2)}, u32[]{:S(2)}) %collective-permute-start.16) | collective-permute-done | bytes 917536 | tf_op jit(solution)/shard_map/ppermute | solution.py:49
  336.3 8.0 %finish_rows.5 = (bf16[16,256,256]{2,1,0:T(8,128)(2,1)S(1)}, bf16[256,256]{1,0:T(8,128)(2,1)S(1)}) custom-call(s32[7]{0:T(128)S(1)} %get-tuple-element.60.refs_0_, s32[7]{0:T(128)S(1)} %get-tuple-element.61.refs_1_, bf16[1792,1024]{1,0:T(8,128)(2,1)} %norm_rows.2.own.refs_2_, bf16[1792,1024]{1,0:T(8,128)(2,1)} %norm_rows.3.other.refs_3_, ...), custom_call_target="tpu_custom_call" | custom-call | flops 1879048192 | bytes 7340032 | tf_op jit(solution)/shard_map/finish_rows/pallas_call | solution.py:241
  344.3 1.3 copy-done.6
  345.6 7.2 %all-to-all-start.2 = ((bf16[16,256,256]{2,1,0:T(8,128)(2,1)}), bf16[16,256,256]{2,1,0:T(8,128)(2,1)}, u32[]{:S(2)}, u32[]{:S(2)}) async-start(bf16[16,256,256]{2,1,0:T(8,128)(2,1)} %copy-done.6), calls=%async_computation.2 | async-start | bytes 4194304 | tf_op jit(solution)/shard_map/all_to_all | solution.py:445
  352.7 2.0 copy-done.2
  354.8 4.8 %far_parts.3 = (bf16[896,256]{1,0:T(8,128)(2,1)S(1)}, bf16[896,256]{1,0:T(8,128)(2,1)S(1)}) custom-call(bf16[1792,1024]{1,0:T(8,128)(2,1)S(1)} %copy-done.2, bf16[1792,1024]{1,0:T(8,128)(2,1)} %norm_rows.3.other.refs_3_, bf16[4,2048,512]{2,1,0:T(8,128)(2,1)} %bitcast.49), custom_call_target="tpu_custom_call" | custom-call | flops 1879048192 | bytes 7340032 | tf_op jit(solution)/shard_map/far_parts/pallas_call | solution.py:126
  360.5 1.9 collective-permute-start.4
  362.4 10.5 %collective-permute-done.3.got_up = bf16[896,256]{1,0:T(8,128)(2,1)S(1)} collective-permute-done((bf16[896,256]{1,0:T(8,128)(2,1)S(1)}, bf16[896,256]{1,0:T(8,128)(2,1)S(1)}, u32[]{:S(2)}, u32[]{:S(2)}) %collective-permute-start.3) | collective-permute-done | bytes 458784 | tf_op jit(solution)/shard_map/ppermute | solution.py:49
  372.9 7.2 %near_parts.3 = (bf16[1792,256]{1,0:T(8,128)(2,1)S(1)}, bf16[1792,256]{1,0:T(8,128)(2,1)S(1)}) custom-call(bf16[1792,1024]{1,0:T(8,128)(2,1)} %norm_rows.2.own.refs_2_, bf16[1792,1024]{1,0:T(8,128)(2,1)} %norm_rows.3.other.refs_3_, bf16[4,2048,512]{2,1,0:T(8,128)(2,1)} %bitcast.50, bf16[4,2048,512]{2,1,0:T(8,128)(2,1)} %bitcast.51, ...), custom_call_target="tpu_custom_call" | custom-call | flops 3758096384 | bytes 7340032 | tf_op jit(solution)/shard_map/near_parts/pallas_call | solution.py:163
  380.8 2.0 collective-permute-start.6
  382.9 19.5 %collective-permute-done.5.refs_5_ = bf16[1792,256]{1,0:T(8,128)(2,1)S(1)} collective-permute-done((bf16[1792,256]{1,0:T(8,128)(2,1)S(1)}, bf16[1792,256]{1,0:T(8,128)(2,1)S(1)}, u32[]{:S(2)}, u32[]{:S(2)}) %collective-permute-start.5) | collective-permute-done | bytes 917536 | tf_op jit(solution)/shard_map/ppermute | solution.py:49
  402.4 7.9 %finish_rows.3 = (bf16[16,256,256]{2,1,0:T(8,128)(2,1)S(1)}, bf16[256,256]{1,0:T(8,128)(2,1)S(1)}) custom-call(s32[7]{0:T(128)S(1)} %get-tuple-element.60.refs_0_, s32[7]{0:T(128)S(1)} %get-tuple-element.61.refs_1_, bf16[1792,1024]{1,0:T(8,128)(2,1)} %norm_rows.2.own.refs_2_, bf16[1792,1024]{1,0:T(8,128)(2,1)} %norm_rows.3.other.refs_3_, ...), custom_call_target="tpu_custom_call" | custom-call | flops 1879048192 | bytes 7340032 | tf_op jit(solution)/shard_map/finish_rows/pallas_call | solution.py:241
  410.4 1.3 copy-done.7
  411.7 6.9 %all-to-all-start = ((bf16[16,256,256]{2,1,0:T(8,128)(2,1)}), bf16[16,256,256]{2,1,0:T(8,128)(2,1)S(1)}, u32[]{:S(2)}, u32[]{:S(2)}) async-start(bf16[16,256,256]{2,1,0:T(8,128)(2,1)} %copy-done.7), calls=%async_computation | async-start | bytes 4194304 | tf_op jit(solution)/shard_map/all_to_all | solution.py:445
  419.1 14.6 %attend.2.refs_7_ = bf16[1792,512]{1,0:T(8,128)(2,1)} custom-call(s32[7]{0:T(128)S(1)} %select_reduce_fusion.refs_0_, s32[1]{0:T(128)} %bitcast.1.picks.refs_1_, s32[4]{0:T(128)S(1)} %bitcast.43, bf16[16,256,256]{2,1,0:T(8,128)(2,1)} %all-to-all-done.2.refs_3_, bf16[256,256]{1,0:T(8,128)(2,1)S(1)} %get-tuple-element.40.refs_4_, ...), custom_call_target="tpu_custom_call" | custom-call | flops 3288334336 | bytes 2752512 | tf_op jit(solution)/shard_map/attend/pallas_call | solution.py:357
  433.7 12.1 %all-to-all-done.refs_3_ = bf16[16,256,256]{2,1,0:T(8,128)(2,1)S(1)} async-done(((bf16[16,256,256]{2,1,0:T(8,128)(2,1)}), bf16[16,256,256]{2,1,0:T(8,128)(2,1)S(1)}, u32[]{:S(2)}, u32[]{:S(2)}) %all-to-all-start) | async-done | bytes 2097184 | tf_op jit(solution)/shard_map/all_to_all | solution.py:445
  445.8 14.5 %attend.3 = bf16[1792,512]{1,0:T(8,128)(2,1)} custom-call(s32[7]{0:T(128)S(1)} %select_reduce_fusion.refs_0_, s32[1]{0:T(128)} %bitcast.1.picks.refs_1_, s32[4]{0:T(128)S(1)} %bitcast.44, bf16[16,256,256]{2,1,0:T(8,128)(2,1)S(1)} %all-to-all-done.refs_3_, bf16[256,256]{1,0:T(8,128)(2,1)S(1)} %get-tuple-element.28.refs_4_, ...), custom_call_target="tpu_custom_call", output_to_operand_aliasing={{}: (7, {})} | custom-call | flops 3288334336 | bytes 2752512 | tf_op jit(solution)/shard_map/attend/pallas_call | solution.py:357
  (69 shorter events, 9.2 us)
Async XLA Ops:
  6.5 280.4 %all-gather.3.cloned.1.call-start = ((), (), s32[]{:S(2)}) async-start(), calls=%async_computation.3 | async-start | bytes 8912896 | tf_op jit(solution)/shard_map/all_gather | solution.py:404
  6.5 1.7 collective-permute-start.2
  8.2 0.8 copy-start.11
  9.1 213.3 %collective-permute-start = (bf16[1536,1024]{1,0:T(8,128)(2,1)}, bf16[1536,1024]{1,0:T(8,128)(2,1)}, u32[]{:S(2)}, u32[]{:S(2)}) collective-permute-start(bf16[1536,1024]{1,0:T(8,128)(2,1)} %tiles.1), channel_id=1, source_target_pairs={{0,1},{1,0},{2,3},{3,2},{4,5},{5,4},{6,7},{7,6},{8,9},{9,8},{10,11... | collective-permute-start | bytes 9437192 | tf_op jit(solution)/shard_map/ppermute | solution.py:53
  63.7 158.7 %collective-permute-start.1 = (bf16[256,1024]{1,0:T(8,128)(2,1)}, bf16[256,1024]{1,0:T(8,128)(2,1)}, u32[]{:S(2)}, u32[]{:S(2)}) collective-permute-start(bf16[256,1024]{1,0:T(8,128)(2,1)} %get-tuple-element.42), channel_id=1, source_target_pairs={{0,1},{1,0},{2,3},{3,2},{4,5},{5,4},{6,7},{7,6},{8,9},{9,8},{10,11... | collective-permute-start | bytes 1572872 | tf_op jit(solution)/shard_map/ppermute | solution.py:53
  76.0 152.9 %collective-permute-start.9 = (bf16[2048,256]{1,0:T(8,128)(2,1)}, bf16[2048,256]{1,0:T(8,128)(2,1)}, u32[]{:S(2)}, u32[]{:S(2)}) collective-permute-start(bf16[2048,256]{1,0:T(8,128)(2,1)} %pad_maximum_fusion.2), channel_id=1, source_target_pairs={{0,4},{1,5},{2,6},{3,7},{4,0},{5,1},{6,2},{7,3},{8,12},{9,13},{10,... | collective-permute-start | bytes 3145736 | tf_op jit(solution)/shard_map/ppermute | solution.py:49
  81.9 3.6 copy-start.3
  83.0 154.1 %collective-permute-start.7 = (bf16[2048,256]{1,0:T(8,128)(2,1)}, bf16[2048,256]{1,0:T(8,128)(2,1)}, u32[]{:S(2)}, u32[]{:S(2)}) collective-permute-start(bf16[2048,256]{1,0:T(8,128)(2,1)} %pad_maximum_fusion), channel_id=1, source_target_pairs={{0,6},{1,7},{2,0},{3,1},{4,2},{5,3},{6,4},{7,5},{8,14},{9,15},{10,... | collective-permute-start | bytes 3145736 | tf_op jit(solution)/shard_map/ppermute | solution.py:49
  84.1 2.2 copy-start.14
  84.1 153.0 %collective-permute-start.8 = (bf16[2048,256]{1,0:T(8,128)(2,1)}, bf16[2048,256]{1,0:T(8,128)(2,1)}, u32[]{:S(2)}, u32[]{:S(2)}) collective-permute-start(bf16[2048,256]{1,0:T(8,128)(2,1)} %pad_maximum_fusion.1), channel_id=1, source_target_pairs={{0,2},{1,3},{2,4},{3,5},{4,6},{5,7},{6,0},{7,1},{8,10},{9,11},{10,... | collective-permute-start | bytes 3145736 | tf_op jit(solution)/shard_map/ppermute | solution.py:49
  216.1 1.2 copy-start.4
  217.3 5.1 %copy-start.5 = (f32[1792,1]{1,0:T(8,128)S(1)}, f32[1792,1]{1,0:T(8,128)}, u32[]{:S(2)}) copy-start(f32[1792,1]{1,0:T(8,128)} %broadcast_in_dim.70.scale) | copy-start | bytes 21508
  222.4 6.5 %copy-start = (bf16[1792,1024]{1,0:T(8,128)(2,1)S(1)}, bf16[1792,1024]{1,0:T(8,128)(2,1)}, u32[]{:S(2)}) copy-start(bf16[1792,1024]{1,0:T(8,128)(2,1)} %norm_rows.2.own.refs_2_) | copy-start | bytes 11010052
  228.9 7.7 %copy-start.12 = (s32[16,6]{0,1:T(8,128)S(1)}, s32[16,6]{0,1:T(8,128)}, u32[]{:S(2)}) copy-start(s32[16,6]{0,1:T(8,128)} %param.17) | copy-start | bytes 1156
  228.9 8.0 %copy-start.9 = (bf16[1024,256]{1,0:T(8,128)(2,1)S(1)}, bf16[1024,256]{1,0:T(8,128)(2,1)}, u32[]{:S(2)}) copy-start(bf16[1024,256]{1,0:T(8,128)(2,1)} %get-tuple-element.51) | copy-start | bytes 1572868
  228.9 8.0 %copy-start.10 = (bf16[1024,256]{1,0:T(8,128)(2,1)S(1)}, bf16[1024,256]{1,0:T(8,128)(2,1)}, u32[]{:S(2)}) copy-start(bf16[1024,256]{1,0:T(8,128)(2,1)} %get-tuple-element.52) | copy-start | bytes 1572868
  233.8 9.3 %collective-permute-start.10 = (bf16[896,256]{1,0:T(8,128)(2,1)S(1)}, bf16[896,256]{1,0:T(8,128)(2,1)S(1)}, u32[]{:S(2)}, u32[]{:S(2)}) collective-permute-start(bf16[896,256]{1,0:T(8,128)(2,1)S(1)} %get-tuple-element.29), channel_id=1, source_target_pairs={{0,2},{1,3},{2,4},{3,5},{4,6},{5,7},{6,0},{7,1},{8,10},{9,11},{10,... | collective-permute-start | bytes 1376264 | tf_op jit(solution)/shard_map/ppermute | solution.py:49
  233.9 9.2 %collective-permute-start.11 = (bf16[896,256]{1,0:T(8,128)(2,1)S(1)}, bf16[896,256]{1,0:T(8,128)(2,1)S(1)}, u32[]{:S(2)}, u32[]{:S(2)}) collective-permute-start(bf16[896,256]{1,0:T(8,128)(2,1)S(1)} %get-tuple-element.30), channel_id=1, source_target_pairs={{0,6},{1,7},{2,0},{3,1},{4,2},{5,3},{6,4},{7,5},{8,14},{9,15},{10,... | collective-permute-start | bytes 1376264 | tf_op jit(solution)/shard_map/ppermute | solution.py:49
  250.3 18.2 %collective-permute-start.12 = (bf16[1792,256]{1,0:T(8,128)(2,1)S(1)}, bf16[1792,256]{1,0:T(8,128)(2,1)S(1)}, u32[]{:S(2)}, u32[]{:S(2)}) collective-permute-start(bf16[1792,256]{1,0:T(8,128)(2,1)S(1)} %get-tuple-element.31), channel_id=1, source_target_pairs={{0,2},{1,3},{2,4},{3,5},{4,6},{5,7},{6,0},{7,1},{8,10},{9,11},{10,... | collective-permute-start | bytes 2752520 | tf_op jit(solution)/shard_map/ppermute | solution.py:49
  250.4 18.2 %collective-permute-start.13 = (bf16[1792,256]{1,0:T(8,128)(2,1)S(1)}, bf16[1792,256]{1,0:T(8,128)(2,1)S(1)}, u32[]{:S(2)}, u32[]{:S(2)}) collective-permute-start(bf16[1792,256]{1,0:T(8,128)(2,1)S(1)} %get-tuple-element.32), channel_id=1, source_target_pairs={{0,6},{1,7},{2,0},{3,1},{4,2},{5,3},{6,4},{7,5},{8,14},{9,15},{10,... | collective-permute-start | bytes 2752520 | tf_op jit(solution)/shard_map/ppermute | solution.py:49
  257.7 10.8 %copy-start.8 = (f32[2,128]{1,0:T(2,128)S(1)}, f32[2,128]{1,0:T(2,128)}, u32[]{:S(2)}) copy-start(f32[2,128]{1,0:T(2,128)} %param.15) | copy-start | bytes 3076
  277.0 68.6 %all-to-all-start.1 = ((bf16[16,256,256]{2,1,0:T(8,128)(2,1)}), bf16[16,256,256]{2,1,0:T(8,128)(2,1)}, u32[]{:S(2)}, u32[]{:S(2)}) async-start(bf16[16,256,256]{2,1,0:T(8,128)(2,1)} %get-tuple-element.33), calls=%async_computation.1 | async-start | bytes 4194304 | tf_op jit(solution)/shard_map/all_to_all | solution.py:445
  286.9 2.0 copy-start.1
  293.7 13.2 %collective-permute-start.14 = (bf16[896,256]{1,0:T(8,128)(2,1)S(1)}, bf16[896,256]{1,0:T(8,128)(2,1)S(1)}, u32[]{:S(2)}, u32[]{:S(2)}) collective-permute-start(bf16[896,256]{1,0:T(8,128)(2,1)S(1)} %get-tuple-element.35), channel_id=1, source_target_pairs={{0,2},{1,3},{2,4},{3,5},{4,6},{5,7},{6,0},{7,1},{8,10},{9,11},{10,... | collective-permute-start | bytes 1376264 | tf_op jit(solution)/shard_map/ppermute | solution.py:49
  294.4 22.5 %copy-start.13 = (f32[512]{0:T(512)S(1)}, f32[512]{0:T(512)}, u32[]{:S(2)}) copy-start(f32[512]{0:T(512)} %param.14) | copy-start | bytes 6148
  294.4 12.6 %collective-permute-start.15 = (bf16[896,256]{1,0:T(8,128)(2,1)S(1)}, bf16[896,256]{1,0:T(8,128)(2,1)S(1)}, u32[]{:S(2)}, u32[]{:S(2)}) collective-permute-start(bf16[896,256]{1,0:T(8,128)(2,1)S(1)} %get-tuple-element.36), channel_id=1, source_target_pairs={{0,6},{1,7},{2,0},{3,1},{4,2},{5,3},{6,4},{7,5},{8,14},{9,15},{10,... | collective-permute-start | bytes 1376264 | tf_op jit(solution)/shard_map/ppermute | solution.py:49
  314.2 22.1 %collective-permute-start.16 = (bf16[1792,256]{1,0:T(8,128)(2,1)S(1)}, bf16[1792,256]{1,0:T(8,128)(2,1)S(1)}, u32[]{:S(2)}, u32[]{:S(2)}) collective-permute-start(bf16[1792,256]{1,0:T(8,128)(2,1)S(1)} %get-tuple-element.37), channel_id=1, source_target_pairs={{0,2},{1,3},{2,4},{3,5},{4,6},{5,7},{6,0},{7,1},{8,10},{9,11},{10,... | collective-permute-start | bytes 2752520 | tf_op jit(solution)/shard_map/ppermute | solution.py:49
  314.8 21.5 %collective-permute-start.17 = (bf16[1792,256]{1,0:T(8,128)(2,1)S(1)}, bf16[1792,256]{1,0:T(8,128)(2,1)S(1)}, u32[]{:S(2)}, u32[]{:S(2)}) collective-permute-start(bf16[1792,256]{1,0:T(8,128)(2,1)S(1)} %get-tuple-element.38), channel_id=1, source_target_pairs={{0,6},{1,7},{2,0},{3,1},{4,2},{5,3},{6,4},{7,5},{8,14},{9,15},{10,... | collective-permute-start | bytes 2752520 | tf_op jit(solution)/shard_map/ppermute | solution.py:49
  344.3 1.3 copy-start.6
  345.6 66.2 %all-to-all-start.2 = ((bf16[16,256,256]{2,1,0:T(8,128)(2,1)}), bf16[16,256,256]{2,1,0:T(8,128)(2,1)}, u32[]{:S(2)}, u32[]{:S(2)}) async-start(bf16[16,256,256]{2,1,0:T(8,128)(2,1)} %copy-done.6), calls=%async_computation.2 | async-start | bytes 4194304 | tf_op jit(solution)/shard_map/all_to_all | solution.py:445
  352.7 2.0 copy-start.2
  359.6 13.4 %collective-permute-start.3 = (bf16[896,256]{1,0:T(8,128)(2,1)S(1)}, bf16[896,256]{1,0:T(8,128)(2,1)S(1)}, u32[]{:S(2)}, u32[]{:S(2)}) collective-permute-start(bf16[896,256]{1,0:T(8,128)(2,1)S(1)} %get-tuple-element.23), channel_id=1, source_target_pairs={{0,2},{1,3},{2,4},{3,5},{4,6},{5,7},{6,0},{7,1},{8,10},{9,11},{10,... | collective-permute-start | bytes 1376264 | tf_op jit(solution)/shard_map/ppermute | solution.py:49
  360.5 12.4 %collective-permute-start.4 = (bf16[896,256]{1,0:T(8,128)(2,1)S(1)}, bf16[896,256]{1,0:T(8,128)(2,1)S(1)}, u32[]{:S(2)}, u32[]{:S(2)}) collective-permute-start(bf16[896,256]{1,0:T(8,128)(2,1)S(1)} %get-tuple-element.24), channel_id=1, source_target_pairs={{0,6},{1,7},{2,0},{3,1},{4,2},{5,3},{6,4},{7,5},{8,14},{9,15},{10,... | collective-permute-start | bytes 1376264 | tf_op jit(solution)/shard_map/ppermute | solution.py:49
  380.1 22.3 %collective-permute-start.5 = (bf16[1792,256]{1,0:T(8,128)(2,1)S(1)}, bf16[1792,256]{1,0:T(8,128)(2,1)S(1)}, u32[]{:S(2)}, u32[]{:S(2)}) collective-permute-start(bf16[1792,256]{1,0:T(8,128)(2,1)S(1)} %get-tuple-element.25), channel_id=1, source_target_pairs={{0,2},{1,3},{2,4},{3,5},{4,6},{5,7},{6,0},{7,1},{8,10},{9,11},{10,... | collective-permute-start | bytes 2752520 | tf_op jit(solution)/shard_map/ppermute | solution.py:49
  380.8 21.6 %collective-permute-start.6 = (bf16[1792,256]{1,0:T(8,128)(2,1)S(1)}, bf16[1792,256]{1,0:T(8,128)(2,1)S(1)}, u32[]{:S(2)}, u32[]{:S(2)}) collective-permute-start(bf16[1792,256]{1,0:T(8,128)(2,1)S(1)} %get-tuple-element.26), channel_id=1, source_target_pairs={{0,6},{1,7},{2,0},{3,1},{4,2},{5,3},{6,4},{7,5},{8,14},{9,15},{10,... | collective-permute-start | bytes 2752520 | tf_op jit(solution)/shard_map/ppermute | solution.py:49
  410.4 1.4 copy-start.7
  411.7 6.9 %copy-start.15 = (s32[1,4]{1,0:T(1,128)S(1)}, s32[1,4]{1,0:T(1,128)}, u32[]{:S(2)}) copy-start(s32[1,4]{1,0:T(1,128)} %param.19) | copy-start | bytes 52
  411.7 34.0 %all-to-all-start = ((bf16[16,256,256]{2,1,0:T(8,128)(2,1)}), bf16[16,256,256]{2,1,0:T(8,128)(2,1)S(1)}, u32[]{:S(2)}, u32[]{:S(2)}) async-start(bf16[16,256,256]{2,1,0:T(8,128)(2,1)} %copy-done.7), calls=%async_computation | async-start | bytes 4194304 | tf_op jit(solution)/shard_map/all_to_all | solution.py:445
Sparse Core Ops, SparseCore 0:
  9.2 142.2 all-gather.2

commit v2 on v1

v2 whole, which is shorter than its diff:
```python
import functools
import math

import jax
import jax.numpy as jnp
from jax import lax
from jax.experimental import pallas as pl
from jax.experimental.pallas import tpu as pltpu
from jax.sharding import PartitionSpec as P

HD = 128
TILE = 256
BLOCKS = 7
SEQ = BLOCKS * TILE
PART = 1024
SLICE = 2 * PART
CORE_PART = PART // 2
WIDE = 2 * HD
ROWS = SEQ // 4
VMEM = 48 * 1024 * 1024

rope_base = 1000000.0
eps = 1e-06
masked_score = -1e30


def params():
    return pltpu.CompilerParams(vmem_limit_bytes=VMEM)


def cost(flops, moved, transcendentals=0):
    return pl.CostEstimate(flops=flops, bytes_accessed=moved, transcendentals=transcendentals)


def rope_tables(length, width):
    half_width = width // 2
    inverse = rope_base ** (-(jnp.arange(half_width, dtype=jnp.float32) * 2.0) / width)
    angles = jnp.arange(length, dtype=jnp.float32)[:, None] * inverse[None, :]
    cosine, sine = jnp.cos(angles), jnp.sin(angles)
    return (
        jnp.concatenate([cosine, cosine], axis=1),
        jnp.concatenate([-sine, sine], axis=1),
    )


def shift_x(value, step):
    pairs = [
        (2 * x + high, 2 * ((x + step) % 4) + high) for x in range(4) for high in range(2)
    ]
    return lax.ppermute(value, "tensor", pairs)


def swap_tensor(value, bits):
    return lax.ppermute(value, "tensor", [(t, t ^ bits) for t in range(8)])


def swap_dp(value, bits):
    return lax.ppermute(value, "dp", [(d, d ^ bits) for d in range(16)])


def shift_z(value, step):
    return lax.ppermute(value, "dp", [(d, (d + 4 * step) % 16) for d in range(16)])


def place(z, low, core, x, high):
    return ((z * 2 + low) * 2 + core) * 8 + x * 2 + high


def all_places():
    return [
        (z, low, core, x, high)
        for z in range(4)
        for low in range(2)
        for core in range(2)
        for x in range(4)
        for high in range(2)
    ]


def ring_x(value):
    pairs = [
        (place(z, low, core, x, high), place(z, low, core, (x + 1 - 2 * core) % 4, high))
        for z, low, core, x, high in all_places()
    ]
    return lax.ppermute(value, ("dp", "tensor"), pairs)


def mirror_z(value):
    pairs = [
        (place(z, low, core, x, high), place((x - z) % 4, low, core, x, high))
        for z, low, core, x, high in all_places()
    ]
    return lax.ppermute(value, ("dp", "tensor"), pairs)


def slide_x(value):
    pairs = [
        (place(z, low, core, x, high), place(z, low, core, (x - z) % 4, high))
        for z, low, core, x, high in all_places()
    ]
    return lax.ppermute(value, ("dp", "tensor"), pairs)


def lock(values, guards):
    return lax.optimization_barrier((tuple(values), tuple(guards)))[0]


def norm_kernel(bounds, begin, picks, *refs):
    parts, scale, gain, out = refs[: len(bounds)], refs[len(bounds)], refs[len(bounds) + 1], refs[-1]
    step = pl.program_id(0) + begin
    core = picks[1]

    def put(rows):
        result = (rows[...].astype(jnp.float32) * scale[...] * gain[...]).astype(jnp.bfloat16)
        front, back = result[:, :CORE_PART], result[:, CORE_PART:]

        @pl.when(core == 0)
        def _():
            out[:, :CORE_PART] = front
            out[:, CORE_PART:] = back

        @pl.when(core == 1)
        def _():
            out[:, :CORE_PART] = back
            out[:, CORE_PART:] = front

    for part, (first, last) in zip(parts, bounds):
        pl.when((step >= first) & (step < last))(functools.partial(put, part))


def norm_rows(picks, parts, bounds, scale, gain, base=None):
    begin, end = bounds[0][0], bounds[-1][1]

    def spec(part, first, last):
        if part.shape[0] == SEQ:
            return pl.BlockSpec((TILE, PART), lambda i, s: (s[0], 0))
        return pl.BlockSpec(
            (TILE, PART), lambda i, s: (jnp.clip(i + begin - first, 0, last - first - 1), 0)
        )

    aliased = [] if base is None else [base]
    grid_spec = pltpu.PrefetchScalarGridSpec(
        num_scalar_prefetch=1,
        grid=(end - begin,),
        in_specs=[spec(part, *bound) for part, bound in zip(parts, bounds)]
        + [
            pl.BlockSpec((TILE, 1), lambda i, s: (i + begin, 0)),
            pl.BlockSpec((1, PART), lambda i, s: (0, 0)),
        ]
        + later(aliased),
        out_specs=pl.BlockSpec((TILE, PART), lambda i, s: (i + begin, 0)),
    )
    rows = (end - begin) * TILE
    return pl.pallas_call(
        functools.partial(norm_kernel, bounds, begin),
        grid_spec=grid_spec,
        out_shape=jax.ShapeDtypeStruct((SEQ, PART), jnp.bfloat16),
        input_output_aliases={len(parts) + 3: 0} if aliased else {},
        compiler_params=params(),
        cost_estimate=cost(3 * rows * PART, 4 * rows * PART),
        name="norm_rows",
    )(picks, *parts, scale, gain, *aliased)


def later(tokens):
    return [pl.BlockSpec(memory_space=pl.ANY)] * len(tokens)


def part_kernel(at, own, other, kv_mine, kv_theirs, q_mine, q_theirs, *rest):
    kv_out, first_out, second_out = rest[-3:]

    def product(mine, theirs):
        total = None
        for columns, part in ((slice(0, CORE_PART), mine), (slice(CORE_PART, PART), theirs)):
            for rows, at in ((own, slice(0, CORE_PART)), (other, slice(CORE_PART, PART))):
                term = jnp.dot(rows[:, columns], part[0, at], preferred_element_type=jnp.float32)
                total = term if total is None else total + term
        return total

    kv_out[...] = product(kv_mine, kv_theirs).astype(kv_out.dtype)
    queries = product(q_mine, q_theirs).astype(first_out.dtype)
    first_out[...] = queries[:, :WIDE]
    second_out[...] = queries[:, WIDE:]


def part_of(at, own, other, kv_mine, kv_theirs, q_mine, q_theirs, dtype, tokens):
    grid_spec = pltpu.PrefetchScalarGridSpec(
        num_scalar_prefetch=1,
        grid=(SEQ // ROWS,),
        in_specs=[
            pl.BlockSpec((ROWS, PART), lambda i, s: (i, 0)),
            pl.BlockSpec((ROWS, PART), lambda i, s: (i, 0)),
            pl.BlockSpec((1, PART, WIDE), lambda i, s: (s[0], 0, 0)),
            pl.BlockSpec((1, PART, WIDE), lambda i, s: (s[0], 0, 0)),
            pl.BlockSpec((1, PART, 2 * WIDE), lambda i, s: (s[1], 0, 0)),
            pl.BlockSpec((1, PART, 2 * WIDE), lambda i, s: (s[1], 0, 0)),
            *later(tokens),
        ],
        out_specs=[pl.BlockSpec((ROWS, WIDE), lambda i, s: (i, 0))] * 3,
    )
    return pl.pallas_call(
        part_kernel,
        grid_spec=grid_spec,
        out_shape=[jax.ShapeDtypeStruct((SEQ, WIDE), dtype)] * 3,
        compiler_params=params(),
        cost_estimate=cost(6 * SEQ * SLICE * WIDE, 2 * SEQ * SLICE),
        name="part_rows",
    )(at, own, other, kv_mine, kv_theirs, q_mine, q_theirs, *tokens)


def finish_kernel(rotated, dest, spots, here, got, bias, cosine, sine, slots, text):
    step = pl.program_id(0)
    total = here[...].astype(jnp.float32) + got[...].astype(jnp.float32) + bias[...]
    heads = []
    for head in range(2):
        values = total[:, head * HD : (head + 1) * HD]
        if head < rotated:
            values = values * cosine[...] + pltpu.roll(values, HD // 2, 1) * sine[...]
        heads.append(values.astype(jnp.bfloat16))

    @pl.when(step < BLOCKS - 1)
    def _():
        for head in range(2):
            slots[0, :, head * HD : (head + 1) * HD] = heads[head]

    @pl.when(step == BLOCKS - 1)
    def _():
        for head in range(2):
            text[:, head * HD : (head + 1) * HD] = heads[head]


def finish(rotated, dest, spots, here, got, bias, tables, shards):
    def row(i, d, s):
        return (i, 0)

    def spot(i, d, s):
        return (s[i], 0)

    def none(i, d, s):
        return (0, 0)

    grid_spec = pltpu.PrefetchScalarGridSpec(
        num_scalar_prefetch=2,
        grid=(BLOCKS,),
        in_specs=[
            pl.BlockSpec((TILE, WIDE), row),
            pl.BlockSpec((TILE, WIDE), row),
            pl.BlockSpec((1, WIDE), none),
            pl.BlockSpec((TILE, HD), spot),
            pl.BlockSpec((TILE, HD), spot),
        ],
        out_specs=[
            pl.BlockSpec((1, TILE, WIDE), lambda i, d, s: (d[i], 0, 0)),
            pl.BlockSpec((TILE, WIDE), none),
        ],
    )
    return pl.pallas_call(
        functools.partial(finish_kernel, rotated),
        grid_spec=grid_spec,
        out_shape=[
            jax.ShapeDtypeStruct((shards, TILE, WIDE), jnp.bfloat16),
            jax.ShapeDtypeStruct((TILE, WIDE), jnp.bfloat16),
        ],
        compiler_params=params(),
        cost_estimate=cost(8 * SEQ * WIDE, 10 * SEQ * WIDE),
        name="finish_rows",
    )(dest, spots, here, got, bias, *tables)


def attend_kernel(
    has_base, source, text_at, ends, slots, text, pair_slots, pair_text, *rest
):
    base, out, keys, values = rest if has_base else (None,) + rest
    block = pl.program_id(0)

    @pl.when(block == 0)
    def _():
        for at in range(BLOCKS):
            rows = slice(at * TILE, (at + 1) * TILE)

            @pl.when(text_at[0] == at)
            def _():
                keys[rows] = pair_text[:, :HD]
                values[rows] = pair_text[:, HD:]

            @pl.when(text_at[0] != at)
            def _():
                keys[rows] = pair_slots[source[at], :, :HD]
                values[rows] = pair_slots[source[at], :, HD:]

    queries = jnp.where(block == text_at[0], text[...], slots[0])
    queries = jnp.concatenate([queries[:, :HD], queries[:, HD:]], axis=0)
    score_scale = 1.0 / math.sqrt(HD)
    first = block * TILE
    index = lax.broadcasted_iota(jnp.int32, (2 * TILE, 1), 0)
    position = first + jnp.where(index >= TILE, index - TILE, index)
    start = jnp.zeros_like(position)
    low = jnp.int32(0)
    for at in range(4):
        end = ends[at]
        start = jnp.where(position >= end, end, start)
        low = jnp.where(first >= end, end, low)
    column = lax.broadcasted_iota(jnp.int32, (2 * TILE, TILE), 1)

    def scores_of(at):
        offset = pl.multiple_of(at * TILE, TILE)
        key_block = keys[pl.ds(offset, TILE), :]
        return (
            lax.dot_general(
                queries, key_block, (((1,), (1,)), ((), ())), preferred_element_type=jnp.float32
            )
            * score_scale
        )

    def mix(weights, at):
        offset = pl.multiple_of(at * TILE, TILE)
        return jnp.dot(
            weights.astype(jnp.bfloat16),
            values[pl.ds(offset, TILE), :],
            preferred_element_type=jnp.float32,
        )

    allowed = (column + first <= position) & (column + first >= start)
    scores = jnp.where(allowed, scores_of(block), masked_score)
    top = jnp.max(scores, axis=1, keepdims=True)
    weights = jnp.exp(scores - top)
    total = jnp.sum(weights, axis=1, keepdims=True)
    mixed = mix(weights, block)

    def body(at, carry):
        top, total, mixed = carry
        scores = jnp.where(column + at * TILE >= start, scores_of(at), masked_score)
        higher = jnp.maximum(top, jnp.max(scores, axis=1, keepdims=True))
        fade = jnp.exp(top - higher)
        weights = jnp.exp(scores - higher)
        total = total * fade + jnp.sum(weights, axis=1, keepdims=True)
        return higher, total, mixed * fade + mix(weights, at)

    top, total, mixed = lax.fori_loop(low // TILE, block, body, (top, total, mixed))
    result = (mixed / total).astype(jnp.bfloat16)
    out[:, :HD] = result[:TILE]
    out[:, HD:] = result[TILE:]


def attend(source, text_at, ends, slots, text, pair_slots, pair_text, base, half):
    shards = pair_slots.shape[0]
    in_specs = [
        pl.BlockSpec((1, TILE, WIDE), lambda i, s, t, e: (s[i], 0, 0)),
        pl.BlockSpec((TILE, WIDE), lambda i, s, t, e: (0, 0)),
        pl.BlockSpec((shards, TILE, WIDE), lambda i, s, t, e: (0, 0, 0)),
        pl.BlockSpec((TILE, WIDE), lambda i, s, t, e: (0, 0)),
    ]
    operands = [source, text_at, ends, slots, text, pair_slots, pair_text]
    aliases = {}
    if base is not None:
        in_specs.append(pl.BlockSpec(memory_space=pl.ANY))
        operands.append(base)
        aliases = {7: 0}
    grid_spec = pltpu.PrefetchScalarGridSpec(
        num_scalar_prefetch=3,
        grid=(BLOCKS,),
        in_specs=in_specs,
        out_specs=pl.BlockSpec((TILE, WIDE), lambda i, s, t, e: (i, half)),
        scratch_shapes=[
            pltpu.VMEM((SEQ, HD), jnp.bfloat16),
            pltpu.VMEM((SEQ, HD), jnp.bfloat16),
        ],
    )

    def body(*refs):
        attend_kernel(base is not None, *refs)

    return pl.pallas_call(
        body,
        grid_spec=grid_spec,
        out_shape=jax.ShapeDtypeStruct((SEQ, 2 * WIDE), jnp.bfloat16),
        input_output_aliases=aliases,
        compiler_params=params(),
        cost_estimate=cost(4 * SEQ * SEQ * WIDE, 6 * SEQ * WIDE, SEQ * SEQ),
        name="attend",
    )(*operands)


def local(
    text_rows,
    vis_rows,
    q_weight,
    kv_weight,
    q_bias,
    kv_bias,
    norm_gain,
    tile_dest,
    tile_block,
    doc_lens,
):
    width = norm_gain.shape[0]
    shards = lax.axis_size("dp")
    me = lax.axis_index("dp")
    tensor_at = lax.axis_index("tensor")
    x_at, high = tensor_at // 2, tensor_at % 2
    z_at, low, core = me // 4, me // 2 % 2, me % 2
    blocks = tile_block[0]
    text_block = sum(range(BLOCKS)) - jnp.sum(blocks)

    def squares(rows):
        floats = rows.astype(jnp.float32)
        return jnp.sum(floats * floats, axis=1)

    pieces = kv_weight.reshape(4, 2, 2, CORE_PART, WIDE)

    def piece(step, core_at):
        rows = lax.dynamic_index_in_dim(pieces, (x_at + step) % 4, 0, keepdims=False)
        rows = lax.dynamic_index_in_dim(rows, core_at, 1, keepdims=False)
        first = lax.dynamic_index_in_dim(rows, high, 0, keepdims=False)
        second = lax.dynamic_index_in_dim(rows, 1 - high, 0, keepdims=False)
        return jnp.concatenate([first, second], axis=0)

    firsts = [vis_rows[at * TILE : (at + 1) * TILE] for at in range(3)]
    text_own = lax.dynamic_slice_in_dim(text_rows, text_block * TILE, TILE, 0)
    last = jnp.concatenate([vis_rows[3 * TILE :], text_own], axis=0)
    spread = jnp.concatenate([squares(vis_rows), squares(text_own)]).reshape(BLOCKS, TILE)

    q_here = mirror_z(q_weight)
    others = [swap_tensor(firsts[0], 1)]
    spread = spread + swap_tensor(spread, 2)
    gathered = jnp.concatenate([tile_block, swap_dp(tile_block, 2)], axis=0)

    q_here, firsts[1], spread, gathered = lock((q_here, firsts[1], spread, gathered), others)
    q_here = slide_x(q_here)
    others.append(swap_tensor(firsts[1], 1))
    spread = spread + swap_tensor(spread, 4)
    gathered = jnp.concatenate([gathered, swap_dp(gathered, 1)], axis=0)

    q_here, firsts[2], spread, gathered, kv_up, kv_down = lock(
        (q_here, firsts[2], spread, gathered, piece(1, core), piece(3, core)), others
    )
    q_low = swap_dp(q_here, 2)
    others.append(swap_tensor(firsts[2], 1))
    spread = spread + swap_tensor(spread, 1)
    kv_third = shift_x(kv_up, 1)
    kv_first = shift_x(kv_down, 3)

    own_half = low == high
    q_pair = jnp.concatenate(
        [jnp.where(own_half, q_here, q_low), jnp.where(own_half, q_low, q_here)], axis=0
    )
    q_pair, last, spread, gathered, kv_far = lock(
        (q_pair, last, spread, gathered, piece(2, core)), (*others, kv_first, kv_third)
    )
    other_last = swap_tensor(last, 1)
    q_mine = jnp.stack([q_pair] + [shift_z(q_pair, step) for step in range(1, 4)])
    kv_second = shift_x(kv_far, 2)
    kv_mine = jnp.stack([piece(0, core), kv_first, kv_second, kv_third])

    q_mine, kv_mine, gathered = lock((q_mine, kv_mine, gathered), (other_last,))
    q_theirs = swap_dp(q_mine, 1)
    kv_theirs = swap_dp(kv_mine, 1)
    for bits in (4, 8):
        gathered = jnp.concatenate([gathered, swap_dp(gathered, bits)], axis=0)
    order = [0]
    for bits in (2, 1, 4, 8):
        order = order + [entry ^ bits for entry in order]

    owner_ids = jnp.arange(shards, dtype=jnp.int32)
    source_of = jnp.sum(jnp.where(tile_dest == me, owner_ids[:, None], 0), axis=0)
    my_dest = lax.dynamic_slice_in_dim(tile_dest, me, 1, 0)[0]
    sent = (me ^ jnp.array(order, jnp.int32))[:, None] == my_dest[None, :]
    spots = jnp.concatenate([jnp.sum(jnp.where(sent, gathered, 0), axis=0), text_block[None]])
    dest = jnp.concatenate([my_dest, my_dest[-1:]])
    at_block = blocks[None, :] == jnp.arange(BLOCKS, dtype=jnp.int32)[:, None]
    source = jnp.sum(jnp.where(at_block, source_of[None, :], 0), axis=1)
    text_at = text_block[None]
    ends = jnp.cumsum(doc_lens[0])

    scale = lax.rsqrt(spread / width + eps).reshape(SEQ, 1)
    gains = norm_gain.reshape(8, 1, PART)
    gain_own = lax.dynamic_index_in_dim(gains, tensor_at, 0, keepdims=False)
    gain_other = lax.dynamic_index_in_dim(gains, tensor_at ^ 1, 0, keepdims=False)
    own = norm_rows(
        jnp.stack([text_block, core]), (vis_rows, text_rows), ((0, 6), (6, 7)), scale, gain_own
    )
    plain = jnp.stack([jnp.int32(0), core])
    other = norm_rows(plain, others, ((0, 1), (1, 2), (2, 3)), scale, gain_other)
    other = norm_rows(plain, (other_last,), ((3, 7),), scale, gain_other, other)

    def part(turn, dtype, tokens):
        group = jnp.where(core == 0, (4 - turn) % 4, turn)
        at = jnp.stack([group, (z_at - group) % 4]).astype(jnp.int32)
        return part_of(at, own, other, kv_mine, kv_theirs, q_mine, q_theirs, dtype, tokens)

    def add(here, got):
        return (here.astype(jnp.float32) + got.astype(jnp.float32)).astype(jnp.bfloat16)

    first = part(1, jnp.bfloat16, [])
    second = part(2, jnp.bfloat16, first[:1])
    third = part(3, jnp.bfloat16, second[:1])
    here = part(0, jnp.float32, third[:1])
    tables = rope_tables(SEQ, HD)
    chunks = [
        (1, kv_bias.reshape(1, WIDE)),
        (2, q_bias[None, :WIDE]),
        (2, q_bias[None, WIDE:]),
    ]
    moving = [ring_x(rows) for rows in first]
    for parts in (second, third):
        for at in range(3):
            moving[at] = ring_x(add(parts[at], moving[at]))
    routed = []
    for at, (rotated, bias) in enumerate(chunks):
        slots, text = finish(rotated, dest, spots, here[at], moving[at], bias, tables, shards)
        arrived = lax.all_to_all(slots, "dp", split_axis=0, concat_axis=0, tiled=True)
        routed.append((arrived, text))
    context = None
    for half in range(2):
        context = attend(source, text_at, ends, *routed[1 + half], *routed[0], context, half)
    return context


def solution(mesh):
    in_specs = (
        P("dp", "tensor"),
        P("dp", "tensor"),
        P("dp", "tensor"),
        P(None, None, "tensor"),
        P("tensor"),
        P(None, "tensor"),
        P(),
        P(),
        P("dp", None),
        P("dp", None),
    )
    out_specs = P("dp", "tensor")
    return jax.shard_map(local, mesh=mesh, in_specs=in_specs, out_specs=out_specs, check_vma=False)
```

time: 469 us -> 330 us (0.70)
  blocking collectives: 128 us -> 0 us
  starting transfers between devices: 100 us -> 69.6 us
  other arithmetic: 12.5 us -> 32.6 us
  waiting for transfers between devices: 88.3 us -> 108 us
  between operations: 14.3 us -> 1.13 us
  Pallas kernels: 101 us -> 90.7 us
    all_gather x1 -> x0, blocking collectives: 107 us -> none  [local(): all_blocks = lax.all_gather(tile_block, 'dp', axis=0, tiled=True)]
    ppermute x3 -> x28, waiting for transfers between devices: 0.01 us -> 76.6 us  [the longest x3 31.2 us: shift_z(): lax.ppermute(value, 'dp', [(d, (d + 4 * step) % 16) for d in range(16)])]
    ppermute x15 -> x3, waiting for transfers between devices: 76.2 us -> 8.99 us  [shift_x(): return lax.ppermute(value, 'tensor', pairs)]
    psum x1 -> x0, blocking collectives: 21.2 us -> none  [local(): spread = lax.psum(spread, 'tensor') / width]
    ppermute x15 -> x3, starting transfers between devices: 24.1 us -> 3.95 us  [shift_x(): return lax.ppermute(value, 'tensor', pairs)]
    pallas_call x11 -> x10, Pallas kernels: 71.9 us -> 61.5 us  [the longest x4 39.2 us: part_of(): pl.pallas_call(part_kernel, grid_spec=grid_spec, out_shape=[jax.ShapeDtyp...]
    convert_element_type x0 -> x6, other arithmetic: none -> 10.3 us  [add(): (here.astype(jnp.float32) + got.astype(jnp.float32)).astype(jnp.bfloat16)]
    all_to_all x3, waiting for transfers between devices: 12.1 us -> 22 us  [local(): lax.all_to_all(slots, 'dp', split_axis=0, concat_axis=0, tiled=True)]
  transfers between devices with their start and end apart: 22 -> 34, of which waited for: 7 -> 15; matrix products, arithmetic and copies ran while one was open for 6% -> 14% of each run, Pallas kernels for 19% -> 20%
where the time goes in v2:
time: 330 us; the launch traced here: 329 us
  waiting for transfers between devices  108 us (33%)
  Pallas kernels  90.7 us (27%)
  starting transfers between devices  69.6 us (21%)
  other arithmetic  32.6 us (10%)
  local copies, waits for them, and re-layouts  27.2 us (8%)
    pallas_call x4, Pallas kernels, part_of(): pl.pallas_call(part_kernel, grid_spec=grid_spec, out_shape=[jax.ShapeDtyp...  39.2 us
    ppermute x3, waiting for transfers between devices, shift_z(): lax.ppermute(value, 'dp', [(d, (d + 4 * step) % 16) for d in range(16)])  31.2 us
    pallas_call x2, Pallas kernels, attend(): pl.pallas_call(body, grid_spec=grid_spec, out_shape=jax.ShapeDtypeStruct(...  29.2 us
    ppermute x9, waiting for transfers between devices, ring_x(): return lax.ppermute(value, ('dp', 'tensor'), pairs)  27.4 us
    all_to_all x3, waiting for transfers between devices, local(): lax.all_to_all(slots, 'dp', split_axis=0, concat_axis=0, tiled=True)  22 us
    all_to_all x3, starting transfers between devices, local(): lax.all_to_all(slots, 'dp', split_axis=0, concat_axis=0, tiled=True)  18 us
    ppermute x7, waiting for transfers between devices, swap_tensor(): return lax.ppermute(value, 'tensor', [(t, t ^ bits) for t in range(8)])  17.8 us
    ppermute x7, starting transfers between devices, swap_tensor(): return lax.ppermute(value, 'tensor', [(t, t ^ bits) for t in range(8)])  13.3 us
  transfers between devices with their start and end apart: 34, of which 15 were waited for; matrix products, arithmetic and copies ran while one was open for 14% of the time, Pallas kernels for 20%

profile of v2, /device:TPU:1, one launch (start us, length us, event | category | flops | bytes accessed | tf_op | source)
XLA Modules:
  0.0 328.8 jit_solution(4613973747014750426)
XLA Ops:
  0.0 2.8 fusion.5
  2.8 3.7 %collective-permute-start.3 = (bf16[256,1024]{1,0:T(8,128)(2,1)}, bf16[256,1024]{1,0:T(8,128)(2,1)}, u32[]{:S(2)}, u32[]{:S(2)}) collective-permute-start(bf16[256,1024]{1,0:T(8,128)(2,1)} %get-tuple-element.90), channel_id=1, source_target_pairs={{0,1},{1,0},{2,3},{3,2},{4,5},{5,4},{6,7},{7,6},{8,9},{9,8},{10,11... | collective-permute-start | bytes 1572872 | tf_op jit(solution)/shard_map/ppermute | solution.py:54
  6.5 5.4 %collective-permute-start = (bf16[512,512]{1,0:T(8,128)(2,1)}, bf16[512,512]{1,0:T(8,128)(2,1)}, u32[]{:S(2)}, u32[]{:S(2)}) collective-permute-start(bf16[512,512]{1,0:T(8,128)(2,1)} %param.13), channel_id=1, source_target_pairs={{0,0},{1,1},{2,34},{3,35},{4,68},{5,69},{6,102},{7,103},{8,8},{9,9... | collective-permute-start | bytes 1572872 | tf_op jit(solution)/shard_map/ppermute | solution.py:93
  13.6 1.9 multiply_reduce_fusion.1
  16.4 7.6 %reshape.79 = bf16[4,2,2,512,256]{4,3,2,1,0:T(8,128)(2,1)} reshape(bf16[8192,2,128]{2,1,0:T(2,128)(2,1)} %param.14) | data formatting | bytes 8388608 | tf_op jit(solution)/shard_map/reshape | solution.py:409
  25.7 5.4 %collective-permute-start.4 = (bf16[512,512]{1,0:T(8,128)(2,1)}, bf16[512,512]{1,0:T(8,128)(2,1)}, u32[]{:S(2)}, u32[]{:S(2)}) collective-permute-start(bf16[512,512]{1,0:T(8,128)(2,1)} %collective-permute-done), channel_id=1, source_target_pairs={{0,0},{1,1},{2,2},{3,3},{4,4},{5,5},{6,6},{7,7},{8,8},{9,9},{10,10... | collective-permute-start | bytes 1572872 | tf_op jit(solution)/shard_map/ppermute | solution.py:101
  31.1 2.3 dynamic-slice_bitcast_fusion.1
  36.6 4.5 %collective-permute-start.5 = (f32[7,256]{1,0:T(8,128)S(1)}, f32[7,256]{1,0:T(8,128)S(1)}, u32[]{:S(2)}, u32[]{:S(2)}) collective-permute-start(f32[7,256]{1,0:T(8,128)S(1)} %add.191), channel_id=1, source_target_pairs={{0,4},{1,5},{2,6},{3,7},{4,0},{5,1},{6,2},{7,3},{8,12},{9,13},{10,... | collective-permute-start | bytes 21512 | tf_op jit(solution)/shard_map/ppermute | solution.py:54
  44.5 3.1 collective-permute-start.9
  47.6 2.2 collective-permute-start.11
  50.6 6.6 %collective-permute-done.9 = f32[7,256]{1,0:T(8,128)S(1)} collective-permute-done((f32[7,256]{1,0:T(8,128)S(1)}, f32[7,256]{1,0:T(8,128)S(1)}, u32[]{:S(2)}, u32[]{:S(2)}) %collective-permute-start.9) | collective-permute-done | bytes 7200 | tf_op jit(solution)/shard_map/ppermute | solution.py:54
  58.7 10.1 %collective-permute-done.10.refs_2_ = bf16[256,1024]{1,0:T(8,128)(2,1)} collective-permute-done((bf16[256,1024]{1,0:T(8,128)(2,1)}, bf16[256,1024]{1,0:T(8,128)(2,1)}, u32[]{:S(2)}, u32[]{:S(2)}) %collective-permute-start.10) | collective-permute-done | bytes 524320 | tf_op jit(solution)/shard_map/ppermute | solution.py:54
  69.1 2.6 collective-permute-start.14
  74.5 9.0 %collective-permute-done.16 = bf16[1024,256]{1,0:T(8,128)(2,1)S(1)} collective-permute-done((bf16[1024,256]{1,0:T(8,128)(2,1)S(1)}, bf16[1024,256]{1,0:T(8,128)(2,1)S(1)}, u32[]{:S(2)}, u32[]{:S(2)}) %collective-permute-start.16) | collective-permute-done | bytes 524320 | tf_op jit(solution)/shard_map/ppermute | solution.py:50
  83.5 2.8 pad_maximum_fusion.2.kv_mine
  86.3 8.0 %collective-permute-done.13 = bf16[1024,512]{1,0:T(8,128)(2,1)S(1)} collective-permute-done((bf16[1024,512]{1,0:T(8,128)(2,1)S(1)}, bf16[1024,512]{1,0:T(8,128)(2,1)S(1)}, u32[]{:S(2)}, u32[]{:S(2)}) %collective-permute-start.13) | collective-permute-done | bytes 1048608 | tf_op jit(solution)/shard_map/ppermute | solution.py:62
  94.3 19.2 %collective-permute-done.14 = bf16[1024,512]{1,0:T(8,128)(2,1)S(1)} collective-permute-done((bf16[1024,512]{1,0:T(8,128)(2,1)S(1)}, bf16[1024,512]{1,0:T(8,128)(2,1)S(1)}, u32[]{:S(2)}, u32[]{:S(2)}) %collective-permute-start.14) | collective-permute-done | bytes 1048608 | tf_op jit(solution)/shard_map/ppermute | solution.py:62
  113.5 4.0 %collective-permute-done.15 = bf16[1024,512]{1,0:T(8,128)(2,1)S(1)} collective-permute-done((bf16[1024,512]{1,0:T(8,128)(2,1)S(1)}, bf16[1024,512]{1,0:T(8,128)(2,1)S(1)}, u32[]{:S(2)}, u32[]{:S(2)}) %collective-permute-start.15) | collective-permute-done | bytes 1048608 | tf_op jit(solution)/shard_map/ppermute | solution.py:62
  117.5 2.3 pad_maximum_fusion.q_mine
  123.6 4.5 %fusion.2 = (f32[1792,64]{1,0:T(8,128)}, f32[1792,64]{1,0:T(8,128)}, f32[1792,64]{1,0:T(8,128)}) fusion(f32[64]{0:T(128)S(1)} %multiply_power_fusion), kind=kLoop, calls=%fused_computation.23 | loop fusion | flops 229376 | bytes 1376512 | tf_op jit(solution)/shard_map/neg | solution.py:42
  131.6 2.5 norm_rows.4.refs_3_
  135.9 5.8 %norm_rows.3.own = bf16[1792,1024]{1,0:T(8,128)(2,1)} custom-call(s32[2]{0:T(128)S(1)} %get-tuple-element.105.picks, bf16[1536,1024]{1,0:T(8,128)(2,1)S(1)} %copy-done, bf16[1792,1024]{1,0:T(8,128)(2,1)} %refs_1_.1, f32[1792,1]{1,0:T(8,128)S(1)} %bitcast.51, f32[1,1024]{1,0:T(1,128)S(1)} %get-tuple-element.95.refs_3_), custom_call_target="tpu_custom_call" | custom-call | flops 5505024 | bytes 7340032 | tf_op jit(solution)/shard_map/norm_rows/pallas_call | solution.py:154
  141.6 2.9 norm_rows.5.other
  144.5 9.9 %part_rows.4 = (bf16[1792,256]{1,0:T(8,128)(2,1)S(1)}, bf16[1792,256]{1,0:T(8,128)(2,1)}, bf16[1792,256]{1,0:T(8,128)(2,1)S(1)}) custom-call(s32[2]{0:T(128)S(1)} %get-tuple-element.108.at, bf16[1792,1024]{1,0:T(8,128)(2,1)} %norm_rows.3.own, bf16[1792,1024]{1,0:T(8,128)(2,1)} %norm_rows.5.other, bf16[4,1024,256]{2,1,0:T(8,128)(2,1)} %pad_maximum_fusion.2.kv_mine, ...), custom_call_target="tpu_custom_call" | custom-call | flops 5637144576 | bytes 7340032 | tf_op jit(solution)/shard_map/part_rows/pallas_call | solution.py:201
  158.2 2.4 pad_maximum_fusion.4
  160.6 9.5 %part_rows.5 = (bf16[1792,256]{1,0:T(8,128)(2,1)S(1)}, bf16[1792,256]{1,0:T(8,128)(2,1)S(1)}, bf16[1792,256]{1,0:T(8,128)(2,1)S(1)}) custom-call(s32[2]{0:T(128)S(1)} %get-tuple-element.107.at, bf16[1792,1024]{1,0:T(8,128)(2,1)} %norm_rows.3.own, bf16[1792,1024]{1,0:T(8,128)(2,1)} %norm_rows.5.other, bf16[4,1024,256]{2,1,0:T(8,128)(2,1)} %pad_maximum_fusion.2.kv_mine, ...), custom_call_target="tpu_custom_call" | custom-call | flops 5637144576 | bytes 7340032 | tf_op jit(solution)/shard_map/part_rows/pallas_call | solution.py:201
  171.1 2.4 add_convert_fusion.1
  174.7 3.3 %collective-permute-start.19 = (s32[8,6]{1,0:T(8,128)S(1)}, s32[8,6]{1,0:T(8,128)S(1)}, u32[]{:S(2)}, u32[]{:S(2)}) collective-permute-start(s32[8,6]{1,0:T(8,128)S(1)} %pad_add_fusion), channel_id=1, source_target_pairs={{0,64},{8,72},{16,80},{24,88},{32,96},{40,104},{48,112},{56,120},{... | collective-permute-start | bytes 584 | tf_op jit(solution)/shard_map/ppermute | solution.py:58
  181.3 9.5 %part_rows.6 = (bf16[1792,256]{1,0:T(8,128)(2,1)S(1)}, bf16[1792,256]{1,0:T(8,128)(2,1)S(1)}, bf16[1792,256]{1,0:T(8,128)(2,1)S(1)}) custom-call(s32[2]{0:T(128)S(1)} %get-tuple-element.106.at, bf16[1792,1024]{1,0:T(8,128)(2,1)} %norm_rows.3.own, bf16[1792,1024]{1,0:T(8,128)(2,1)} %norm_rows.5.other, bf16[4,1024,256]{2,1,0:T(8,128)(2,1)} %pad_maximum_fusion.2.kv_mine, ...), custom_call_target="tpu_custom_call" | custom-call | flops 5637144576 | bytes 7340032 | tf_op jit(solution)/shard_map/part_rows/pallas_call | solution.py:201
  190.9 2.1 add_convert_fusion
  194.1 1.9 collective-permute-done.25
  197.4 2.0 collective-permute-start.26
  199.4 10.3 %part_rows.7 = (f32[1792,256]{1,0:T(8,128)S(1)}, f32[1792,256]{1,0:T(8,128)S(1)}, f32[1792,256]{1,0:T(8,128)}) custom-call(s32[2]{0:T(128)S(1)} %get-tuple-element.102.at, bf16[1792,1024]{1,0:T(8,128)(2,1)} %norm_rows.3.own, bf16[1792,1024]{1,0:T(8,128)(2,1)} %norm_rows.5.other, bf16[4,1024,256]{2,1,0:T(8,128)(2,1)} %pad_maximum_fusion.2.kv_mine, ...), custom_call_target="tpu_custom_call" | custom-call | flops 5637144576 | bytes 7340032 | tf_op jit(solution)/shard_map/part_rows/pallas_call | solution.py:201
  210.9 3.8 %finish_rows.5 = (bf16[16,256,256]{2,1,0:T(8,128)(2,1)}, bf16[256,256]{1,0:T(8,128)(2,1)S(1)}) custom-call(s32[7]{0:T(128)S(1)} %get-tuple-element.103.dest, s32[7]{0:T(128)S(1)} %get-tuple-element.104.spots, f32[1792,256]{1,0:T(8,128)S(1)} %get-tuple-element.71.here, bf16[1792,256]{1,0:T(8,128)(2,1)S(1)} %collective-permute-done.30.got, ...), custom_call_target="tpu_custom_call" | custom-call | flops 3670016 | bytes 4587520 | tf_op jit(solution)/shard_map/finish_rows/pallas_call | solution.py:257
  214.7 6.4 %all-to-all-start.2 = ((bf16[16,256,256]{2,1,0:T(8,128)(2,1)}), bf16[16,256,256]{2,1,0:T(8,128)(2,1)}, u32[]{:S(2)}, u32[]{:S(2)}) async-start(bf16[16,256,256]{2,1,0:T(8,128)(2,1)} %get-tuple-element.75), calls=%async_computation.2 | async-start | bytes 4194304 | tf_op jit(solution)/shard_map/all_to_all | solution.py:511
  221.1 2.2 collective-permute-start.22
  225.1 8.9 %collective-permute-done.22 = bf16[1792,256]{1,0:T(8,128)(2,1)S(1)} collective-permute-done((bf16[1792,256]{1,0:T(8,128)(2,1)}, bf16[1792,256]{1,0:T(8,128)(2,1)S(1)}, u32[]{:S(2)}, u32[]{:S(2)}) %collective-permute-start.22) | collective-permute-done | bytes 917536 | tf_op jit(solution)/shard_map/ppermute | solution.py:85
  235.3 3.3 %collective-permute-start.23 = (bf16[1792,256]{1,0:T(8,128)(2,1)}, bf16[1792,256]{1,0:T(8,128)(2,1)}, u32[]{:S(2)}, u32[]{:S(2)}) collective-permute-start(bf16[1792,256]{1,0:T(8,128)(2,1)} %add_convert_fusion.5), channel_id=1, source_target_pairs={{0,2},{1,3},{2,4},{3,5},{4,6},{5,7},{6,0},{7,1},{8,14},{9,15},{10,... | collective-permute-start | bytes 2752520 | tf_op jit(solution)/shard_map/ppermute | solution.py:85
  238.6 5.3 %collective-permute-done.27.got = bf16[1792,256]{1,0:T(8,128)(2,1)S(1)} collective-permute-done((bf16[1792,256]{1,0:T(8,128)(2,1)S(1)}, bf16[1792,256]{1,0:T(8,128)(2,1)S(1)}, u32[]{:S(2)}, u32[]{:S(2)}) %collective-permute-start.27) | collective-permute-done | bytes 917536 | tf_op jit(solution)/shard_map/ppermute | solution.py:85
  243.8 3.7 %finish_rows.4 = (bf16[16,256,256]{2,1,0:T(8,128)(2,1)}, bf16[256,256]{1,0:T(8,128)(2,1)S(1)}) custom-call(s32[7]{0:T(128)S(1)} %get-tuple-element.103.dest, s32[7]{0:T(128)S(1)} %get-tuple-element.104.spots, f32[1792,256]{1,0:T(8,128)S(1)} %copy-done.8, bf16[1792,256]{1,0:T(8,128)(2,1)S(1)} %collective-permute-done.27.got, f32[1,256]{1,0:T(1,128)S(1)} %bitcast.55, ...), custom_call_target="tpu_custom_call" | custom-call | flops 3670016 | bytes 4587520 | tf_op jit(solution)/shard_map/finish_rows/pallas_call | solution.py:257
  248.3 7.1 %all-to-all-start.1 = ((bf16[16,256,256]{2,1,0:T(8,128)(2,1)}), bf16[16,256,256]{2,1,0:T(8,128)(2,1)}, u32[]{:S(2)}, u32[]{:S(2)}) async-start(bf16[16,256,256]{2,1,0:T(8,128)(2,1)} %get-tuple-element.69), calls=%async_computation.1 | async-start | bytes 4194304 | tf_op jit(solution)/shard_map/all_to_all | solution.py:511
  258.3 11.3 %collective-permute-done.24.got = bf16[1792,256]{1,0:T(8,128)(2,1)S(1)} collective-permute-done((bf16[1792,256]{1,0:T(8,128)(2,1)S(1)}, bf16[1792,256]{1,0:T(8,128)(2,1)S(1)}, u32[]{:S(2)}, u32[]{:S(2)}) %collective-permute-start.24) | collective-permute-done | bytes 917536 | tf_op jit(solution)/shard_map/ppermute | solution.py:85
  269.7 3.8 %finish_rows.3 = (bf16[16,256,256]{2,1,0:T(8,128)(2,1)}, bf16[256,256]{1,0:T(8,128)(2,1)S(1)}) custom-call(s32[7]{0:T(128)S(1)} %get-tuple-element.103.dest, s32[7]{0:T(128)S(1)} %get-tuple-element.104.spots, f32[1792,256]{1,0:T(8,128)S(1)} %copy-done.6, bf16[1792,256]{1,0:T(8,128)(2,1)S(1)} %collective-permute-done.24.got, f32[1,256]{1,0:T(1,128)S(1)} %bitcast.53, ...), custom_call_target="tpu_custom_call" | custom-call | flops 3670016 | bytes 4587520 | tf_op jit(solution)/shard_map/finish_rows/pallas_call | solution.py:257
  273.5 9.1 %all-to-all-done.1.refs_5_ = bf16[16,256,256]{2,1,0:T(8,128)(2,1)} async-done(((bf16[16,256,256]{2,1,0:T(8,128)(2,1)}), bf16[16,256,256]{2,1,0:T(8,128)(2,1)}, u32[]{:S(2)}, u32[]{:S(2)}) %all-to-all-start.1) | async-done | bytes 2097184 | tf_op jit(solution)/shard_map/all_to_all | solution.py:511
  282.6 4.5 %all-to-all-start = ((bf16[16,256,256]{2,1,0:T(8,128)(2,1)}), bf16[16,256,256]{2,1,0:T(8,128)(2,1)S(1)}, u32[]{:S(2)}, u32[]{:S(2)}) async-start(bf16[16,256,256]{2,1,0:T(8,128)(2,1)} %get-tuple-element.66), calls=%async_computation | async-start | bytes 4194304 | tf_op jit(solution)/shard_map/all_to_all | solution.py:511
  287.5 14.7 %attend.2.refs_7_ = bf16[1792,512]{1,0:T(8,128)(2,1)} custom-call(s32[7]{0:T(128)S(1)} %select_reduce_fusion.refs_0_, s32[1]{0:T(128)} %bitcast.1.refs_1_, s32[4]{0:T(128)S(1)} %bitcast.56, bf16[16,256,256]{2,1,0:T(8,128)(2,1)} %all-to-all-done.2.refs_3_, bf16[256,256]{1,0:T(8,128)(2,1)S(1)} %get-tuple-element.76.refs_4_, ...), custom_call_target="tpu_custom_call" | custom-call | flops 3288334336 | bytes 2752512 | tf_op jit(solution)/shard_map/attend/pallas_call | solution.py:373
  302.2 12.1 %all-to-all-done.refs_3_ = bf16[16,256,256]{2,1,0:T(8,128)(2,1)S(1)} async-done(((bf16[16,256,256]{2,1,0:T(8,128)(2,1)}), bf16[16,256,256]{2,1,0:T(8,128)(2,1)S(1)}, u32[]{:S(2)}, u32[]{:S(2)}) %all-to-all-start) | async-done | bytes 2097184 | tf_op jit(solution)/shard_map/all_to_all | solution.py:511
  314.3 14.5 %attend.3 = bf16[1792,512]{1,0:T(8,128)(2,1)} custom-call(s32[7]{0:T(128)S(1)} %select_reduce_fusion.refs_0_, s32[1]{0:T(128)} %bitcast.1.refs_1_, s32[4]{0:T(128)S(1)} %bitcast.57, bf16[16,256,256]{2,1,0:T(8,128)(2,1)S(1)} %all-to-all-done.refs_3_, bf16[256,256]{1,0:T(8,128)(2,1)S(1)} %get-tuple-element.67.refs_4_, ...), custom_call_target="tpu_custom_call", output_to_operand_aliasing={{}: (7, {})} | custom-call | flops 3288334336 | bytes 2752512 | tf_op jit(solution)/shard_map/attend/pallas_call | solution.py:373
  (145 shorter events, 45.0 us)
Async XLA Ops:
  0.0 15.5 %copy-start = (bf16[1536,1024]{1,0:T(8,128)(2,1)S(1)}, bf16[1536,1024]{1,0:T(8,128)(2,1)}, u32[]{:S(2)}) copy-start(bf16[1536,1024]{1,0:T(8,128)(2,1)} %refs_0_.1) | copy-start | bytes 9437188
  0.0 11.9 %copy-start.27 = (s32[1,6]{1,0:T(1,128)S(1)}, s32[1,6]{1,0:T(1,128)}, u32[]{:S(2)}) copy-start(s32[1,6]{1,0:T(1,128)} %param.19) | copy-start | bytes 76
  2.8 21.3 %collective-permute-start.3 = (bf16[256,1024]{1,0:T(8,128)(2,1)}, bf16[256,1024]{1,0:T(8,128)(2,1)}, u32[]{:S(2)}, u32[]{:S(2)}) collective-permute-start(bf16[256,1024]{1,0:T(8,128)(2,1)} %get-tuple-element.90), channel_id=1, source_target_pairs={{0,1},{1,0},{2,3},{3,2},{4,5},{5,4},{6,7},{7,6},{8,9},{9,8},{10,11... | collective-permute-start | bytes 1572872 | tf_op jit(solution)/shard_map/ppermute | solution.py:54
  6.5 17.6 %collective-permute-start = (bf16[512,512]{1,0:T(8,128)(2,1)}, bf16[512,512]{1,0:T(8,128)(2,1)}, u32[]{:S(2)}, u32[]{:S(2)}) collective-permute-start(bf16[512,512]{1,0:T(8,128)(2,1)} %param.13), channel_id=1, source_target_pairs={{0,0},{1,1},{2,34},{3,35},{4,68},{5,69},{6,102},{7,103},{8,8},{9,9... | collective-permute-start | bytes 1572872 | tf_op jit(solution)/shard_map/ppermute | solution.py:93
  11.9 12.2 %collective-permute-start.2 = (s32[1,6]{1,0:T(1,128)S(1)}, s32[1,6]{1,0:T(1,128)S(1)}, u32[]{:S(2)}, u32[]{:S(2)}) collective-permute-start(s32[1,6]{1,0:T(1,128)S(1)} %copy-done.27), channel_id=1, source_target_pairs={{0,16},{8,24},{16,0},{24,8},{32,48},{40,56},{48,32},{56,40},{64,80... | collective-permute-start | bytes 80 | tf_op jit(solution)/shard_map/ppermute | solution.py:58
  16.2 7.9 %collective-permute-start.1 = (f32[7,256]{1,0:T(8,128)S(1)}, f32[7,256]{1,0:T(8,128)S(1)}, u32[]{:S(2)}, u32[]{:S(2)}) collective-permute-start(f32[7,256]{1,0:T(8,128)S(1)} %reshape.78), channel_id=1, source_target_pairs={{0,2},{1,3},{2,0},{3,1},{4,6},{5,7},{6,4},{7,5},{8,10},{9,11},{10,... | collective-permute-start | bytes 21512 | tf_op jit(solution)/shard_map/ppermute | solution.py:54
  24.1 18.0 %collective-permute-start.7 = (bf16[256,1024]{1,0:T(8,128)(2,1)}, bf16[256,1024]{1,0:T(8,128)(2,1)S(1)}, u32[]{:S(2)}, u32[]{:S(2)}) collective-permute-start(bf16[256,1024]{1,0:T(8,128)(2,1)} %get-tuple-element.44), channel_id=1, source_target_pairs={{0,1},{1,0},{2,3},{3,2},{4,5},{5,4},{6,7},{7,6},{8,9},{9,8},{10,11... | collective-permute-start | bytes 1572872 | tf_op jit(solution)/shard_map/ppermute | solution.py:54
  25.7 17.2 %collective-permute-start.4 = (bf16[512,512]{1,0:T(8,128)(2,1)}, bf16[512,512]{1,0:T(8,128)(2,1)}, u32[]{:S(2)}, u32[]{:S(2)}) collective-permute-start(bf16[512,512]{1,0:T(8,128)(2,1)} %collective-permute-done), channel_id=1, source_target_pairs={{0,0},{1,1},{2,2},{3,3},{4,4},{5,5},{6,6},{7,7},{8,8},{9,9},{10,10... | collective-permute-start | bytes 1572872 | tf_op jit(solution)/shard_map/ppermute | solution.py:101
  34.3 8.7 %slice-start = ((bf16[1536,1024]{1,0:T(8,128)(2,1)}), bf16[768,1024]{1,0:T(8,128)(2,1)S(1)}, s32[]{:S(2)}) async-start(bf16[1536,1024]{1,0:T(8,128)(2,1)} %refs_0_.1), calls=%async_computation.3 | async-start | bytes 3145728 | tf_op jit(solution)/shard_map/slice | solution.py:420
  34.3 8.7 %copy-start.22 = (bf16[256,1024]{1,0:T(8,128)(2,1)S(1)}, bf16[256,1024]{1,0:T(8,128)(2,1)}, u32[]{:S(2)}) copy-start(bf16[256,1024]{1,0:T(8,128)(2,1)} %get-tuple-element.78) | copy-start | bytes 1572868
  35.1 6.0 %collective-permute-start.6 = (s32[2,6]{1,0:T(2,128)S(1)}, s32[2,6]{1,0:T(2,128)S(1)}, u32[]{:S(2)}, u32[]{:S(2)}) collective-permute-start(s32[2,6]{1,0:T(2,128)S(1)} %pad_add_fusion.2), channel_id=1, source_target_pairs={{0,8},{8,0},{16,24},{24,16},{32,40},{40,32},{48,56},{56,48},{64,72... | collective-permute-start | bytes 152 | tf_op jit(solution)/shard_map/ppermute | solution.py:58
  36.6 5.5 %collective-permute-start.5 = (f32[7,256]{1,0:T(8,128)S(1)}, f32[7,256]{1,0:T(8,128)S(1)}, u32[]{:S(2)}, u32[]{:S(2)}) collective-permute-start(f32[7,256]{1,0:T(8,128)S(1)} %add.191), channel_id=1, source_target_pairs={{0,4},{1,5},{2,6},{3,7},{4,0},{5,1},{6,2},{7,3},{8,12},{9,13},{10,... | collective-permute-start | bytes 21512 | tf_op jit(solution)/shard_map/ppermute | solution.py:54
  42.9 14.3 %collective-permute-start.8 = (bf16[512,512]{1,0:T(8,128)(2,1)}, bf16[512,512]{1,0:T(8,128)(2,1)}, u32[]{:S(2)}, u32[]{:S(2)}) collective-permute-start(bf16[512,512]{1,0:T(8,128)(2,1)} %collective-permute-done.4), channel_id=1, source_target_pairs={{0,16},{8,24},{16,0},{24,8},{32,48},{40,56},{48,32},{56,40},{64,80... | collective-permute-start | bytes 1572872 | tf_op jit(solution)/shard_map/ppermute | solution.py:58
  44.5 12.7 %collective-permute-start.9 = (f32[7,256]{1,0:T(8,128)S(1)}, f32[7,256]{1,0:T(8,128)S(1)}, u32[]{:S(2)}, u32[]{:S(2)}) collective-permute-start(f32[7,256]{1,0:T(8,128)S(1)} %add.192), channel_id=1, source_target_pairs={{0,1},{1,0},{2,3},{3,2},{4,5},{5,4},{6,7},{7,6},{8,9},{9,8},{10,11... | collective-permute-start | bytes 21512 | tf_op jit(solution)/shard_map/ppermute | solution.py:54
  47.5 21.3 %collective-permute-start.10 = (bf16[256,1024]{1,0:T(8,128)(2,1)}, bf16[256,1024]{1,0:T(8,128)(2,1)}, u32[]{:S(2)}, u32[]{:S(2)}) collective-permute-start(bf16[256,1024]{1,0:T(8,128)(2,1)} %get-tuple-element.48), channel_id=1, source_target_pairs={{0,1},{1,0},{2,3},{3,2},{4,5},{5,4},{6,7},{7,6},{8,9},{9,8},{10,11... | collective-permute-start | bytes 1572872 | tf_op jit(solution)/shard_map/ppermute | solution.py:54
  47.6 21.3 %collective-permute-start.11 = (bf16[1024,256]{1,0:T(8,128)(2,1)}, bf16[1024,256]{1,0:T(8,128)(2,1)}, u32[]{:S(2)}, u32[]{:S(2)}) collective-permute-start(bf16[1024,256]{1,0:T(8,128)(2,1)} %pad_maximum_fusion.7), channel_id=1, source_target_pairs={{0,6},{1,7},{2,0},{3,1},{4,2},{5,3},{6,4},{7,5},{8,14},{9,15},{10,... | collective-permute-start | bytes 1572872 | tf_op jit(solution)/shard_map/ppermute | solution.py:50
  49.7 19.1 %collective-permute-start.12 = (bf16[1024,256]{1,0:T(8,128)(2,1)}, bf16[1024,256]{1,0:T(8,128)(2,1)}, u32[]{:S(2)}, u32[]{:S(2)}) collective-permute-start(bf16[1024,256]{1,0:T(8,128)(2,1)} %pad_maximum_fusion.6), channel_id=1, source_target_pairs={{0,2},{1,3},{2,4},{3,5},{4,6},{5,7},{6,0},{7,1},{8,10},{9,11},{10,... | collective-permute-start | bytes 1572872 | tf_op jit(solution)/shard_map/ppermute | solution.py:50
  57.2 11.6 %copy-start.21 = (bf16[1024,1024]{1,0:T(8,128)(2,1)S(1)}, bf16[1024,1024]{1,0:T(8,128)(2,1)}, u32[]{:S(2)}) copy-start(bf16[1024,1024]{1,0:T(8,128)(2,1)} %pad_maximum_fusion.1) | copy-start | bytes 6291460
  57.2 15.5 %copy-start.24 = (bf16[1024,256]{1,0:T(8,128)(2,1)S(1)}, bf16[1024,256]{1,0:T(8,128)(2,1)}, u32[]{:S(2)}) copy-start(bf16[1024,256]{1,0:T(8,128)(2,1)} %pad_maximum_fusion.8) | copy-start | bytes 1572868
  57.2 17.3 %copy-start.23 = (bf16[512,256]{1,0:T(8,128)(2,1)S(1)}, bf16[512,256]{1,0:T(8,128)(2,1)}, u32[]{:S(2)}) copy-start(bf16[512,256]{1,0:T(8,128)(2,1)} %get-tuple-element.82) | copy-start | bytes 786436
  68.8 50.9 %collective-permute-start.17 = (bf16[1024,1024]{1,0:T(8,128)(2,1)S(1)}, bf16[1024,1024]{1,0:T(8,128)(2,1)S(1)}, u32[]{:S(2)}, u32[]{:S(2)}) collective-permute-start(bf16[1024,1024]{1,0:T(8,128)(2,1)S(1)} %copy-done.21), channel_id=1, source_target_pairs={{0,1},{1,0},{2,3},{3,2},{4,5},{5,4},{6,7},{7,6},{8,9},{9,8},{10,11... | collective-permute-start | bytes 6291464 | tf_op jit(solution)/shard_map/ppermute | solution.py:54
  69.1 25.2 %collective-permute-start.13 = (bf16[1024,512]{1,0:T(8,128)(2,1)S(1)}, bf16[1024,512]{1,0:T(8,128)(2,1)S(1)}, u32[]{:S(2)}, u32[]{:S(2)}) collective-permute-start(bf16[1024,512]{1,0:T(8,128)(2,1)S(1)} %pad_maximum_fusion.3), channel_id=1, source_target_pairs={{0,32},{8,40},{16,48},{24,56},{32,64},{40,72},{48,80},{56,88},{64,... | collective-permute-start | bytes 3145736 | tf_op jit(solution)/shard_map/ppermute | solution.py:62
  69.1 44.3 %collective-permute-start.14 = (bf16[1024,512]{1,0:T(8,128)(2,1)S(1)}, bf16[1024,512]{1,0:T(8,128)(2,1)S(1)}, u32[]{:S(2)}, u32[]{:S(2)}) collective-permute-start(bf16[1024,512]{1,0:T(8,128)(2,1)S(1)} %pad_maximum_fusion.3), channel_id=1, source_target_pairs={{0,64},{8,72},{16,80},{24,88},{32,96},{40,104},{48,112},{56,120},{... | collective-permute-start | bytes 3145736 | tf_op jit(solution)/shard_map/ppermute | solution.py:62
  71.7 45.8 %collective-permute-start.15 = (bf16[1024,512]{1,0:T(8,128)(2,1)S(1)}, bf16[1024,512]{1,0:T(8,128)(2,1)S(1)}, u32[]{:S(2)}, u32[]{:S(2)}) collective-permute-start(bf16[1024,512]{1,0:T(8,128)(2,1)S(1)} %pad_maximum_fusion.3), channel_id=1, source_target_pairs={{0,96},{8,104},{16,112},{24,120},{32,0},{40,8},{48,16},{56,24},{64... | collective-permute-start | bytes 3145736 | tf_op jit(solution)/shard_map/ppermute | solution.py:62
  72.7 10.8 %collective-permute-start.16 = (bf16[1024,256]{1,0:T(8,128)(2,1)S(1)}, bf16[1024,256]{1,0:T(8,128)(2,1)S(1)}, u32[]{:S(2)}, u32[]{:S(2)}) collective-permute-start(bf16[1024,256]{1,0:T(8,128)(2,1)S(1)} %copy-done.24), channel_id=1, source_target_pairs={{0,4},{1,5},{2,6},{3,7},{4,0},{5,1},{6,2},{7,3},{8,12},{9,13},{10,... | collective-permute-start | bytes 1572872 | tf_op jit(solution)/shard_map/ppermute | solution.py:50
  121.0 23.5 %collective-permute-start.21 = (bf16[4,1024,512]{2,1,0:T(8,128)(2,1)}, bf16[4,1024,512]{2,1,0:T(8,128)(2,1)}, u32[]{:S(2)}, u32[]{:S(2)}) collective-permute-start(bf16[4,1024,512]{2,1,0:T(8,128)(2,1)} %pad_maximum_fusion.q_mine), channel_id=1, source_target_pairs={{0,8},{8,0},{16,24},{24,16},{32,40},{40,32},{48,56},{56,48},{64,72... | collective-permute-start | bytes 12582920 | tf_op jit(solution)/shard_map/ppermute | solution.py:58
  122.6 21.9 %collective-permute-start.20 = (bf16[4,1024,256]{2,1,0:T(8,128)(2,1)}, bf16[4,1024,256]{2,1,0:T(8,128)(2,1)}, u32[]{:S(2)}, u32[]{:S(2)}) collective-permute-start(bf16[4,1024,256]{2,1,0:T(8,128)(2,1)} %pad_maximum_fusion.2.kv_mine), channel_id=1, source_target_pairs={{0,8},{8,0},{16,24},{24,16},{32,40},{40,32},{48,56},{56,48},{64,72... | collective-permute-start | bytes 6291464 | tf_op jit(solution)/shard_map/ppermute | solution.py:58
  144.5 13.7 %copy-start.29 = (s32[16]{0:T(128)S(1)}, s32[16]{0:T(128)}, u32[]{:S(2)}) copy-start(s32[16]{0:T(128)} %constant.473.clone) | copy-start | bytes 196
  144.5 13.7 %copy-start.20 = (f32[1792,64]{1,0:T(8,128)S(1)}, f32[1792,64]{1,0:T(8,128)}, u32[]{:S(2)}) copy-start(f32[1792,64]{1,0:T(8,128)} %get-tuple-element.98) | copy-start | bytes 1376260
  156.3 14.8 %collective-permute-start.28 = (bf16[1792,256]{1,0:T(8,128)(2,1)}, bf16[1792,256]{1,0:T(8,128)(2,1)}, u32[]{:S(2)}, u32[]{:S(2)}) collective-permute-start(bf16[1792,256]{1,0:T(8,128)(2,1)} %get-tuple-element.74), channel_id=1, source_target_pairs={{0,2},{1,3},{2,4},{3,5},{4,6},{5,7},{6,0},{7,1},{8,14},{9,15},{10,... | collective-permute-start | bytes 2752520 | tf_op jit(solution)/shard_map/ppermute | solution.py:85
  160.5 14.2 %collective-permute-start.18 = (s32[4,6]{1,0:T(4,128)S(1)}, s32[4,6]{1,0:T(4,128)S(1)}, u32[]{:S(2)}, u32[]{:S(2)}) collective-permute-start(s32[4,6]{1,0:T(4,128)S(1)} %pad_add_fusion.1), channel_id=1, source_target_pairs={{0,32},{8,40},{16,48},{24,56},{32,0},{40,8},{48,16},{56,24},{64,96... | collective-permute-start | bytes 296 | tf_op jit(solution)/shard_map/ppermute | solution.py:58
  173.5 17.4 %collective-permute-start.29 = (bf16[1792,256]{1,0:T(8,128)(2,1)}, bf16[1792,256]{1,0:T(8,128)(2,1)}, u32[]{:S(2)}, u32[]{:S(2)}) collective-permute-start(bf16[1792,256]{1,0:T(8,128)(2,1)} %add_convert_fusion.1), channel_id=1, source_target_pairs={{0,2},{1,3},{2,4},{3,5},{4,6},{5,7},{6,0},{7,1},{8,14},{9,15},{10,... | collective-permute-start | bytes 2752520 | tf_op jit(solution)/shard_map/ppermute | solution.py:85
  174.7 4.3 %collective-permute-start.19 = (s32[8,6]{1,0:T(8,128)S(1)}, s32[8,6]{1,0:T(8,128)S(1)}, u32[]{:S(2)}, u32[]{:S(2)}) collective-permute-start(s32[8,6]{1,0:T(8,128)S(1)} %pad_add_fusion), channel_id=1, source_target_pairs={{0,64},{8,72},{16,80},{24,88},{32,96},{40,104},{48,112},{56,120},{... | collective-permute-start | bytes 584 | tf_op jit(solution)/shard_map/ppermute | solution.py:58
  180.1 16.0 %collective-permute-start.25 = (bf16[1792,256]{1,0:T(8,128)(2,1)}, bf16[1792,256]{1,0:T(8,128)(2,1)S(1)}, u32[]{:S(2)}, u32[]{:S(2)}) collective-permute-start(bf16[1792,256]{1,0:T(8,128)(2,1)} %copy-done.18), channel_id=1, source_target_pairs={{0,2},{1,3},{2,4},{3,5},{4,6},{5,7},{6,0},{7,1},{8,14},{9,15},{10,... | collective-permute-start | bytes 2752520 | tf_op jit(solution)/shard_map/ppermute | solution.py:85
  190.8 8.5 %copy-start.13 = (bf16[1792,256]{1,0:T(8,128)(2,1)}, bf16[1792,256]{1,0:T(8,128)(2,1)S(1)}, u32[]{:S(2)}) copy-start(bf16[1792,256]{1,0:T(8,128)(2,1)S(1)} %get-tuple-element.61.rest_0_) | copy-start | bytes 2752516
  193.0 17.9 %collective-permute-start.30 = (bf16[1792,256]{1,0:T(8,128)(2,1)S(1)}, bf16[1792,256]{1,0:T(8,128)(2,1)S(1)}, u32[]{:S(2)}, u32[]{:S(2)}) collective-permute-start(bf16[1792,256]{1,0:T(8,128)(2,1)S(1)} %add_convert_fusion), channel_id=1, source_target_pairs={{0,2},{1,3},{2,4},{3,5},{4,6},{5,7},{6,0},{7,1},{8,14},{9,15},{10,... | collective-permute-start | bytes 2752520 | tf_op jit(solution)/shard_map/ppermute | solution.py:85
  197.4 25.9 %collective-permute-start.26 = (bf16[1792,256]{1,0:T(8,128)(2,1)}, bf16[1792,256]{1,0:T(8,128)(2,1)}, u32[]{:S(2)}, u32[]{:S(2)}) collective-permute-start(bf16[1792,256]{1,0:T(8,128)(2,1)} %add_convert_fusion.3), channel_id=1, source_target_pairs={{0,2},{1,3},{2,4},{3,5},{4,6},{5,7},{6,0},{7,1},{8,14},{9,15},{10,... | collective-permute-start | bytes 2752520 | tf_op jit(solution)/shard_map/ppermute | solution.py:85
  214.7 33.6 %all-to-all-start.2 = ((bf16[16,256,256]{2,1,0:T(8,128)(2,1)}), bf16[16,256,256]{2,1,0:T(8,128)(2,1)}, u32[]{:S(2)}, u32[]{:S(2)}) async-start(bf16[16,256,256]{2,1,0:T(8,128)(2,1)} %get-tuple-element.75), calls=%async_computation.2 | async-start | bytes 4194304 | tf_op jit(solution)/shard_map/all_to_all | solution.py:511
  221.1 22.8 %copy-start.8 = (f32[1792,256]{1,0:T(8,128)S(1)}, f32[1792,256]{1,0:T(8,128)}, u32[]{:S(2)}) copy-start(f32[1792,256]{1,0:T(8,128)} %copy-done.7) | copy-start | bytes 5505028
  221.1 22.8 %copy-start.16 = (f32[2,128]{1,0:T(2,128)S(1)}, f32[2,128]{1,0:T(2,128)}, u32[]{:S(2)}) copy-start(f32[2,128]{1,0:T(2,128)} %param.16) | copy-start | bytes 3076
  221.1 12.9 %collective-permute-start.22 = (bf16[1792,256]{1,0:T(8,128)(2,1)}, bf16[1792,256]{1,0:T(8,128)(2,1)S(1)}, u32[]{:S(2)}, u32[]{:S(2)}) collective-permute-start(bf16[1792,256]{1,0:T(8,128)(2,1)} %copy-done.17), channel_id=1, source_target_pairs={{0,2},{1,3},{2,4},{3,5},{4,6},{5,7},{6,0},{7,1},{8,14},{9,15},{10,... | collective-permute-start | bytes 2752520 | tf_op jit(solution)/shard_map/ppermute | solution.py:85
  224.9 18.9 %collective-permute-start.27 = (bf16[1792,256]{1,0:T(8,128)(2,1)S(1)}, bf16[1792,256]{1,0:T(8,128)(2,1)S(1)}, u32[]{:S(2)}, u32[]{:S(2)}) collective-permute-start(bf16[1792,256]{1,0:T(8,128)(2,1)S(1)} %add_convert_fusion.2), channel_id=1, source_target_pairs={{0,2},{1,3},{2,4},{3,5},{4,6},{5,7},{6,0},{7,1},{8,14},{9,15},{10,... | collective-permute-start | bytes 2752520 | tf_op jit(solution)/shard_map/ppermute | solution.py:85
  235.3 20.1 %collective-permute-start.23 = (bf16[1792,256]{1,0:T(8,128)(2,1)}, bf16[1792,256]{1,0:T(8,128)(2,1)}, u32[]{:S(2)}, u32[]{:S(2)}) collective-permute-start(bf16[1792,256]{1,0:T(8,128)(2,1)} %add_convert_fusion.5), channel_id=1, source_target_pairs={{0,2},{1,3},{2,4},{3,5},{4,6},{5,7},{6,0},{7,1},{8,14},{9,15},{10,... | collective-permute-start | bytes 2752520 | tf_op jit(solution)/shard_map/ppermute | solution.py:85
  248.3 7.1 %copy-start.10 = (bf16[1792,256]{1,0:T(8,128)(2,1)S(1)}, bf16[1792,256]{1,0:T(8,128)(2,1)}, u32[]{:S(2)}) copy-start(bf16[1792,256]{1,0:T(8,128)(2,1)} %copy-done.9) | copy-start | bytes 2752516
  248.3 34.3 %all-to-all-start.1 = ((bf16[16,256,256]{2,1,0:T(8,128)(2,1)}), bf16[16,256,256]{2,1,0:T(8,128)(2,1)}, u32[]{:S(2)}, u32[]{:S(2)}) async-start(bf16[16,256,256]{2,1,0:T(8,128)(2,1)} %get-tuple-element.69), calls=%async_computation.1 | async-start | bytes 4194304 | tf_op jit(solution)/shard_map/all_to_all | solution.py:511
  255.4 14.3 %copy-start.6 = (f32[1792,256]{1,0:T(8,128)S(1)}, f32[1792,256]{1,0:T(8,128)}, u32[]{:S(2)}) copy-start(f32[1792,256]{1,0:T(8,128)} %get-tuple-element.62.here) | copy-start | bytes 5505028
  256.9 12.7 %collective-permute-start.24 = (bf16[1792,256]{1,0:T(8,128)(2,1)S(1)}, bf16[1792,256]{1,0:T(8,128)(2,1)S(1)}, u32[]{:S(2)}, u32[]{:S(2)}) collective-permute-start(bf16[1792,256]{1,0:T(8,128)(2,1)S(1)} %add_convert_fusion.4), channel_id=1, source_target_pairs={{0,2},{1,3},{2,4},{3,5},{4,6},{5,7},{6,0},{7,1},{8,14},{9,15},{10,... | collective-permute-start | bytes 2752520 | tf_op jit(solution)/shard_map/ppermute | solution.py:85
  282.6 31.7 %all-to-all-start = ((bf16[16,256,256]{2,1,0:T(8,128)(2,1)}), bf16[16,256,256]{2,1,0:T(8,128)(2,1)S(1)}, u32[]{:S(2)}, u32[]{:S(2)}) async-start(bf16[16,256,256]{2,1,0:T(8,128)(2,1)} %get-tuple-element.66), calls=%async_computation | async-start | bytes 4194304 | tf_op jit(solution)/shard_map/all_to_all | solution.py:511
  (17 other events, 44.5 us)

commit v3 on v2

v3 whole, which is shorter than its diff:
```python
import functools
import math

import jax
import jax.numpy as jnp
from jax import lax
from jax.experimental import pallas as pl
from jax.experimental.pallas import tpu as pltpu
from jax.sharding import PartitionSpec as P

HD = 128
TILE = 256
BLOCKS = 7
SEQ = BLOCKS * TILE
PART = 1024
SLICE = 2 * PART
CORE_PART = PART // 2
TAIL = 16
WIDE = 2 * HD
ROWS = SEQ // 4
VMEM = 48 * 1024 * 1024

rope_base = 1000000.0
eps = 1e-06
masked_score = -1e30


def params():
    return pltpu.CompilerParams(vmem_limit_bytes=VMEM)


def cost(flops, moved, transcendentals=0):
    return pl.CostEstimate(flops=flops, bytes_accessed=moved, transcendentals=transcendentals)


def rope_tables(length, width):
    half_width = width // 2
    inverse = rope_base ** (-(jnp.arange(half_width, dtype=jnp.float32) * 2.0) / width)
    angles = jnp.arange(length, dtype=jnp.float32)[:, None] * inverse[None, :]
    cosine, sine = jnp.cos(angles), jnp.sin(angles)
    return (
        jnp.concatenate([cosine, cosine], axis=1),
        jnp.concatenate([-sine, sine], axis=1),
    )


def shift_x(value, step):
    pairs = [
        (2 * x + high, 2 * ((x + step) % 4) + high) for x in range(4) for high in range(2)
    ]
    return lax.ppermute(value, "tensor", pairs)


def swap_tensor(value, bits):
    return lax.ppermute(value, "tensor", [(t, t ^ bits) for t in range(8)])


def swap_dp(value, bits):
    return lax.ppermute(value, "dp", [(d, d ^ bits) for d in range(16)])


def place(z, low, core, x, high):
    return ((z * 2 + low) * 2 + core) * 8 + x * 2 + high


def all_places():
    return [
        (z, low, core, x, high)
        for z in range(4)
        for low in range(2)
        for core in range(2)
        for x in range(4)
        for high in range(2)
    ]


def ring_x(value):
    pairs = [
        (place(z, low, core, x, high), place(z, low, core, (x + 1 - 2 * core) % 4, high))
        for z, low, core, x, high in all_places()
    ]
    return lax.ppermute(value, ("dp", "tensor"), pairs)


def shift_z(value, step):
    return lax.ppermute(value, "dp", [(d, (d + 4 * step) % 16) for d in range(16)])


def mirror_z(value):
    pairs = [
        (place(z, low, core, x, high), place((x - z) % 4, low, core, x, high))
        for z, low, core, x, high in all_places()
    ]
    return lax.ppermute(value, ("dp", "tensor"), pairs)


def slide_x(value):
    pairs = [
        (place(z, low, core, x, high), place(z, low, core, (x - z) % 4, high))
        for z, low, core, x, high in all_places()
    ]
    return lax.ppermute(value, ("dp", "tensor"), pairs)


def lock(values, guards):
    return lax.optimization_barrier((tuple(values), tuple(guards)))[0]


def norm_kernel(bounds, begin, picks, *refs):
    parts, scale, gain, out = refs[: len(bounds)], refs[len(bounds)], refs[len(bounds) + 1], refs[-1]
    step = pl.program_id(0) + begin
    core = picks[1]

    def put(rows):
        result = (rows[...].astype(jnp.float32) * scale[...] * gain[...]).astype(jnp.bfloat16)
        front, back = result[:, :CORE_PART], result[:, CORE_PART:]

        @pl.when(core == 0)
        def _():
            out[:, :CORE_PART] = front
            out[:, CORE_PART:] = back

        @pl.when(core == 1)
        def _():
            out[:, :CORE_PART] = back
            out[:, CORE_PART:] = front

    for part, (first, last) in zip(parts, bounds):
        pl.when((step >= first) & (step < last))(functools.partial(put, part))


def norm_rows(picks, parts, bounds, scale, gain, base=None):
    begin, end = bounds[0][0], bounds[-1][1]

    def spec(part, first, last):
        if part.shape[0] == SEQ:
            return pl.BlockSpec((TILE, PART), lambda i, s: (s[0], 0))
        return pl.BlockSpec(
            (TILE, PART), lambda i, s: (jnp.clip(i + begin - first, 0, last - first - 1), 0)
        )

    aliased = [] if base is None else [base]
    grid_spec = pltpu.PrefetchScalarGridSpec(
        num_scalar_prefetch=1,
        grid=(end - begin,),
        in_specs=[spec(part, *bound) for part, bound in zip(parts, bounds)]
        + [
            pl.BlockSpec((TILE, 1), lambda i, s: (i + begin, 0)),
            pl.BlockSpec((1, PART), lambda i, s: (0, 0)),
        ]
        + later(aliased),
        out_specs=pl.BlockSpec((TILE, PART), lambda i, s: (i + begin, 0)),
    )
    rows = (end - begin) * TILE
    return pl.pallas_call(
        functools.partial(norm_kernel, bounds, begin),
        grid_spec=grid_spec,
        out_shape=jax.ShapeDtypeStruct((SEQ, PART), jnp.bfloat16),
        input_output_aliases={len(parts) + 3: 0} if aliased else {},
        compiler_params=params(),
        cost_estimate=cost(0, 0),
        name="norm_rows",
    )(picks, *parts, scale, gain, *aliased)


def later(tokens):
    return [pl.BlockSpec(memory_space=pl.ANY)] * len(tokens)


def part_kernel(count, at, own, other, *rest):
    weights, outs = rest[: 2 * count], rest[-count:]
    for turn in range(count):
        total = None
        for columns, part in zip(
            (slice(0, CORE_PART), slice(CORE_PART, PART)), weights[2 * turn : 2 * turn + 2]
        ):
            for rows, at in ((own, slice(0, CORE_PART)), (other, slice(CORE_PART, PART))):
                term = jnp.dot(rows[:, columns], part[0, at], preferred_element_type=jnp.float32)
                total = term if total is None else total + term
        outs[turn][...] = total.astype(outs[turn].dtype)


def parts_of(at, own, other, mine, theirs, half, dtypes, tokens):
    count = len(dtypes)

    def weight_spec(turn):
        return pl.BlockSpec((1, PART, WIDE), lambda i, s: (s[turn], 0, half))

    grid_spec = pltpu.PrefetchScalarGridSpec(
        num_scalar_prefetch=1,
        grid=(SEQ // ROWS,),
        in_specs=[
            pl.BlockSpec((ROWS, PART), lambda i, s: (i, 0)),
            pl.BlockSpec((ROWS, PART), lambda i, s: (i, 0)),
            *[weight_spec(turn) for turn in range(count) for _ in range(2)],
            *later(tokens),
        ],
        out_specs=[pl.BlockSpec((ROWS, WIDE), lambda i, s: (i, 0))] * count,
    )
    return pl.pallas_call(
        functools.partial(part_kernel, count),
        grid_spec=grid_spec,
        out_shape=[jax.ShapeDtypeStruct((SEQ, WIDE), dtype) for dtype in dtypes],
        compiler_params=params(),
        cost_estimate=cost(2 * count * SEQ * SLICE * WIDE, 2 * SEQ * SLICE),
        name="part_rows",
    )(at, own, other, *[mine, theirs] * count, *tokens)


def finish_kernel(rotated, dest, spots, *refs):
    count = len(rotated) // 2
    heres, gots, biases = refs[:count], refs[count : 2 * count], refs[2 * count : 3 * count]
    cosine, sine, slots, text = refs[3 * count :]
    step = pl.program_id(0)
    heads = []
    for at in range(count):
        total = heres[at][...] + gots[at][...].astype(jnp.float32) + biases[at][...]
        for head in range(2):
            values = total[:, head * HD : (head + 1) * HD]
            if rotated[2 * at + head]:
                values = values * cosine[...] + pltpu.roll(values, HD // 2, 1) * sine[...]
            heads.append(values.astype(jnp.bfloat16))

    @pl.when(step < BLOCKS - 1)
    def _():
        for head, values in enumerate(heads):
            slots[0, :, head * HD : (head + 1) * HD] = values

    @pl.when(step == BLOCKS - 1)
    def _():
        for head, values in enumerate(heads):
            text[:, head * HD : (head + 1) * HD] = values


def finish(rotated, dest, spots, heres, gots, biases, tables, shards):
    count = len(heres)

    def row(i, d, s):
        return (i, 0)

    def spot(i, d, s):
        return (s[i], 0)

    def none(i, d, s):
        return (0, 0)

    grid_spec = pltpu.PrefetchScalarGridSpec(
        num_scalar_prefetch=2,
        grid=(BLOCKS,),
        in_specs=[
            *[pl.BlockSpec((TILE, WIDE), row)] * (2 * count),
            *[pl.BlockSpec((1, WIDE), none)] * count,
            pl.BlockSpec((TILE, HD), spot),
            pl.BlockSpec((TILE, HD), spot),
        ],
        out_specs=[
            pl.BlockSpec((1, TILE, count * WIDE), lambda i, d, s: (d[i], 0, 0)),
            pl.BlockSpec((TILE, count * WIDE), none),
        ],
    )
    return pl.pallas_call(
        functools.partial(finish_kernel, rotated),
        grid_spec=grid_spec,
        out_shape=[
            jax.ShapeDtypeStruct((shards, TILE, count * WIDE), jnp.bfloat16),
            jax.ShapeDtypeStruct((TILE, count * WIDE), jnp.bfloat16),
        ],
        compiler_params=params(),
        cost_estimate=cost(8 * count * SEQ * WIDE, 10 * count * SEQ * WIDE),
        name="finish_rows",
    )(dest, spots, *heres, *gots, *biases, *tables)


def pair_kernel(source, text_at, slots, text, keys, values):
    block = pl.program_id(0)

    def put(rows):
        keys[...] = rows[:, :HD]
        values[:HD] = rows[:, HD:].T
        values[HD:] = jnp.ones((TAIL, TILE), jnp.bfloat16)

    @pl.when(text_at[0] == block)
    def _():
        put(text[...])

    @pl.when(text_at[0] != block)
    def _():
        put(slots[0])


def gather_pair(source, text_at, slots, text):
    grid_spec = pltpu.PrefetchScalarGridSpec(
        num_scalar_prefetch=2,
        grid=(BLOCKS,),
        in_specs=[
            pl.BlockSpec((1, TILE, WIDE), lambda i, s, t: (s[i], 0, 0)),
            pl.BlockSpec((TILE, WIDE), lambda i, s, t: (0, 0)),
        ],
        out_specs=[
            pl.BlockSpec((TILE, HD), lambda i, s, t: (i, 0)),
            pl.BlockSpec((HD + TAIL, TILE), lambda i, s, t: (0, i)),
        ],
    )
    return pl.pallas_call(
        pair_kernel,
        grid_spec=grid_spec,
        out_shape=[
            jax.ShapeDtypeStruct((SEQ, HD), jnp.bfloat16),
            jax.ShapeDtypeStruct((HD + TAIL, SEQ), jnp.bfloat16),
        ],
        compiler_params=params(),
        cost_estimate=cost(SEQ * WIDE, 4 * SEQ * WIDE),
        name="gather_pair",
    )(source, text_at, slots, text)


def attend_kernel(has_base, source, text_at, ends, slots, text, keys, values, *rest):
    out = rest[-1]
    block = pl.program_id(0)
    queries = jnp.where(block == text_at[0], text[...], slots[0])
    queries = jnp.concatenate([queries[:, :HD], queries[:, HD:]], axis=0)
    score_scale = 1.0 / (math.sqrt(HD) * math.log(2.0))
    first = block * TILE
    index = lax.broadcasted_iota(jnp.int32, (1, 2 * TILE), 1)
    position = first + jnp.where(index >= TILE, index - TILE, index)
    start = jnp.zeros_like(position)
    low = jnp.int32(0)
    for at in range(4):
        end = ends[at]
        start = jnp.where(position >= end, end, start)
        low = jnp.where(first >= end, end, low)
    row = lax.broadcasted_iota(jnp.int32, (TILE, 2 * TILE), 0)

    def scores_of(at):
        offset = pl.multiple_of(at * TILE, TILE)
        return lax.dot_general(
            keys[pl.ds(offset, TILE), :],
            queries,
            (((1,), (1,)), ((), ())),
            preferred_element_type=jnp.float32,
        )

    def mix(scores, top, at):
        weights = jnp.exp2((scores - top) * score_scale).astype(jnp.bfloat16)
        offset = pl.multiple_of(at * TILE, TILE)
        return jnp.dot(
            values[:, pl.ds(offset, TILE)], weights, preferred_element_type=jnp.float32
        )

    allowed = (row <= position - first) & (row >= start - first)
    scores = jnp.where(allowed, scores_of(block), masked_score)
    top = jnp.max(scores, axis=0, keepdims=True)
    mixed = mix(scores, top, block)

    def body(at, carry):
        top, mixed = carry
        scores = jnp.where(row >= start - at * TILE, scores_of(at), masked_score)
        higher = jnp.maximum(top, jnp.max(scores, axis=0, keepdims=True))
        fade = jnp.exp2((top - higher) * score_scale)
        return higher, mixed * fade + mix(scores, higher, at)

    top, mixed = lax.fori_loop(low // TILE, block, body, (top, mixed))
    result = (mixed[:HD] / mixed[HD : HD + 1]).T.astype(jnp.bfloat16)
    out[:, :HD] = result[:TILE]
    out[:, HD:] = result[TILE:]


def attend(source, text_at, ends, slots, text, keys, values, base, half, column):
    in_specs = [
        pl.BlockSpec((1, TILE, WIDE), lambda i, s, t, e: (s[i], 0, column)),
        pl.BlockSpec((TILE, WIDE), lambda i, s, t, e: (0, column)),
        pl.BlockSpec((SEQ, HD), lambda i, s, t, e: (0, 0)),
        pl.BlockSpec((HD + TAIL, SEQ), lambda i, s, t, e: (0, 0)),
    ]
    operands = [source, text_at, ends, slots, text, keys, values]
    aliases = {}
    if base is not None:
        in_specs.append(pl.BlockSpec(memory_space=pl.ANY))
        operands.append(base)
        aliases = {7: 0}
    grid_spec = pltpu.PrefetchScalarGridSpec(
        num_scalar_prefetch=3,
        grid=(BLOCKS,),
        in_specs=in_specs,
        out_specs=pl.BlockSpec((TILE, WIDE), lambda i, s, t, e: (i, half)),
    )

    def body(*refs):
        attend_kernel(base is not None, *refs)

    return pl.pallas_call(
        body,
        grid_spec=grid_spec,
        out_shape=jax.ShapeDtypeStruct((SEQ, 2 * WIDE), jnp.bfloat16),
        input_output_aliases=aliases,
        compiler_params=params(),
        cost_estimate=cost(4 * SEQ * SEQ * WIDE, 6 * SEQ * WIDE, SEQ * SEQ),
        name="attend",
    )(*operands)


def local(
    text_rows,
    vis_rows,
    q_weight,
    kv_weight,
    q_bias,
    kv_bias,
    norm_gain,
    tile_dest,
    tile_block,
    doc_lens,
):
    width = norm_gain.shape[0]
    shards = lax.axis_size("dp")
    me = lax.axis_index("dp")
    tensor_at = lax.axis_index("tensor")
    x_at, high = tensor_at // 2, tensor_at % 2
    z_at, low, core = me // 4, me // 2 % 2, me % 2
    blocks = tile_block[0]
    text_block = sum(range(BLOCKS)) - jnp.sum(blocks)

    def squares(rows):
        floats = rows.astype(jnp.float32)
        return jnp.sum(floats * floats, axis=1)

    text_own = lax.dynamic_slice_in_dim(text_rows, text_block * TILE, TILE, 0)
    spread = jnp.concatenate([squares(vis_rows), squares(text_own)]).reshape(BLOCKS, TILE)

    def share(value, bits):
        return jnp.concatenate([value, swap_dp(value, bits)], axis=0)

    def piece(step):
        rows = lax.dynamic_index_in_dim(pieces, (x_at + step) % 4, 0, keepdims=False)
        rows = lax.dynamic_index_in_dim(rows, core, 1, keepdims=False)
        first = lax.dynamic_index_in_dim(rows, high, 0, keepdims=False)
        second = lax.dynamic_index_in_dim(rows, 1 - high, 0, keepdims=False)
        return jnp.concatenate([first, second], axis=0)

    others = [swap_tensor(vis_rows[: 2 * TILE], 1)]
    q_here = mirror_z(q_weight)
    spread = spread + swap_tensor(spread, 2)
    gathered = share(share(tile_block, 2), 1)
    pieces = kv_weight.reshape(4, 2, 2, CORE_PART, WIDE)
    kv_pieces = [piece(step) for step in range(4)]

    q_here, spread, gathered, rows, *kv_pieces = lock(
        (q_here, spread, gathered, vis_rows, *kv_pieces), others
    )
    others.append(swap_tensor(rows[2 * TILE : 4 * TILE], 1))
    q_here = slide_x(q_here)
    spread = spread + swap_tensor(spread, 4)
    kv_third, kv_first = shift_x(kv_pieces[1], 1), shift_x(kv_pieces[3], 3)

    tables = rope_tables(SEQ, HD)
    q_here, spread, gathered, rows, kv_far, kv_first, kv_third, *tables = lock(
        (q_here, spread, gathered, vis_rows, kv_pieces[2], kv_first, kv_third, *tables), others
    )
    q_low = swap_dp(q_here, 2)
    others.append(swap_tensor(rows[4 * TILE : 5 * TILE], 1))
    spread = spread + swap_tensor(spread, 1)
    kv_second = shift_x(kv_far, 2)
    gathered = share(share(gathered, 4), 8)
    last = jnp.concatenate([rows[5 * TILE :], text_own], axis=0)

    own_half = low == high
    q_pair = jnp.concatenate(
        [jnp.where(own_half, q_here, q_low), jnp.where(own_half, q_low, q_here)], axis=0
    )
    q_pair, last, spread, *kv_pieces = lock(
        (q_pair, last, spread, kv_pieces[0], kv_first, kv_second, kv_third), others
    )
    other_last = swap_tensor(last, 1)
    q_pairs = [q_pair[:, :WIDE], q_pair[:, WIDE:]]

    def over_z(pair):
        return [pair] + [shift_z(pair, step) for step in range(1, 4)]

    q_blocks = over_z(q_pairs[0])
    kv_mine = jnp.stack(kv_pieces)
    kv_theirs = swap_dp(kv_mine, 1)

    scale = lax.rsqrt(spread / width + eps).reshape(SEQ, 1)
    gains = norm_gain.reshape(8, 1, PART)
    gain_own = lax.dynamic_index_in_dim(gains, tensor_at, 0, keepdims=False)
    gain_other = lax.dynamic_index_in_dim(gains, tensor_at ^ 1, 0, keepdims=False)
    own = norm_rows(
        jnp.stack([text_block, core]), (vis_rows, text_rows), ((0, 6), (6, 7)), scale, gain_own
    )
    plain = jnp.stack([jnp.int32(0), core])
    other = norm_rows(
        plain, (*others, other_last), ((0, 2), (2, 4), (4, 5), (5, 7)), scale, gain_other
    )

    held = lock((other, own, kv_theirs, q_pairs[1], *q_blocks), ())
    other, own, kv_theirs, q_late = held[:4]
    q_mine = jnp.stack(held[4:])
    q_theirs = swap_dp(q_mine, 1)
    order = [0]
    for bits in (2, 1, 4, 8):
        order = order + [entry ^ bits for entry in order]

    owner_ids = jnp.arange(shards, dtype=jnp.int32)
    source_of = jnp.sum(jnp.where(tile_dest == me, owner_ids[:, None], 0), axis=0)
    my_dest = lax.dynamic_slice_in_dim(tile_dest, me, 1, 0)[0]
    sent = (me ^ jnp.array(order, jnp.int32))[:, None] == my_dest[None, :]
    spots = jnp.concatenate([jnp.sum(jnp.where(sent, gathered, 0), axis=0), text_block[None]])
    dest = jnp.concatenate([my_dest, my_dest[-1:]])
    at_block = blocks[None, :] == jnp.arange(BLOCKS, dtype=jnp.int32)[:, None]
    source = jnp.sum(jnp.where(at_block, source_of[None, :], 0), axis=1)
    text_at = text_block[None]
    ends = jnp.cumsum(doc_lens[0])

    weights = [(kv_mine, kv_theirs, 0), (q_mine, q_theirs, 0)]
    token = []

    def parts(chunk, turns):
        at = []
        for turn in turns:
            group = jnp.where(core == 0, (4 - turn) % 4, turn)
            at.append(group if chunk == 0 else (z_at - group) % 4)
        dtypes = [jnp.bfloat16 if turn else jnp.float32 for turn in turns]
        at = jnp.stack(at).astype(jnp.int32)
        outs = parts_of(at, own, other, *weights[chunk], dtypes, token)
        token[:] = outs[:1]
        return list(outs)

    sums = [parts(0, (1,)), parts(1, (1,))]
    (q_late,) = lock((q_late,), sums[1])
    q_blocks = over_z(q_late)
    sums[0] += parts(0, (2, 3, 0))

    arrived, done = {}, []
    for chunk, turn in [(0, 1), (1, 1), (0, 2), (1, 2), (0, 3), (1, 3), (2, 1), (2, 2), (2, 3)]:
        if (chunk, turn) == (1, 2):
            token[:] = [rows]
            sums[1] += parts(1, (2, 3, 0))
            q_mine = jnp.stack(lock(q_blocks, sums[1][3:]))
            weights.append((q_mine, swap_dp(q_mine, 1), 0))
            sums.append(parts(2, (1, 2, 3, 0)))
        if (chunk, turn) == (2, 1):
            (arrived[0],) = lock((arrived[0],), sums[2][:1])
        rows = sums[chunk][turn - 1]
        guards = done[-2:-1]
        if turn > 1:
            rows, got = lock((rows, arrived[chunk]), guards)
            rows = (rows.astype(jnp.float32) + got.astype(jnp.float32)).astype(jnp.bfloat16)
        elif guards:
            (rows,) = lock((rows,), guards)
        arrived[chunk] = ring_x(rows)
        done.append(arrived[chunk])

    biases = [kv_bias.reshape(1, WIDE), q_bias[None, :WIDE], q_bias[None, WIDE:]]
    routed = []
    for chunks, rotated in (((0, 1), (1, 0, 1, 1)), ((2,), (1, 1))):
        slots, text = finish(
            rotated,
            dest,
            spots,
            [sums[chunk][3] for chunk in chunks],
            [arrived[chunk] for chunk in chunks],
            [biases[chunk] for chunk in chunks],
            tables,
            shards,
        )
        filled = lax.all_to_all(slots, "dp", split_axis=0, concat_axis=0, tiled=True)
        routed.append((filled, text))
    pair = gather_pair(source, text_at, *routed[0])
    context = attend(source, text_at, ends, *routed[0], *pair, None, 0, 1)
    return attend(source, text_at, ends, *routed[1], *pair, context, 1, 0)


def solution(mesh):
    in_specs = (
        P("dp", "tensor"),
        P("dp", "tensor"),
        P("dp", "tensor"),
        P(None, None, "tensor"),
        P("tensor"),
        P(None, "tensor"),
        P(),
        P(),
        P("dp", None),
        P("dp", None),
    )
    out_specs = P("dp", "tensor")
    return jax.shard_map(local, mesh=mesh, in_specs=in_specs, out_specs=out_specs, check_vma=False)
```

time: 330 us -> 316 us (0.958)
  waiting for transfers between devices: 108 us -> 94.3 us
  starting transfers between devices: 69.6 us -> 77 us
  other arithmetic: 32.6 us -> 27.5 us
  local copies, waits for them, and re-layouts: 27.2 us -> 22.2 us
    ppermute x3 -> x6, waiting for transfers between devices: 31.2 us -> 6.02 us  [shift_z(): lax.ppermute(value, 'dp', [(d, (d + 4 * step) % 16) for d in range(16)])]
    ppermute x3 -> x6, starting transfers between devices: 3.55 us -> 16.1 us  [shift_z(): lax.ppermute(value, 'dp', [(d, (d + 4 * step) % 16) for d in range(16)])]
    ppermute x9, waiting for transfers between devices: 27.4 us -> 38.5 us  [ring_x(): return lax.ppermute(value, ('dp', 'tensor'), pairs)]
    ppermute x7, waiting for transfers between devices: 17.8 us -> 27.4 us  [swap_tensor(): return lax.ppermute(value, 'tensor', [(t, t ^ bits) for t in range(8)])]
    ppermute x3, waiting for transfers between devices: 8.99 us -> 0.84 us  [shift_x(): return lax.ppermute(value, 'tensor', pairs)]
    pallas_call x4 -> x6, Pallas kernels: 39.2 us -> 46.3 us  [the longest x5 41.7 us: parts_of(): pl.pallas_call(functools.partial(part_kernel, count), grid_spec=grid_spec...]
    all_to_all x3 -> x2, waiting for transfers between devices: 22 us -> 16.5 us  [local(): lax.all_to_all(slots, 'dp', split_axis=0, concat_axis=0, tiled=True)]
    pallas_call x2, Pallas kernels: 29.2 us -> 24.1 us  [attend(): pl.pallas_call(body, grid_spec=grid_spec, out_shape=jax.ShapeDtypeStruct(...]
  transfers between devices with their start and end apart: 34 -> 37, of which waited for: 15 -> 20; matrix products, arithmetic and copies ran while one was open for 14% -> 13% of each run, Pallas kernels for 20% -> 24%
where the time goes in v3:
time: 316 us; the launch traced here: 315 us
  waiting for transfers between devices  94.3 us (30%)
  Pallas kernels  92.8 us (29%)
  starting transfers between devices  77 us (24%)
  other arithmetic  27.5 us (9%)
  local copies, waits for them, and re-layouts  22.2 us (7%)
    pallas_call x5, Pallas kernels, parts_of(): pl.pallas_call(functools.partial(part_kernel, count), grid_spec=grid_spec...  41.7 us
    ppermute x9, waiting for transfers between devices, ring_x(): return lax.ppermute(value, ('dp', 'tensor'), pairs)  38.5 us
    ppermute x7, waiting for transfers between devices, swap_tensor(): return lax.ppermute(value, 'tensor', [(t, t ^ bits) for t in range(8)])  27.4 us
    pallas_call x2, Pallas kernels, attend(): pl.pallas_call(body, grid_spec=grid_spec, out_shape=jax.ShapeDtypeStruct(...  24.1 us
    all_to_all x2, waiting for transfers between devices, local(): lax.all_to_all(slots, 'dp', split_axis=0, concat_axis=0, tiled=True)  16.5 us
    ppermute x6, starting transfers between devices, shift_z(): lax.ppermute(value, 'dp', [(d, (d + 4 * step) % 16) for d in range(16)])  16.1 us
    all_to_all x2, starting transfers between devices, local(): lax.all_to_all(slots, 'dp', split_axis=0, concat_axis=0, tiled=True)  13.5 us
    pallas_call x2, Pallas kernels, norm_rows(): pl.pallas_call(functools.partial(norm_kernel, bounds, begin), grid_spec=g...  12.4 us
  transfers between devices with their start and end apart: 37, of which 20 were waited for; matrix products, arithmetic and copies ran while one was open for 13% of the time, Pallas kernels for 24%

profile of v3, /device:TPU:1, one launch (start us, length us, event | category | flops | bytes accessed | tf_op | source)
XLA Modules:
  0.0 314.9 jit_solution(10783328296560829210)
XLA Ops:
  0.0 2.1 collective-permute-start.2
  2.1 2.3 slice.32
  4.4 2.6 collective-permute-start.4
  7.0 2.6 multiply_reduce_fusion
  10.9 1.9 multiply_reduce_fusion.1
  14.2 5.4 %collective-permute-start = (bf16[512,512]{1,0:T(8,128)(2,1)}, bf16[512,512]{1,0:T(8,128)(2,1)}, u32[]{:S(2)}, u32[]{:S(2)}) collective-permute-start(bf16[512,512]{1,0:T(8,128)(2,1)} %param.13), channel_id=1, source_target_pairs={{0,0},{1,1},{2,34},{3,35},{4,68},{5,69},{6,102},{7,103},{8,8},{9,9... | collective-permute-start | bytes 1572872 | tf_op jit(solution)/shard_map/ppermute | solution.py:94
  19.6 7.6 %reshape.79 = bf16[4,2,2,512,256]{4,3,2,1,0:T(8,128)(2,1)} reshape(bf16[8192,2,128]{2,1,0:T(2,128)(2,1)} %param.14) | data formatting | bytes 8388608 | tf_op jit(solution)/shard_map/reshape | solution.py:444
  33.6 5.4 %collective-permute-start.5 = (bf16[512,512]{1,0:T(8,128)(2,1)}, bf16[512,512]{1,0:T(8,128)(2,1)}, u32[]{:S(2)}, u32[]{:S(2)}) collective-permute-start(bf16[512,512]{1,0:T(8,128)(2,1)} %collective-permute-done), channel_id=1, source_target_pairs={{0,0},{1,1},{2,2},{3,3},{4,4},{5,5},{6,6},{7,7},{8,8},{9,9},{10,10... | collective-permute-start | bytes 1572872 | tf_op jit(solution)/shard_map/ppermute | solution.py:102
  38.9 2.5 collective-permute-start.7
  41.5 3.4 %fusion.2 = (f32[1792,64]{1,0:T(8,128)S(1)}, f32[1792,64]{1,0:T(8,128)S(1)}, f32[1792,64]{1,0:T(8,128)S(1)}) fusion(f32[64]{0:T(128)S(1)} %multiply_power_fusion), kind=kLoop, calls=%fused_computation.24 | loop fusion | flops 229376 | bytes 1376512 | tf_op jit(solution)/shard_map/neg | solution.py:43
  46.2 1.9 collective-permute-start.6
  49.4 4.9 %collective-permute-done.6 = f32[7,256]{1,0:T(8,128)S(1)} collective-permute-done((f32[7,256]{1,0:T(8,128)S(1)}, f32[7,256]{1,0:T(8,128)S(1)}, u32[]{:S(2)}, u32[]{:S(2)}) %collective-permute-start.6) | collective-permute-done | bytes 7200 | tf_op jit(solution)/shard_map/ppermute | solution.py:55
  54.7 4.5 %collective-permute-done.9.refs_1_ = bf16[512,1024]{1,0:T(8,128)(2,1)S(1)} collective-permute-done((bf16[512,1024]{1,0:T(8,128)(2,1)S(1)}, bf16[512,1024]{1,0:T(8,128)(2,1)S(1)}, u32[]{:S(2)}, u32[]{:S(2)}) %collective-permute-start.9) | collective-permute-done | bytes 1048608 | tf_op jit(solution)/shard_map/ppermute | solution.py:55
  60.8 3.3 %collective-permute-start.15 = (bf16[1024,256]{1,0:T(8,128)(2,1)}, bf16[1024,256]{1,0:T(8,128)(2,1)S(1)}, u32[]{:S(2)}, u32[]{:S(2)}) collective-permute-start(bf16[1024,256]{1,0:T(8,128)(2,1)} %pad_maximum_fusion.9), channel_id=1, source_target_pairs={{0,4},{1,5},{2,6},{3,7},{4,0},{5,1},{6,2},{7,3},{8,12},{9,13},{10,... | collective-permute-start | bytes 1572872 | tf_op jit(solution)/shard_map/ppermute | solution.py:51
  64.2 2.1 collective-permute-start.12
  67.3 4.2 %collective-permute-done.14 = f32[7,256]{1,0:T(8,128)S(1)} collective-permute-done((f32[7,256]{1,0:T(8,128)S(1)}, f32[7,256]{1,0:T(8,128)S(1)}, u32[]{:S(2)}, u32[]{:S(2)}) %collective-permute-start.14) | collective-permute-done | bytes 7200 | tf_op jit(solution)/shard_map/ppermute | solution.py:55
  74.5 8.3 %collective-permute-done.12.refs_2_ = bf16[256,1024]{1,0:T(8,128)(2,1)S(1)} collective-permute-done((bf16[256,1024]{1,0:T(8,128)(2,1)S(1)}, bf16[256,1024]{1,0:T(8,128)(2,1)S(1)}, u32[]{:S(2)}, u32[]{:S(2)}) %collective-permute-start.12) | collective-permute-done | bytes 524320 | tf_op jit(solution)/shard_map/ppermute | solution.py:55
  85.3 2.5 collective-permute-start.17
  87.8 2.3 collective-permute-start.16
  91.2 6.5 %collective-permute-start.20 = (bf16[1024,256]{1,0:T(8,128)(2,1)}, bf16[1024,256]{1,0:T(8,128)(2,1)}, u32[]{:S(2)}, u32[]{:S(2)}) collective-permute-start(bf16[1024,256]{1,0:T(8,128)(2,1)} %get-tuple-element.97), channel_id=1, source_target_pairs={{0,96},{8,104},{16,112},{24,120},{32,0},{40,8},{48,16},{56,24},{64... | collective-permute-start | bytes 1572872 | tf_op jit(solution)/shard_map/ppermute | solution.py:86
  103.0 5.8 %norm_rows.3.own = bf16[1792,1024]{1,0:T(8,128)(2,1)} custom-call(s32[2]{0:T(128)S(1)} %get-tuple-element.167.picks, bf16[1536,1024]{1,0:T(8,128)(2,1)S(1)} %copy-done, bf16[1792,1024]{1,0:T(8,128)(2,1)} %refs_1_.1, f32[1792,1]{1,0:T(8,128)S(1)} %bitcast.53, f32[1,1024]{1,0:T(1,128)S(1)} %get-tuple-element.157.refs_3_), custom_call_target="tpu_custom_call" | custom-call | tf_op jit(solution)/shard_map/norm_rows/pallas_call | solution.py:155
  108.9 5.6 %collective-permute-done.16.refs_3_ = bf16[512,1024]{1,0:T(8,128)(2,1)} collective-permute-done((bf16[512,1024]{1,0:T(8,128)(2,1)}, bf16[512,1024]{1,0:T(8,128)(2,1)}, u32[]{:S(2)}, u32[]{:S(2)}) %collective-permute-start.16) | collective-permute-done | bytes 1048608 | tf_op jit(solution)/shard_map/ppermute | solution.py:55
  114.5 6.5 %norm_rows.2.other = bf16[1792,1024]{1,0:T(8,128)(2,1)} custom-call(s32[2]{0:T(128)S(1)} %get-tuple-element.166.picks, bf16[512,1024]{1,0:T(8,128)(2,1)} %collective-permute-done.4.refs_0_, bf16[512,1024]{1,0:T(8,128)(2,1)S(1)} %copy-done.12, bf16[256,1024]{1,0:T(8,128)(2,1)S(1)} %copy-done.18, bf16[512,1024]{1,0:T(8,128)(2,1)} %collective-permute-done.16.refs_3_, ...), custom_call_target="tpu_custom_call" | custom-call | tf_op jit(solution)/shard_map/norm_rows/pallas_call | solution.py:155
  121.0 3.5 %collective-permute-done.18 = bf16[1024,256]{1,0:T(8,128)(2,1)} collective-permute-done((bf16[1024,256]{1,0:T(8,128)(2,1)}, bf16[1024,256]{1,0:T(8,128)(2,1)}, u32[]{:S(2)}, u32[]{:S(2)}) %collective-permute-start.18) | collective-permute-done | bytes 524320 | tf_op jit(solution)/shard_map/ppermute | solution.py:86
  124.5 1.8 pad_maximum_fusion.1.rest_0_.rest_2_.rest_4_
  127.0 5.4 %part_rows.5.rest_2_ = bf16[1792,256]{1,0:T(8,128)(2,1)S(1)} custom-call(s32[1]{0:T(128)} %bitcast.29.at, bf16[1792,1024]{1,0:T(8,128)(2,1)} %norm_rows.3.own, bf16[1792,1024]{1,0:T(8,128)(2,1)} %norm_rows.2.other, bf16[4,1024,256]{2,1,0:T(8,128)(2,1)} %pad_maximum_fusion.rest_0_.rest_2_.rest_4_, ...), custom_call_target="tpu_custom_call" | custom-call | flops 1879048192 | bytes 7340032 | tf_op jit(solution)/shard_map/part_rows/pallas_call | solution.py:200
  132.7 5.3 %part_rows.6.rest_6_ = bf16[1792,256]{1,0:T(8,128)(2,1)S(1)} custom-call(s32[1]{0:T(128)} %bitcast.13.at, bf16[1792,1024]{1,0:T(8,128)(2,1)} %norm_rows.3.own, bf16[1792,1024]{1,0:T(8,128)(2,1)} %norm_rows.2.other, bf16[4,1024,256]{2,1,0:T(8,128)(2,1)S(1)} %pad_maximum_fusion.1.rest_0_.rest_2_.rest_4_, ...), custom_call_target="tpu_custom_call" | custom-call | flops 1879048192 | bytes 7340032 | tf_op jit(solution)/shard_map/part_rows/pallas_call | solution.py:200
  138.0 5.6 %collective-permute-start.24 = (bf16[1024,256]{1,0:T(8,128)(2,1)S(1)}, bf16[1024,256]{1,0:T(8,128)(2,1)S(1)}, u32[]{:S(2)}, u32[]{:S(2)}) collective-permute-start(bf16[1024,256]{1,0:T(8,128)(2,1)S(1)} %copy-done.23), channel_id=1, source_target_pairs={{0,96},{8,104},{16,112},{24,120},{32,0},{40,8},{48,16},{56,24},{64... | collective-permute-start | bytes 1572872 | tf_op jit(solution)/shard_map/ppermute | solution.py:86
  145.7 9.5 %part_rows.7 = (bf16[1792,256]{1,0:T(8,128)(2,1)S(1)}, bf16[1792,256]{1,0:T(8,128)(2,1)S(1)}, f32[1792,256]{1,0:T(8,128)S(1)}) custom-call(s32[3]{0:T(128)S(1)} %get-tuple-element.169.at, bf16[1792,1024]{1,0:T(8,128)(2,1)} %norm_rows.3.own, bf16[1792,1024]{1,0:T(8,128)(2,1)} %norm_rows.2.other, ...), custom_call_target="tpu_custom_call" | custom-call | flops 5637144576 | bytes 7340032 | tf_op jit(solution)/shard_map/part_rows/pallas_call | solution.py:200
  158.2 9.5 %part_rows.8 = (bf16[1792,256]{1,0:T(8,128)(2,1)S(1)}, bf16[1792,256]{1,0:T(8,128)(2,1)S(1)}, f32[1792,256]{1,0:T(8,128)S(1)}) custom-call(s32[3]{0:T(128)S(1)} %get-tuple-element.168.at, bf16[1792,1024]{1,0:T(8,128)(2,1)} %norm_rows.3.own, bf16[1792,1024]{1,0:T(8,128)(2,1)} %norm_rows.2.other, bf16[4,1024,256]{2,1,0:T(8,128)(2,1)} %copy-done.1, ...), custom_call_target="tpu_custom_call" | custom-call | flops 5637144576 | bytes 7340032 | tf_op jit(solution)/shard_map/part_rows/pallas_call | solution.py:200
  167.7 2.5 collective-permute-done.22
  174.8 2.0 collective-permute-start.10
  180.5 1.8 collective-permute-done.11
  184.8 2.3 collective-permute-done.31
  190.9 12.1 %part_rows.9 = (bf16[1792,256]{1,0:T(8,128)(2,1)S(1)}, bf16[1792,256]{1,0:T(8,128)(2,1)S(1)}, bf16[1792,256]{1,0:T(8,128)(2,1)S(1)}, f32[1792,256]{1,0:T(8,128)S(1)}) custom-call(s32[4]{0:T(128)S(1)} %pad_add_fusion.5.at, bf16[1792,1024]{1,0:T(8,128)(2,1)} %norm_rows.3.own, bf16[1792,1024]{1,0:T(8,128)(2,1)} %norm_rows.2.other, ...), custom_call_target="tpu_custom_call" | custom-call | flops 7516192768 | bytes 7340032 | tf_op jit(solution)/shard_map/part_rows/pallas_call | solution.py:200
  206.7 6.3 %finish_rows.3 = (bf16[16,256,512]{2,1,0:T(8,128)(2,1)}, bf16[256,512]{1,0:T(8,128)(2,1)S(1)}) custom-call(s32[7]{0:T(128)S(1)} %get-tuple-element.164.dest, s32[7]{0:T(128)S(1)} %get-tuple-element.165.spots, f32[1792,256]{1,0:T(8,128)S(1)} %copy-done.7, f32[1792,256]{1,0:T(8,128)} %copy-done.8, bf16[1792,256]{1,0:T(8,128)(2,1)S(1)} %collective-permute-done.28.refs_2_, ...), custom_call_target="tpu_custom_call" | custom-call | flops 7340032 | bytes 9175040 | tf_op jit(solution)/shard_map/finish_rows/pallas_call | solution.py:261
  213.0 8.8 %all-to-all-start.1 = ((bf16[16,256,512]{2,1,0:T(8,128)(2,1)}), bf16[16,256,512]{2,1,0:T(8,128)(2,1)}, u32[]{:S(2)}, u32[]{:S(2)}) async-start(bf16[16,256,512]{2,1,0:T(8,128)(2,1)} %get-tuple-element.135), calls=%async_computation.1 | async-start | bytes 8388608 | tf_op jit(solution)/shard_map/all_to_all | solution.py:566
  221.9 12.8 %collective-permute-done.29 = bf16[1792,256]{1,0:T(8,128)(2,1)S(1)} collective-permute-done((bf16[1792,256]{1,0:T(8,128)(2,1)}, bf16[1792,256]{1,0:T(8,128)(2,1)S(1)}, u32[]{:S(2)}, u32[]{:S(2)}) %collective-permute-start.29) | collective-permute-done | bytes 917536 | tf_op jit(solution)/shard_map/ppermute | solution.py:82
  236.3 11.4 %collective-permute-done.33 = bf16[1792,256]{1,0:T(8,128)(2,1)S(1)} collective-permute-done((bf16[1792,256]{1,0:T(8,128)(2,1)S(1)}, bf16[1792,256]{1,0:T(8,128)(2,1)S(1)}, u32[]{:S(2)}, u32[]{:S(2)}) %collective-permute-start.33) | collective-permute-done | bytes 917536 | tf_op jit(solution)/shard_map/ppermute | solution.py:82
  248.0 2.5 collective-permute-start.34
  250.4 10.3 %collective-permute-done.34.refs_1_ = bf16[1792,256]{1,0:T(8,128)(2,1)S(1)} collective-permute-done((bf16[1792,256]{1,0:T(8,128)(2,1)S(1)}, bf16[1792,256]{1,0:T(8,128)(2,1)S(1)}, u32[]{:S(2)}, u32[]{:S(2)}) %collective-permute-start.34) | collective-permute-done | bytes 917536 | tf_op jit(solution)/shard_map/ppermute | solution.py:82
  260.8 3.8 %finish_rows.2 = (bf16[16,256,256]{2,1,0:T(8,128)(2,1)}, bf16[256,256]{1,0:T(8,128)(2,1)S(1)}) custom-call(s32[7]{0:T(128)S(1)} %get-tuple-element.164.dest, s32[7]{0:T(128)S(1)} %get-tuple-element.165.spots, f32[1792,256]{1,0:T(8,128)S(1)} %copy-done.10, bf16[1792,256]{1,0:T(8,128)(2,1)S(1)} %collective-permute-done.34.refs_1_, f32[1,256]{1,0:T(1,128)S(1)} %bitcast.56, ...), custom_call_target="tpu_custom_call" | custom-call | flops 3670016 | bytes 4587520 | tf_op jit(solution)/shard_map/finish_rows/pallas_call | solution.py:261
  264.6 7.0 %all-to-all-done.1.slots.refs_3_ = bf16[16,256,512]{2,1,0:T(8,128)(2,1)} async-done(((bf16[16,256,512]{2,1,0:T(8,128)(2,1)}), bf16[16,256,512]{2,1,0:T(8,128)(2,1)}, u32[]{:S(2)}, u32[]{:S(2)}) %all-to-all-start.1) | async-done | bytes 4194336 | tf_op jit(solution)/shard_map/all_to_all | solution.py:566
  271.6 4.6 %all-to-all-start = ((bf16[16,256,256]{2,1,0:T(8,128)(2,1)}), bf16[16,256,256]{2,1,0:T(8,128)(2,1)S(1)}, u32[]{:S(2)}, u32[]{:S(2)}) async-start(bf16[16,256,256]{2,1,0:T(8,128)(2,1)} %get-tuple-element.131), calls=%async_computation | async-start | bytes 4194304 | tf_op jit(solution)/shard_map/all_to_all | solution.py:566
  276.7 4.6 %gather_pair.1 = (bf16[1792,128]{1,0:T(8,128)(2,1)S(1)}, bf16[144,1792]{1,0:T(8,128)(2,1)S(1)}) custom-call(s32[7]{0:T(128)S(1)} %select_reduce_fusion.source.refs_0_, s32[1]{0:T(128)} %bitcast.1.text_at.refs_1_, bf16[16,256,512]{2,1,0:T(8,128)(2,1)} %all-to-all-done.1.slots.refs_3_, bf16[256,512]{1,0:T(8,128)(2,1)S(1)} %get-tuple-element.136.text.refs_4_), custom_call_target="tpu_custom_call" | custom-call | flops 458752 | bytes 1835008 | tf_op jit(solution)/shard_map/gather_pair/pallas_call | solution.py:304
  281.3 12.6 %attend.2.refs_7_ = bf16[1792,512]{1,0:T(8,128)(2,1)} custom-call(s32[7]{0:T(128)S(1)} %select_reduce_fusion.source.refs_0_, s32[1]{0:T(128)} %bitcast.1.text_at.refs_1_, s32[4]{0:T(128)S(1)} %bitcast.58, bf16[16,256,512]{2,1,0:T(8,128)(2,1)} %all-to-all-done.1.slots.refs_3_, bf16[256,512]{1,0:T(8,128)(2,1)S(1)} %get-tuple-element.136.text.refs_4_, ...), custom_call_target="tpu_custom_call" | custom-call | flops 3288334336 | bytes 2752512 | tf_op jit(solution)/shard_map/attend/pallas_call | solution.py:391
  293.8 9.5 %all-to-all-done.refs_3_ = bf16[16,256,256]{2,1,0:T(8,128)(2,1)S(1)} async-done(((bf16[16,256,256]{2,1,0:T(8,128)(2,1)}), bf16[16,256,256]{2,1,0:T(8,128)(2,1)S(1)}, u32[]{:S(2)}, u32[]{:S(2)}) %all-to-all-start) | async-done | bytes 2097184 | tf_op jit(solution)/shard_map/all_to_all | solution.py:566
  303.4 11.5 %attend.3 = bf16[1792,512]{1,0:T(8,128)(2,1)} custom-call(s32[7]{0:T(128)S(1)} %select_reduce_fusion.source.refs_0_, s32[1]{0:T(128)} %bitcast.1.text_at.refs_1_, s32[4]{0:T(128)S(1)} %bitcast.59, bf16[16,256,256]{2,1,0:T(8,128)(2,1)S(1)} %all-to-all-done.refs_3_, bf16[256,256]{1,0:T(8,128)(2,1)S(1)} %get-tuple-element.132.refs_4_, ...), custom_call_target="tpu_custom_call", output_to_operand_aliasing={{}: (7, {})} | custom-call | flops 3288334336 | bytes 2752512 | tf_op jit(solution)/shard_map/attend/pallas_call | solution.py:391
  (160 shorter events, 52.7 us)
Async XLA Ops:
  0.0 30.6 %collective-permute-start.2 = (s32[1,6]{1,0:T(1,128)}, s32[1,6]{1,0:T(1,128)S(1)}, u32[]{:S(2)}, u32[]{:S(2)}) collective-permute-start(s32[1,6]{1,0:T(1,128)} %param.19), channel_id=1, source_target_pairs={{0,16},{8,24},{16,0},{24,8},{32,48},{40,56},{48,32},{56,40},{64,80... | collective-permute-start | bytes 80 | tf_op jit(solution)/shard_map/ppermute | solution.py:59
  4.4 28.6 %collective-permute-start.4 = (bf16[512,1024]{1,0:T(8,128)(2,1)}, bf16[512,1024]{1,0:T(8,128)(2,1)}, u32[]{:S(2)}, u32[]{:S(2)}) collective-permute-start(bf16[512,1024]{1,0:T(8,128)(2,1)} %slice.32), channel_id=1, source_target_pairs={{0,1},{1,0},{2,3},{3,2},{4,5},{5,4},{6,7},{7,6},{8,9},{9,8},{10,11... | collective-permute-start | bytes 3145736 | tf_op jit(solution)/shard_map/ppermute | solution.py:55
  12.9 20.1 %collective-permute-start.1 = (f32[7,256]{1,0:T(8,128)S(1)}, f32[7,256]{1,0:T(8,128)S(1)}, u32[]{:S(2)}, u32[]{:S(2)}) collective-permute-start(f32[7,256]{1,0:T(8,128)S(1)} %reshape.78), channel_id=1, source_target_pairs={{0,2},{1,3},{2,0},{3,1},{4,6},{5,7},{6,4},{7,5},{8,10},{9,11},{10,... | collective-permute-start | bytes 21512 | tf_op jit(solution)/shard_map/ppermute | solution.py:55
  14.2 18.8 %collective-permute-start = (bf16[512,512]{1,0:T(8,128)(2,1)}, bf16[512,512]{1,0:T(8,128)(2,1)}, u32[]{:S(2)}, u32[]{:S(2)}) collective-permute-start(bf16[512,512]{1,0:T(8,128)(2,1)} %param.13), channel_id=1, source_target_pairs={{0,0},{1,1},{2,34},{3,35},{4,68},{5,69},{6,102},{7,103},{8,8},{9,9... | collective-permute-start | bytes 1572872 | tf_op jit(solution)/shard_map/ppermute | solution.py:94
  30.6 2.4 collective-permute-start.3
  33.1 26.0 %collective-permute-start.9 = (bf16[512,1024]{1,0:T(8,128)(2,1)S(1)}, bf16[512,1024]{1,0:T(8,128)(2,1)S(1)}, u32[]{:S(2)}, u32[]{:S(2)}) collective-permute-start(bf16[512,1024]{1,0:T(8,128)(2,1)S(1)} %slice.33), channel_id=1, source_target_pairs={{0,1},{1,0},{2,3},{3,2},{4,5},{5,4},{6,7},{7,6},{8,9},{9,8},{10,11... | collective-permute-start | bytes 3145736 | tf_op jit(solution)/shard_map/ppermute | solution.py:55
  33.6 20.7 %collective-permute-start.5 = (bf16[512,512]{1,0:T(8,128)(2,1)}, bf16[512,512]{1,0:T(8,128)(2,1)}, u32[]{:S(2)}, u32[]{:S(2)}) collective-permute-start(bf16[512,512]{1,0:T(8,128)(2,1)} %collective-permute-done), channel_id=1, source_target_pairs={{0,0},{1,1},{2,2},{3,3},{4,4},{5,5},{6,6},{7,7},{8,8},{9,9},{10,10... | collective-permute-start | bytes 1572872 | tf_op jit(solution)/shard_map/ppermute | solution.py:102
  38.9 15.3 %collective-permute-start.7 = (bf16[1024,256]{1,0:T(8,128)(2,1)S(1)}, bf16[1024,256]{1,0:T(8,128)(2,1)S(1)}, u32[]{:S(2)}, u32[]{:S(2)}) collective-permute-start(bf16[1024,256]{1,0:T(8,128)(2,1)S(1)} %pad_maximum_fusion.10), channel_id=1, source_target_pairs={{0,6},{1,7},{2,0},{3,1},{4,2},{5,3},{6,4},{7,5},{8,14},{9,15},{10,... | collective-permute-start | bytes 1572872 | tf_op jit(solution)/shard_map/ppermute | solution.py:51
  41.5 13.2 %collective-permute-start.8 = (bf16[1024,256]{1,0:T(8,128)(2,1)S(1)}, bf16[1024,256]{1,0:T(8,128)(2,1)S(1)}, u32[]{:S(2)}, u32[]{:S(2)}) collective-permute-start(bf16[1024,256]{1,0:T(8,128)(2,1)S(1)} %pad_maximum_fusion.8), channel_id=1, source_target_pairs={{0,2},{1,3},{2,4},{3,5},{4,6},{5,7},{6,0},{7,1},{8,10},{9,11},{10,... | collective-permute-start | bytes 1572872 | tf_op jit(solution)/shard_map/ppermute | solution.py:51
  46.2 8.0 %collective-permute-start.6 = (f32[7,256]{1,0:T(8,128)S(1)}, f32[7,256]{1,0:T(8,128)S(1)}, u32[]{:S(2)}, u32[]{:S(2)}) collective-permute-start(f32[7,256]{1,0:T(8,128)S(1)} %add.193), channel_id=1, source_target_pairs={{0,4},{1,5},{2,6},{3,7},{4,0},{5,1},{6,2},{7,3},{8,12},{9,13},{10,... | collective-permute-start | bytes 21512 | tf_op jit(solution)/shard_map/ppermute | solution.py:55
  60.1 12.6 %collective-permute-start.13 = (bf16[512,512]{1,0:T(8,128)(2,1)}, bf16[512,512]{1,0:T(8,128)(2,1)}, u32[]{:S(2)}, u32[]{:S(2)}) collective-permute-start(bf16[512,512]{1,0:T(8,128)(2,1)} %collective-permute-done.5), channel_id=1, source_target_pairs={{0,16},{8,24},{16,0},{24,8},{32,48},{40,56},{48,32},{56,40},{64,80... | collective-permute-start | bytes 1572872 | tf_op jit(solution)/shard_map/ppermute | solution.py:59
  60.1 11.4 %collective-permute-start.14 = (f32[7,256]{1,0:T(8,128)S(1)}, f32[7,256]{1,0:T(8,128)S(1)}, u32[]{:S(2)}, u32[]{:S(2)}) collective-permute-start(f32[7,256]{1,0:T(8,128)S(1)} %add.210), channel_id=1, source_target_pairs={{0,1},{1,0},{2,3},{3,2},{4,5},{5,4},{6,7},{7,6},{8,9},{9,8},{10,11... | collective-permute-start | bytes 21512 | tf_op jit(solution)/shard_map/ppermute | solution.py:55
  60.8 13.7 %collective-permute-start.15 = (bf16[1024,256]{1,0:T(8,128)(2,1)}, bf16[1024,256]{1,0:T(8,128)(2,1)S(1)}, u32[]{:S(2)}, u32[]{:S(2)}) collective-permute-start(bf16[1024,256]{1,0:T(8,128)(2,1)} %pad_maximum_fusion.9), channel_id=1, source_target_pairs={{0,4},{1,5},{2,6},{3,7},{4,0},{5,1},{6,2},{7,3},{8,12},{9,13},{10,... | collective-permute-start | bytes 1572872 | tf_op jit(solution)/shard_map/ppermute | solution.py:51
  64.2 18.6 %collective-permute-start.12 = (bf16[256,1024]{1,0:T(8,128)(2,1)S(1)}, bf16[256,1024]{1,0:T(8,128)(2,1)S(1)}, u32[]{:S(2)}, u32[]{:S(2)}) collective-permute-start(bf16[256,1024]{1,0:T(8,128)(2,1)S(1)} %get-tuple-element.152), channel_id=1, source_target_pairs={{0,1},{1,0},{2,3},{3,2},{4,5},{5,4},{6,7},{7,6},{8,9},{9,8},{10,11... | collective-permute-start | bytes 1572872 | tf_op jit(solution)/shard_map/ppermute | solution.py:55
  71.6 12.1 %copy-start.22 = (bf16[1024,256]{1,0:T(8,128)(2,1)S(1)}, bf16[1024,256]{1,0:T(8,128)(2,1)}, u32[]{:S(2)}) copy-start(bf16[1024,256]{1,0:T(8,128)(2,1)} %pad_maximum_fusion.7) | copy-start | bytes 1572868
  71.6 12.1 %copy-start.25 = (bf16[1024,256]{1,0:T(8,128)(2,1)S(1)}, bf16[1024,256]{1,0:T(8,128)(2,1)}, u32[]{:S(2)}) copy-start(bf16[1024,256]{1,0:T(8,128)(2,1)} %copy-done.24) | copy-start | bytes 1572868
  71.6 12.1 %copy-start.27 = (bf16[1024,256]{1,0:T(8,128)(2,1)S(1)}, bf16[1024,256]{1,0:T(8,128)(2,1)}, u32[]{:S(2)}) copy-start(bf16[1024,256]{1,0:T(8,128)(2,1)} %copy-done.26) | copy-start | bytes 1572868
  85.3 39.2 %collective-permute-start.17 = (bf16[4,1024,256]{2,1,0:T(8,128)(2,1)}, bf16[4,1024,256]{2,1,0:T(8,128)(2,1)}, u32[]{:S(2)}, u32[]{:S(2)}) collective-permute-start(bf16[4,1024,256]{2,1,0:T(8,128)(2,1)} %pad_maximum_fusion.rest_0_.rest_2_.rest_4_), channel_id=1, source_target_pairs={{0,8},{8,0},{16,24},{24,16},{32,40},{40,32},{48,56},{56,48},{64,72... | collective-permute-start | bytes 6291464 | tf_op jit(solution)/shard_map/ppermute | solution.py:59
  87.8 26.6 %collective-permute-start.16 = (bf16[512,1024]{1,0:T(8,128)(2,1)}, bf16[512,1024]{1,0:T(8,128)(2,1)}, u32[]{:S(2)}, u32[]{:S(2)}) collective-permute-start(bf16[512,1024]{1,0:T(8,128)(2,1)} %pad_maximum_fusion.4), channel_id=1, source_target_pairs={{0,1},{1,0},{2,3},{3,2},{4,5},{5,4},{6,7},{7,6},{8,9},{9,8},{10,11... | collective-permute-start | bytes 3145736 | tf_op jit(solution)/shard_map/ppermute | solution.py:55
  91.2 29.8 %collective-permute-start.20 = (bf16[1024,256]{1,0:T(8,128)(2,1)}, bf16[1024,256]{1,0:T(8,128)(2,1)}, u32[]{:S(2)}, u32[]{:S(2)}) collective-permute-start(bf16[1024,256]{1,0:T(8,128)(2,1)} %get-tuple-element.97), channel_id=1, source_target_pairs={{0,96},{8,104},{16,112},{24,120},{32,0},{40,8},{48,16},{56,24},{64... | collective-permute-start | bytes 1572872 | tf_op jit(solution)/shard_map/ppermute | solution.py:86
  97.6 23.4 %collective-permute-start.19 = (bf16[1024,256]{1,0:T(8,128)(2,1)}, bf16[1024,256]{1,0:T(8,128)(2,1)}, u32[]{:S(2)}, u32[]{:S(2)}) collective-permute-start(bf16[1024,256]{1,0:T(8,128)(2,1)} %get-tuple-element.97), channel_id=1, source_target_pairs={{0,64},{8,72},{16,80},{24,88},{32,96},{40,104},{48,112},{56,120},{... | collective-permute-start | bytes 1572872 | tf_op jit(solution)/shard_map/ppermute | solution.py:86
  98.9 25.6 %collective-permute-start.18 = (bf16[1024,256]{1,0:T(8,128)(2,1)}, bf16[1024,256]{1,0:T(8,128)(2,1)}, u32[]{:S(2)}, u32[]{:S(2)}) collective-permute-start(bf16[1024,256]{1,0:T(8,128)(2,1)} %get-tuple-element.97), channel_id=1, source_target_pairs={{0,32},{8,40},{16,48},{24,56},{32,64},{40,72},{48,80},{56,88},{64,... | collective-permute-start | bytes 1572872 | tf_op jit(solution)/shard_map/ppermute | solution.py:86
  103.0 11.4 %copy-start.18 = (bf16[256,1024]{1,0:T(8,128)(2,1)S(1)}, bf16[256,1024]{1,0:T(8,128)(2,1)}, u32[]{:S(2)}) copy-start(bf16[256,1024]{1,0:T(8,128)(2,1)} %copy-done.17) | copy-start | bytes 1572868
  126.3 6.3 %collective-permute-start.21 = (bf16[4,1024,256]{2,1,0:T(8,128)(2,1)S(1)}, bf16[4,1024,256]{2,1,0:T(8,128)(2,1)}, u32[]{:S(2)}, u32[]{:S(2)}) collective-permute-start(bf16[4,1024,256]{2,1,0:T(8,128)(2,1)S(1)} %pad_maximum_fusion.1.rest_0_.rest_2_.rest_4_), channel_id=1, source_target_pairs={{0,8},{8,0},{16,24},{24,16},{32,40},{40,32},{48,56},{56,48},{64,72... | collective-permute-start | bytes 6291464 | tf_op jit(solution)/shard_map/ppermute | solution.py:59
  132.4 24.1 %collective-permute-start.25 = (bf16[1792,256]{1,0:T(8,128)(2,1)S(1)}, bf16[1792,256]{1,0:T(8,128)(2,1)S(1)}, u32[]{:S(2)}, u32[]{:S(2)}) collective-permute-start(bf16[1792,256]{1,0:T(8,128)(2,1)S(1)} %part_rows.5.rest_2_), channel_id=1, source_target_pairs={{0,2},{1,3},{2,4},{3,5},{4,6},{5,7},{6,0},{7,1},{8,14},{9,15},{10,... | collective-permute-start | bytes 2752520 | tf_op jit(solution)/shard_map/ppermute | solution.py:82
  138.0 29.7 %collective-permute-start.24 = (bf16[1024,256]{1,0:T(8,128)(2,1)S(1)}, bf16[1024,256]{1,0:T(8,128)(2,1)S(1)}, u32[]{:S(2)}, u32[]{:S(2)}) collective-permute-start(bf16[1024,256]{1,0:T(8,128)(2,1)S(1)} %copy-done.23), channel_id=1, source_target_pairs={{0,96},{8,104},{16,112},{24,120},{32,0},{40,8},{48,16},{56,24},{64... | collective-permute-start | bytes 1572872 | tf_op jit(solution)/shard_map/ppermute | solution.py:86
  143.5 24.2 %collective-permute-start.23 = (bf16[1024,256]{1,0:T(8,128)(2,1)S(1)}, bf16[1024,256]{1,0:T(8,128)(2,1)S(1)}, u32[]{:S(2)}, u32[]{:S(2)}) collective-permute-start(bf16[1024,256]{1,0:T(8,128)(2,1)S(1)} %copy-done.23), channel_id=1, source_target_pairs={{0,64},{8,72},{16,80},{24,88},{32,96},{40,104},{48,112},{56,120},{... | collective-permute-start | bytes 1572872 | tf_op jit(solution)/shard_map/ppermute | solution.py:86
  144.7 25.5 %collective-permute-start.22 = (bf16[1024,256]{1,0:T(8,128)(2,1)S(1)}, bf16[1024,256]{1,0:T(8,128)(2,1)S(1)}, u32[]{:S(2)}, u32[]{:S(2)}) collective-permute-start(bf16[1024,256]{1,0:T(8,128)(2,1)S(1)} %copy-done.23), channel_id=1, source_target_pairs={{0,32},{8,40},{16,48},{24,56},{32,64},{40,72},{48,80},{56,88},{64,... | collective-permute-start | bytes 1572872 | tf_op jit(solution)/shard_map/ppermute | solution.py:86
  145.4 26.7 %collective-permute-start.30 = (bf16[1792,256]{1,0:T(8,128)(2,1)S(1)}, bf16[1792,256]{1,0:T(8,128)(2,1)S(1)}, u32[]{:S(2)}, u32[]{:S(2)}) collective-permute-start(bf16[1792,256]{1,0:T(8,128)(2,1)S(1)} %part_rows.6.rest_6_), channel_id=1, source_target_pairs={{0,2},{1,3},{2,4},{3,5},{4,6},{5,7},{6,0},{7,1},{8,14},{9,15},{10,... | collective-permute-start | bytes 2752520 | tf_op jit(solution)/shard_map/ppermute | solution.py:82
  157.7 24.7 %collective-permute-start.27 = (bf16[1792,256]{1,0:T(8,128)(2,1)}, bf16[1792,256]{1,0:T(8,128)(2,1)}, u32[]{:S(2)}, u32[]{:S(2)}) collective-permute-start(bf16[1792,256]{1,0:T(8,128)(2,1)} %add_convert_fusion.5.rest_6_), channel_id=1, source_target_pairs={{0,2},{1,3},{2,4},{3,5},{4,6},{5,7},{6,0},{7,1},{8,14},{9,15},{10,... | collective-permute-start | bytes 2752520 | tf_op jit(solution)/shard_map/ppermute | solution.py:82
  171.8 19.2 %collective-permute-start.26 = (bf16[4,1024,256]{2,1,0:T(8,128)(2,1)}, bf16[4,1024,256]{2,1,0:T(8,128)(2,1)}, u32[]{:S(2)}, u32[]{:S(2)}) collective-permute-start(bf16[4,1024,256]{2,1,0:T(8,128)(2,1)} %pad_maximum_fusion.2.rest_0_.rest_2_.rest_4_.rest_6_), channel_id=1, source_target_pairs={{0,8},{8,0},{16,24},{24,16},{32,40},{40,32},{48,56},{56,48},{64,72... | collective-permute-start | bytes 6291464 | tf_op jit(solution)/shard_map/ppermute | solution.py:59
  173.4 13.8 %collective-permute-start.31 = (bf16[1792,256]{1,0:T(8,128)(2,1)}, bf16[1792,256]{1,0:T(8,128)(2,1)}, u32[]{:S(2)}, u32[]{:S(2)}) collective-permute-start(bf16[1792,256]{1,0:T(8,128)(2,1)} %add_convert_fusion.3), channel_id=1, source_target_pairs={{0,2},{1,3},{2,4},{3,5},{4,6},{5,7},{6,0},{7,1},{8,14},{9,15},{10,... | collective-permute-start | bytes 2752520 | tf_op jit(solution)/shard_map/ppermute | solution.py:82
  174.8 3.4 %collective-permute-start.10 = (s32[4,6]{1,0:T(4,128)S(1)}, s32[4,6]{1,0:T(4,128)S(1)}, u32[]{:S(2)}, u32[]{:S(2)}) collective-permute-start(s32[4,6]{1,0:T(4,128)S(1)} %pad_add_fusion.1), channel_id=1, source_target_pairs={{0,32},{8,40},{16,48},{24,56},{32,0},{40,8},{48,16},{56,24},{64,96... | collective-permute-start | bytes 296 | tf_op jit(solution)/shard_map/ppermute | solution.py:59
  178.2 4.0 %collective-permute-start.11 = (s32[8,6]{1,0:T(8,128)S(1)}, s32[8,6]{1,0:T(8,128)S(1)}, u32[]{:S(2)}, u32[]{:S(2)}) collective-permute-start(s32[8,6]{1,0:T(8,128)S(1)} %pad_add_fusion), channel_id=1, source_target_pairs={{0,64},{8,72},{16,80},{24,88},{32,96},{40,104},{48,112},{56,120},{... | collective-permute-start | bytes 584 | tf_op jit(solution)/shard_map/ppermute | solution.py:59
  183.8 21.4 %collective-permute-start.28 = (bf16[1792,256]{1,0:T(8,128)(2,1)S(1)}, bf16[1792,256]{1,0:T(8,128)(2,1)S(1)}, u32[]{:S(2)}, u32[]{:S(2)}) collective-permute-start(bf16[1792,256]{1,0:T(8,128)(2,1)S(1)} %add_convert_fusion.4), channel_id=1, source_target_pairs={{0,2},{1,3},{2,4},{3,5},{4,6},{5,7},{6,0},{7,1},{8,14},{9,15},{10,... | collective-permute-start | bytes 2752520 | tf_op jit(solution)/shard_map/ppermute | solution.py:82
  188.6 18.1 %collective-permute-start.32 = (bf16[1792,256]{1,0:T(8,128)(2,1)S(1)}, bf16[1792,256]{1,0:T(8,128)(2,1)S(1)}, u32[]{:S(2)}, u32[]{:S(2)}) collective-permute-start(bf16[1792,256]{1,0:T(8,128)(2,1)S(1)} %add_convert_fusion.2), channel_id=1, source_target_pairs={{0,2},{1,3},{2,4},{3,5},{4,6},{5,7},{6,0},{7,1},{8,14},{9,15},{10,... | collective-permute-start | bytes 2752520 | tf_op jit(solution)/shard_map/ppermute | solution.py:82
  190.9 15.8 %copy-start.2 = (f32[1792,128]{1,0:T(8,128)S(1)}, f32[1792,128]{1,0:T(8,128)}, u32[]{:S(2)}) copy-start(f32[1792,128]{1,0:T(8,128)} %pad_maximum_fusion.5.refs_3_.refs_6_) | copy-start | bytes 2752516
  190.9 15.8 %copy-start.5 = (f32[1792,128]{1,0:T(8,128)S(1)}, f32[1792,128]{1,0:T(8,128)}, u32[]{:S(2)}) copy-start(f32[1792,128]{1,0:T(8,128)} %pad_maximum_fusion.6.refs_4_.refs_7_) | copy-start | bytes 2752516
  190.9 15.8 %copy-start.7 = (f32[1792,256]{1,0:T(8,128)S(1)}, f32[1792,256]{1,0:T(8,128)}, u32[]{:S(2)}) copy-start(f32[1792,256]{1,0:T(8,128)} %copy-done.6) | copy-start | bytes 5505028
  190.9 15.8 %copy-start.19 = (f32[2,128]{1,0:T(2,128)S(1)}, f32[2,128]{1,0:T(2,128)}, u32[]{:S(2)}) copy-start(f32[2,128]{1,0:T(2,128)} %param.16) | copy-start | bytes 3076
  213.0 21.7 %copy-start.16 = (bf16[1792,256]{1,0:T(8,128)(2,1)S(1)}, bf16[1792,256]{1,0:T(8,128)(2,1)}, u32[]{:S(2)}) copy-start(bf16[1792,256]{1,0:T(8,128)(2,1)} %copy-done.15) | copy-start | bytes 2752516
  213.0 58.6 %all-to-all-start.1 = ((bf16[16,256,512]{2,1,0:T(8,128)(2,1)}), bf16[16,256,512]{2,1,0:T(8,128)(2,1)}, u32[]{:S(2)}, u32[]{:S(2)}) async-start(bf16[16,256,512]{2,1,0:T(8,128)(2,1)} %get-tuple-element.135), calls=%async_computation.1 | async-start | bytes 8388608 | tf_op jit(solution)/shard_map/all_to_all | solution.py:566
  221.8 25.9 %copy-start.14 = (bf16[1792,256]{1,0:T(8,128)(2,1)S(1)}, bf16[1792,256]{1,0:T(8,128)(2,1)}, u32[]{:S(2)}) copy-start(bf16[1792,256]{1,0:T(8,128)(2,1)} %copy-done.13) | copy-start | bytes 2752516
  221.8 12.9 %collective-permute-start.29 = (bf16[1792,256]{1,0:T(8,128)(2,1)}, bf16[1792,256]{1,0:T(8,128)(2,1)S(1)}, u32[]{:S(2)}, u32[]{:S(2)}) collective-permute-start(bf16[1792,256]{1,0:T(8,128)(2,1)} %copy-done.20), channel_id=1, source_target_pairs={{0,2},{1,3},{2,4},{3,5},{4,6},{5,7},{6,0},{7,1},{8,14},{9,15},{10,... | collective-permute-start | bytes 2752520 | tf_op jit(solution)/shard_map/ppermute | solution.py:82
  234.8 26.0 %copy-start.10 = (f32[1792,256]{1,0:T(8,128)S(1)}, f32[1792,256]{1,0:T(8,128)}, u32[]{:S(2)}) copy-start(f32[1792,256]{1,0:T(8,128)} %copy-done.9) | copy-start | bytes 5505028
  235.0 12.7 %collective-permute-start.33 = (bf16[1792,256]{1,0:T(8,128)(2,1)S(1)}, bf16[1792,256]{1,0:T(8,128)(2,1)S(1)}, u32[]{:S(2)}, u32[]{:S(2)}) collective-permute-start(bf16[1792,256]{1,0:T(8,128)(2,1)S(1)} %add_convert_fusion.1), channel_id=1, source_target_pairs={{0,2},{1,3},{2,4},{3,5},{4,6},{5,7},{6,0},{7,1},{8,14},{9,15},{10,... | collective-permute-start | bytes 2752520 | tf_op jit(solution)/shard_map/ppermute | solution.py:82
  248.0 12.8 %collective-permute-start.34 = (bf16[1792,256]{1,0:T(8,128)(2,1)S(1)}, bf16[1792,256]{1,0:T(8,128)(2,1)S(1)}, u32[]{:S(2)}, u32[]{:S(2)}) collective-permute-start(bf16[1792,256]{1,0:T(8,128)(2,1)S(1)} %add_convert_fusion), channel_id=1, source_target_pairs={{0,2},{1,3},{2,4},{3,5},{4,6},{5,7},{6,0},{7,1},{8,14},{9,15},{10,... | collective-permute-start | bytes 2752520 | tf_op jit(solution)/shard_map/ppermute | solution.py:82
  271.6 31.8 %all-to-all-start = ((bf16[16,256,256]{2,1,0:T(8,128)(2,1)}), bf16[16,256,256]{2,1,0:T(8,128)(2,1)S(1)}, u32[]{:S(2)}, u32[]{:S(2)}) async-start(bf16[16,256,256]{2,1,0:T(8,128)(2,1)} %get-tuple-element.131), calls=%async_computation | async-start | bytes 4194304 | tf_op jit(solution)/shard_map/all_to_all | solution.py:566
  (22 other events, 101.6 us)

commit v4 on v3

--- a/solution.py
+++ b/solution.py
@@ -492,9 +492,9 @@
         plain, (*others, other_last), ((0, 2), (2, 4), (4, 5), (5, 7)), scale, gain_other
     )
 
-    held = lock((other, own, kv_theirs, q_pairs[1], *q_blocks), ())
-    other, own, kv_theirs, q_late = held[:4]
-    q_mine = jnp.stack(held[4:])
+    held = lock((other, own, kv_theirs, q_pairs[1], gathered, *q_blocks), ())
+    other, own, kv_theirs, q_late, gathered = held[:5]
+    q_mine = jnp.stack(held[5:])
     q_theirs = swap_dp(q_mine, 1)
     order = [0]
     for bits in (2, 1, 4, 8):

time: 316 us -> 314 us (level)
  waiting for transfers between devices: 94.3 us -> 104 us
  starting transfers between devices: 77 us -> 69.4 us
    ppermute x6, starting transfers between devices: 16.1 us -> 3.61 us  [shift_z(): lax.ppermute(value, 'dp', [(d, (d + 4 * step) % 16) for d in range(16)])]
    ppermute x9, waiting for transfers between devices: 38.5 us -> 49.2 us  [ring_x(): return lax.ppermute(value, ('dp', 'tensor'), pairs)]
    ppermute x6, waiting for transfers between devices: 6.02 us -> 14.1 us  [shift_z(): lax.ppermute(value, 'dp', [(d, (d + 4 * step) % 16) for d in range(16)])]
    ppermute x7, waiting for transfers between devices: 27.4 us -> 21.3 us  [swap_tensor(): return lax.ppermute(value, 'tensor', [(t, t ^ bits) for t in range(8)])]
    ppermute x8, starting transfers between devices: 10.8 us -> 16.4 us  [swap_dp(): return lax.ppermute(value, 'dp', [(d, d ^ bits) for d in range(16)])]
    unnamed x68 -> x60, local copies, waits for them, and re-layouts: 7.84 us -> 5.57 us
  transfers between devices with their start and end apart: 37 -> 37, of which waited for: 20 -> 18; matrix products, arithmetic and copies ran while one was open for 13% -> 12% of each run, Pallas kernels for 24% -> 24%
where the time goes in v4:
time: 314 us; the launch traced here: 313 us
  waiting for transfers between devices  104 us (33%)
  Pallas kernels  92.6 us (29%)
  starting transfers between devices  69.4 us (22%)
  other arithmetic  24.5 us (8%)
  local copies, waits for them, and re-layouts  21.1 us (7%)
    ppermute x9, waiting for transfers between devices, ring_x(): return lax.ppermute(value, ('dp', 'tensor'), pairs)  49.2 us
    pallas_call x5, Pallas kernels, parts_of(): pl.pallas_call(functools.partial(part_kernel, count), grid_spec=grid_spec...  41.4 us
    pallas_call x2, Pallas kernels, attend(): pl.pallas_call(body, grid_spec=grid_spec, out_shape=jax.ShapeDtypeStruct(...  24.1 us
    ppermute x7, waiting for transfers between devices, swap_tensor(): return lax.ppermute(value, 'tensor', [(t, t ^ bits) for t in range(8)])  21.3 us
    ppermute x8, starting transfers between devices, swap_dp(): return lax.ppermute(value, 'dp', [(d, d ^ bits) for d in range(16)])  16.4 us
    all_to_all x2, waiting for transfers between devices, local(): lax.all_to_all(slots, 'dp', split_axis=0, concat_axis=0, tiled=True)  15.3 us
    ppermute x6, waiting for transfers between devices, shift_z(): lax.ppermute(value, 'dp', [(d, (d + 4 * step) % 16) for d in range(16)])  14.1 us
    all_to_all x2, starting transfers between devices, local(): lax.all_to_all(slots, 'dp', split_axis=0, concat_axis=0, tiled=True)  12.3 us
  transfers between devices with their start and end apart: 37, of which 18 were waited for; matrix products, arithmetic and copies ran while one was open for 12% of the time, Pallas kernels for 24%

profile of v4, /device:TPU:1, one launch (start us, length us, event | category | flops | bytes accessed | tf_op | source)
XLA Modules:
  0.0 312.5 jit_solution(6791197737622386783)
XLA Ops:
  0.0 2.1 collective-permute-start.3
  2.1 2.3 slice.32
  4.4 2.6 collective-permute-start
  7.0 2.6 multiply_reduce_fusion
  10.8 1.9 multiply_reduce_fusion.1
  14.0 5.4 %collective-permute-start.1 = (bf16[512,512]{1,0:T(8,128)(2,1)}, bf16[512,512]{1,0:T(8,128)(2,1)}, u32[]{:S(2)}, u32[]{:S(2)}) collective-permute-start(bf16[512,512]{1,0:T(8,128)(2,1)} %param.13), channel_id=1, source_target_pairs={{0,0},{1,1},{2,34},{3,35},{4,68},{5,69},{6,102},{7,103},{8,8},{9,9... | collective-permute-start | bytes 1572872 | tf_op jit(solution)/shard_map/ppermute | solution.py:94
  19.4 7.6 %reshape.79 = bf16[4,2,2,512,256]{4,3,2,1,0:T(8,128)(2,1)} reshape(bf16[8192,2,128]{2,1,0:T(2,128)(2,1)} %param.14) | data formatting | bytes 8388608 | tf_op jit(solution)/shard_map/reshape | solution.py:444
  33.4 5.4 %collective-permute-start.6 = (bf16[512,512]{1,0:T(8,128)(2,1)}, bf16[512,512]{1,0:T(8,128)(2,1)}, u32[]{:S(2)}, u32[]{:S(2)}) collective-permute-start(bf16[512,512]{1,0:T(8,128)(2,1)} %collective-permute-done.1), channel_id=1, source_target_pairs={{0,0},{1,1},{2,2},{3,3},{4,4},{5,5},{6,6},{7,7},{8,8},{9,9},{10,10... | collective-permute-start | bytes 1572872 | tf_op jit(solution)/shard_map/ppermute | solution.py:102
  38.8 2.6 collective-permute-start.8
  41.3 3.4 %fusion.2 = (f32[1792,64]{1,0:T(8,128)S(1)}, f32[1792,64]{1,0:T(8,128)S(1)}, f32[1792,64]{1,0:T(8,128)S(1)}) fusion(f32[64]{0:T(128)S(1)} %multiply_power_fusion), kind=kLoop, calls=%fused_computation.24 | loop fusion | flops 229376 | bytes 1376512 | tf_op jit(solution)/shard_map/neg | solution.py:43
  46.0 1.9 collective-permute-start.7
  49.2 4.8 %collective-permute-done.7 = f32[7,256]{1,0:T(8,128)S(1)} collective-permute-done((f32[7,256]{1,0:T(8,128)S(1)}, f32[7,256]{1,0:T(8,128)S(1)}, u32[]{:S(2)}, u32[]{:S(2)}) %collective-permute-start.7) | collective-permute-done | bytes 7200 | tf_op jit(solution)/shard_map/ppermute | solution.py:55
  54.4 4.6 %collective-permute-done.5.refs_1_ = bf16[512,1024]{1,0:T(8,128)(2,1)S(1)} collective-permute-done((bf16[512,1024]{1,0:T(8,128)(2,1)S(1)}, bf16[512,1024]{1,0:T(8,128)(2,1)S(1)}, u32[]{:S(2)}, u32[]{:S(2)}) %collective-permute-start.5) | collective-permute-done | bytes 1048608 | tf_op jit(solution)/shard_map/ppermute | solution.py:55
  60.5 3.4 %collective-permute-start.13 = (bf16[1024,256]{1,0:T(8,128)(2,1)}, bf16[1024,256]{1,0:T(8,128)(2,1)S(1)}, u32[]{:S(2)}, u32[]{:S(2)}) collective-permute-start(bf16[1024,256]{1,0:T(8,128)(2,1)} %pad_maximum_fusion.9), channel_id=1, source_target_pairs={{0,4},{1,5},{2,6},{3,7},{4,0},{5,1},{6,2},{7,3},{8,12},{9,13},{10,... | collective-permute-start | bytes 1572872 | tf_op jit(solution)/shard_map/ppermute | solution.py:51
  63.9 2.2 collective-permute-start.10
  67.2 3.9 %collective-permute-done.12 = f32[7,256]{1,0:T(8,128)S(1)} collective-permute-done((f32[7,256]{1,0:T(8,128)S(1)}, f32[7,256]{1,0:T(8,128)S(1)}, u32[]{:S(2)}, u32[]{:S(2)}) %collective-permute-start.12) | collective-permute-done | bytes 7200 | tf_op jit(solution)/shard_map/ppermute | solution.py:55
  74.9 7.4 %collective-permute-done.10.refs_2_ = bf16[256,1024]{1,0:T(8,128)(2,1)S(1)} collective-permute-done((bf16[256,1024]{1,0:T(8,128)(2,1)S(1)}, bf16[256,1024]{1,0:T(8,128)(2,1)S(1)}, u32[]{:S(2)}, u32[]{:S(2)}) %collective-permute-start.10) | collective-permute-done | bytes 524320 | tf_op jit(solution)/shard_map/ppermute | solution.py:55
  84.8 2.7 collective-permute-start.15
  87.5 2.4 collective-permute-start.14
  90.0 3.1 collective-permute-start.16
  94.5 5.8 %collective-permute-start.17 = (s32[8,6]{1,0:T(8,128)S(1)}, s32[8,6]{1,0:T(8,128)S(1)}, u32[]{:S(2)}, u32[]{:S(2)}) collective-permute-start(s32[8,6]{1,0:T(8,128)S(1)} %pad_add_fusion), channel_id=1, source_target_pairs={{0,64},{8,72},{16,80},{24,88},{32,96},{40,104},{48,112},{56,120},{... | collective-permute-start | bytes 584 | tf_op jit(solution)/shard_map/ppermute | solution.py:59
  100.3 2.2 fusion.5
  107.6 5.8 %norm_rows.3.own = bf16[1792,1024]{1,0:T(8,128)(2,1)} custom-call(s32[2]{0:T(128)S(1)} %pad_add_fusion.6.picks, bf16[1536,1024]{1,0:T(8,128)(2,1)S(1)} %copy-done, bf16[1792,1024]{1,0:T(8,128)(2,1)} %refs_1_.1, f32[1792,1]{1,0:T(8,128)S(1)} %bitcast.53, f32[1,1024]{1,0:T(1,128)S(1)} %get-tuple-element.159.refs_3_), custom_call_target="tpu_custom_call" | custom-call | tf_op jit(solution)/shard_map/norm_rows/pallas_call | solution.py:155
  114.1 6.5 %norm_rows.2.other = bf16[1792,1024]{1,0:T(8,128)(2,1)} custom-call(s32[2]{0:T(128)S(1)} %pad_add_fusion.5.picks, bf16[512,1024]{1,0:T(8,128)(2,1)} %collective-permute-done.refs_0_, bf16[512,1024]{1,0:T(8,128)(2,1)S(1)} %copy-done.10, bf16[256,1024]{1,0:T(8,128)(2,1)S(1)} %copy-done.13, bf16[512,1024]{1,0:T(8,128)(2,1)} %collective-permute-done.14.refs_3_, ...), custom_call_target="tpu_custom_call" | custom-call | tf_op jit(solution)/shard_map/norm_rows/pallas_call | solution.py:155
  120.6 8.8 %collective-permute-done.18 = bf16[1024,256]{1,0:T(8,128)(2,1)} collective-permute-done((bf16[1024,256]{1,0:T(8,128)(2,1)}, bf16[1024,256]{1,0:T(8,128)(2,1)}, u32[]{:S(2)}, u32[]{:S(2)}) %collective-permute-start.18) | collective-permute-done | bytes 524320 | tf_op jit(solution)/shard_map/ppermute | solution.py:86
  129.4 1.8 pad_maximum_fusion.1.rest_0_.rest_2_.rest_4_
  131.9 5.4 %part_rows.5.rest_2_ = bf16[1792,256]{1,0:T(8,128)(2,1)S(1)} custom-call(s32[1]{0:T(128)} %bitcast.29.at, bf16[1792,1024]{1,0:T(8,128)(2,1)} %norm_rows.3.own, bf16[1792,1024]{1,0:T(8,128)(2,1)} %norm_rows.2.other, bf16[4,1024,256]{2,1,0:T(8,128)(2,1)} %pad_maximum_fusion.rest_0_.rest_2_.rest_4_, ...), custom_call_target="tpu_custom_call" | custom-call | flops 1879048192 | bytes 7340032 | tf_op jit(solution)/shard_map/part_rows/pallas_call | solution.py:200
  137.3 1.9 collective-permute-start.25
  139.2 5.3 %part_rows.6.rest_6_ = bf16[1792,256]{1,0:T(8,128)(2,1)S(1)} custom-call(s32[1]{0:T(128)} %bitcast.21.at, bf16[1792,1024]{1,0:T(8,128)(2,1)} %norm_rows.3.own, bf16[1792,1024]{1,0:T(8,128)(2,1)} %norm_rows.2.other, bf16[4,1024,256]{2,1,0:T(8,128)(2,1)S(1)} %pad_maximum_fusion.1.rest_0_.rest_2_.rest_4_, ...), custom_call_target="tpu_custom_call" | custom-call | flops 1879048192 | bytes 7340032 | tf_op jit(solution)/shard_map/part_rows/pallas_call | solution.py:200
  146.9 9.5 %part_rows.7 = (bf16[1792,256]{1,0:T(8,128)(2,1)S(1)}, bf16[1792,256]{1,0:T(8,128)(2,1)S(1)}, f32[1792,256]{1,0:T(8,128)S(1)}) custom-call(s32[3]{0:T(128)S(1)} %get-tuple-element.169.at, bf16[1792,1024]{1,0:T(8,128)(2,1)} %norm_rows.3.own, bf16[1792,1024]{1,0:T(8,128)(2,1)} %norm_rows.2.other, ...), custom_call_target="tpu_custom_call" | custom-call | flops 5637144576 | bytes 7340032 | tf_op jit(solution)/shard_map/part_rows/pallas_call | solution.py:200
  157.3 9.5 %part_rows.8 = (bf16[1792,256]{1,0:T(8,128)(2,1)S(1)}, bf16[1792,256]{1,0:T(8,128)(2,1)S(1)}, f32[1792,256]{1,0:T(8,128)S(1)}) custom-call(s32[3]{0:T(128)S(1)} %get-tuple-element.168.at, bf16[1792,1024]{1,0:T(8,128)(2,1)} %norm_rows.3.own, bf16[1792,1024]{1,0:T(8,128)(2,1)} %norm_rows.2.other, bf16[4,1024,256]{2,1,0:T(8,128)(2,1)} %copy-done.1, ...), custom_call_target="tpu_custom_call" | custom-call | flops 5637144576 | bytes 7340032 | tf_op jit(solution)/shard_map/part_rows/pallas_call | solution.py:200
  166.8 5.2 %collective-permute-done.22 = bf16[1024,256]{1,0:T(8,128)(2,1)S(1)} collective-permute-done((bf16[1024,256]{1,0:T(8,128)(2,1)S(1)}, bf16[1024,256]{1,0:T(8,128)(2,1)S(1)}, u32[]{:S(2)}, u32[]{:S(2)}) %collective-permute-start.22) | collective-permute-done | bytes 524320 | tf_op jit(solution)/shard_map/ppermute | solution.py:86
  175.2 10.6 %collective-permute-done.31 = bf16[1792,256]{1,0:T(8,128)(2,1)S(1)} collective-permute-done((bf16[1792,256]{1,0:T(8,128)(2,1)S(1)}, bf16[1792,256]{1,0:T(8,128)(2,1)S(1)}, u32[]{:S(2)}, u32[]{:S(2)}) %collective-permute-start.31) | collective-permute-done | bytes 917536 | tf_op jit(solution)/shard_map/ppermute | solution.py:82
  188.4 11.8 %part_rows.9 = (bf16[1792,256]{1,0:T(8,128)(2,1)S(1)}, bf16[1792,256]{1,0:T(8,128)(2,1)S(1)}, bf16[1792,256]{1,0:T(8,128)(2,1)S(1)}, f32[1792,256]{1,0:T(8,128)S(1)}) custom-call(s32[4]{0:T(128)S(1)} %pad_add_fusion.8.at, bf16[1792,1024]{1,0:T(8,128)(2,1)} %norm_rows.3.own, bf16[1792,1024]{1,0:T(8,128)(2,1)} %norm_rows.2.other, ...), custom_call_target="tpu_custom_call" | custom-call | flops 7516192768 | bytes 7340032 | tf_op jit(solution)/shard_map/part_rows/pallas_call | solution.py:200
  201.5 4.0 %collective-permute-done.32.refs_3_ = bf16[1792,256]{1,0:T(8,128)(2,1)S(1)} collective-permute-done((bf16[1792,256]{1,0:T(8,128)(2,1)S(1)}, bf16[1792,256]{1,0:T(8,128)(2,1)S(1)}, u32[]{:S(2)}, u32[]{:S(2)}) %collective-permute-start.32) | collective-permute-done | bytes 917536 | tf_op jit(solution)/shard_map/ppermute | solution.py:82
  205.4 6.3 %finish_rows.3 = (bf16[16,256,512]{2,1,0:T(8,128)(2,1)}, bf16[256,512]{1,0:T(8,128)(2,1)S(1)}) custom-call(s32[7]{0:T(128)S(1)} %get-tuple-element.166.dest, s32[7]{0:T(128)S(1)} %get-tuple-element.167.spots, f32[1792,256]{1,0:T(8,128)S(1)} %get-tuple-element.135.refs_0_, f32[1792,256]{1,0:T(8,128)} %copy-done.6, ...), custom_call_target="tpu_custom_call" | custom-call | flops 7340032 | bytes 9175040 | tf_op jit(solution)/shard_map/finish_rows/pallas_call | solution.py:261
  211.8 6.4 %all-to-all-start.1 = ((bf16[16,256,512]{2,1,0:T(8,128)(2,1)}), bf16[16,256,512]{2,1,0:T(8,128)(2,1)}, u32[]{:S(2)}, u32[]{:S(2)}) async-start(bf16[16,256,512]{2,1,0:T(8,128)(2,1)} %get-tuple-element.137), calls=%async_computation.1 | async-start | bytes 8388608 | tf_op jit(solution)/shard_map/all_to_all | solution.py:566
  218.2 12.8 %collective-permute-done.29 = bf16[1792,256]{1,0:T(8,128)(2,1)S(1)} collective-permute-done((bf16[1792,256]{1,0:T(8,128)(2,1)}, bf16[1792,256]{1,0:T(8,128)(2,1)S(1)}, u32[]{:S(2)}, u32[]{:S(2)}) %collective-permute-start.29) | collective-permute-done | bytes 917536 | tf_op jit(solution)/shard_map/ppermute | solution.py:82
  233.9 11.4 %collective-permute-done.33 = bf16[1792,256]{1,0:T(8,128)(2,1)S(1)} collective-permute-done((bf16[1792,256]{1,0:T(8,128)(2,1)S(1)}, bf16[1792,256]{1,0:T(8,128)(2,1)S(1)}, u32[]{:S(2)}, u32[]{:S(2)}) %collective-permute-start.33) | collective-permute-done | bytes 917536 | tf_op jit(solution)/shard_map/ppermute | solution.py:82
  245.5 2.5 collective-permute-start.34
  248.0 10.3 %collective-permute-done.34.refs_1_ = bf16[1792,256]{1,0:T(8,128)(2,1)S(1)} collective-permute-done((bf16[1792,256]{1,0:T(8,128)(2,1)S(1)}, bf16[1792,256]{1,0:T(8,128)(2,1)S(1)}, u32[]{:S(2)}, u32[]{:S(2)}) %collective-permute-start.34) | collective-permute-done | bytes 917536 | tf_op jit(solution)/shard_map/ppermute | solution.py:82
  258.4 3.8 %finish_rows.2 = (bf16[16,256,256]{2,1,0:T(8,128)(2,1)}, bf16[256,256]{1,0:T(8,128)(2,1)S(1)}) custom-call(s32[7]{0:T(128)S(1)} %get-tuple-element.166.dest, s32[7]{0:T(128)S(1)} %get-tuple-element.167.spots, f32[1792,256]{1,0:T(8,128)S(1)} %copy-done.8, bf16[1792,256]{1,0:T(8,128)(2,1)S(1)} %collective-permute-done.34.refs_1_, f32[1,256]{1,0:T(1,128)S(1)} %bitcast.56, ...), custom_call_target="tpu_custom_call" | custom-call | flops 3670016 | bytes 4587520 | tf_op jit(solution)/shard_map/finish_rows/pallas_call | solution.py:261
  262.2 5.8 %all-to-all-done.1.slots.refs_3_ = bf16[16,256,512]{2,1,0:T(8,128)(2,1)} async-done(((bf16[16,256,512]{2,1,0:T(8,128)(2,1)}), bf16[16,256,512]{2,1,0:T(8,128)(2,1)}, u32[]{:S(2)}, u32[]{:S(2)}) %all-to-all-start.1) | async-done | bytes 4194336 | tf_op jit(solution)/shard_map/all_to_all | solution.py:566
  267.9 5.9 %all-to-all-start = ((bf16[16,256,256]{2,1,0:T(8,128)(2,1)}), bf16[16,256,256]{2,1,0:T(8,128)(2,1)S(1)}, u32[]{:S(2)}, u32[]{:S(2)}) async-start(bf16[16,256,256]{2,1,0:T(8,128)(2,1)} %get-tuple-element.133), calls=%async_computation | async-start | bytes 4194304 | tf_op jit(solution)/shard_map/all_to_all | solution.py:566
  274.3 4.6 %gather_pair.1 = (bf16[1792,128]{1,0:T(8,128)(2,1)S(1)}, bf16[144,1792]{1,0:T(8,128)(2,1)S(1)}) custom-call(s32[7]{0:T(128)S(1)} %select_reduce_fusion.1.source.refs_0_, s32[1]{0:T(128)} %bitcast.1.text_at.refs_1_, bf16[16,256,512]{2,1,0:T(8,128)(2,1)} %all-to-all-done.1.slots.refs_3_, bf16[256,512]{1,0:T(8,128)(2,1)S(1)} %get-tuple-element.138.text.refs_4_), custom_call_target="tpu_custom_call" | custom-call | flops 458752 | bytes 1835008 | tf_op jit(solution)/shard_map/gather_pair/pallas_call | solution.py:304
  278.9 12.6 %attend.2.refs_7_ = bf16[1792,512]{1,0:T(8,128)(2,1)} custom-call(s32[7]{0:T(128)S(1)} %select_reduce_fusion.1.source.refs_0_, s32[1]{0:T(128)} %bitcast.1.text_at.refs_1_, s32[4]{0:T(128)S(1)} %bitcast.58, bf16[16,256,512]{2,1,0:T(8,128)(2,1)} %all-to-all-done.1.slots.refs_3_, bf16[256,512]{1,0:T(8,128)(2,1)S(1)} %get-tuple-element.138.text.refs_4_, ...), custom_call_target="tpu_custom_call" | custom-call | flops 3288334336 | bytes 2752512 | tf_op jit(solution)/shard_map/attend/pallas_call | solution.py:391
  291.5 9.5 %all-to-all-done.refs_3_ = bf16[16,256,256]{2,1,0:T(8,128)(2,1)S(1)} async-done(((bf16[16,256,256]{2,1,0:T(8,128)(2,1)}), bf16[16,256,256]{2,1,0:T(8,128)(2,1)S(1)}, u32[]{:S(2)}, u32[]{:S(2)}) %all-to-all-start) | async-done | bytes 2097184 | tf_op jit(solution)/shard_map/all_to_all | solution.py:566
  301.0 11.5 %attend.3 = bf16[1792,512]{1,0:T(8,128)(2,1)} custom-call(s32[7]{0:T(128)S(1)} %select_reduce_fusion.1.source.refs_0_, s32[1]{0:T(128)} %bitcast.1.text_at.refs_1_, s32[4]{0:T(128)S(1)} %bitcast.59, bf16[16,256,256]{2,1,0:T(8,128)(2,1)S(1)} %all-to-all-done.refs_3_, bf16[256,256]{1,0:T(8,128)(2,1)S(1)} %get-tuple-element.134.refs_4_, ...), custom_call_target="tpu_custom_call", output_to_operand_aliasing={{}: (7, {})} | custom-call | flops 3288334336 | bytes 2752512 | tf_op jit(solution)/shard_map/attend/pallas_call | solution.py:391
  (154 shorter events, 41.8 us)
Async XLA Ops:
  0.0 30.4 %collective-permute-start.3 = (s32[1,6]{1,0:T(1,128)}, s32[1,6]{1,0:T(1,128)S(1)}, u32[]{:S(2)}, u32[]{:S(2)}) collective-permute-start(s32[1,6]{1,0:T(1,128)} %param.19), channel_id=1, source_target_pairs={{0,16},{8,24},{16,0},{24,8},{32,48},{40,56},{48,32},{56,40},{64,80... | collective-permute-start | bytes 80 | tf_op jit(solution)/shard_map/ppermute | solution.py:59
  4.4 28.5 %collective-permute-start = (bf16[512,1024]{1,0:T(8,128)(2,1)}, bf16[512,1024]{1,0:T(8,128)(2,1)}, u32[]{:S(2)}, u32[]{:S(2)}) collective-permute-start(bf16[512,1024]{1,0:T(8,128)(2,1)} %slice.32), channel_id=1, source_target_pairs={{0,1},{1,0},{2,3},{3,2},{4,5},{5,4},{6,7},{7,6},{8,9},{9,8},{10,11... | collective-permute-start | bytes 3145736 | tf_op jit(solution)/shard_map/ppermute | solution.py:55
  12.7 20.1 %collective-permute-start.2 = (f32[7,256]{1,0:T(8,128)S(1)}, f32[7,256]{1,0:T(8,128)S(1)}, u32[]{:S(2)}, u32[]{:S(2)}) collective-permute-start(f32[7,256]{1,0:T(8,128)S(1)} %reshape.78), channel_id=1, source_target_pairs={{0,2},{1,3},{2,0},{3,1},{4,6},{5,7},{6,4},{7,5},{8,10},{9,11},{10,... | collective-permute-start | bytes 21512 | tf_op jit(solution)/shard_map/ppermute | solution.py:55
  14.0 18.8 %collective-permute-start.1 = (bf16[512,512]{1,0:T(8,128)(2,1)}, bf16[512,512]{1,0:T(8,128)(2,1)}, u32[]{:S(2)}, u32[]{:S(2)}) collective-permute-start(bf16[512,512]{1,0:T(8,128)(2,1)} %param.13), channel_id=1, source_target_pairs={{0,0},{1,1},{2,34},{3,35},{4,68},{5,69},{6,102},{7,103},{8,8},{9,9... | collective-permute-start | bytes 1572872 | tf_op jit(solution)/shard_map/ppermute | solution.py:94
  30.4 2.4 collective-permute-start.4
  33.0 26.0 %collective-permute-start.5 = (bf16[512,1024]{1,0:T(8,128)(2,1)S(1)}, bf16[512,1024]{1,0:T(8,128)(2,1)S(1)}, u32[]{:S(2)}, u32[]{:S(2)}) collective-permute-start(bf16[512,1024]{1,0:T(8,128)(2,1)S(1)} %slice.33), channel_id=1, source_target_pairs={{0,1},{1,0},{2,3},{3,2},{4,5},{5,4},{6,7},{7,6},{8,9},{9,8},{10,11... | collective-permute-start | bytes 3145736 | tf_op jit(solution)/shard_map/ppermute | solution.py:55
  33.4 20.5 %collective-permute-start.6 = (bf16[512,512]{1,0:T(8,128)(2,1)}, bf16[512,512]{1,0:T(8,128)(2,1)}, u32[]{:S(2)}, u32[]{:S(2)}) collective-permute-start(bf16[512,512]{1,0:T(8,128)(2,1)} %collective-permute-done.1), channel_id=1, source_target_pairs={{0,0},{1,1},{2,2},{3,3},{4,4},{5,5},{6,6},{7,7},{8,8},{9,9},{10,10... | collective-permute-start | bytes 1572872 | tf_op jit(solution)/shard_map/ppermute | solution.py:102
  38.8 15.2 %collective-permute-start.8 = (bf16[1024,256]{1,0:T(8,128)(2,1)S(1)}, bf16[1024,256]{1,0:T(8,128)(2,1)S(1)}, u32[]{:S(2)}, u32[]{:S(2)}) collective-permute-start(bf16[1024,256]{1,0:T(8,128)(2,1)S(1)} %pad_maximum_fusion.10), channel_id=1, source_target_pairs={{0,6},{1,7},{2,0},{3,1},{4,2},{5,3},{6,4},{7,5},{8,14},{9,15},{10,... | collective-permute-start | bytes 1572872 | tf_op jit(solution)/shard_map/ppermute | solution.py:51
  41.3 13.1 %collective-permute-start.9 = (bf16[1024,256]{1,0:T(8,128)(2,1)S(1)}, bf16[1024,256]{1,0:T(8,128)(2,1)S(1)}, u32[]{:S(2)}, u32[]{:S(2)}) collective-permute-start(bf16[1024,256]{1,0:T(8,128)(2,1)S(1)} %pad_maximum_fusion.8), channel_id=1, source_target_pairs={{0,2},{1,3},{2,4},{3,5},{4,6},{5,7},{6,0},{7,1},{8,10},{9,11},{10,... | collective-permute-start | bytes 1572872 | tf_op jit(solution)/shard_map/ppermute | solution.py:51
  46.0 7.9 %collective-permute-start.7 = (f32[7,256]{1,0:T(8,128)S(1)}, f32[7,256]{1,0:T(8,128)S(1)}, u32[]{:S(2)}, u32[]{:S(2)}) collective-permute-start(f32[7,256]{1,0:T(8,128)S(1)} %add.194), channel_id=1, source_target_pairs={{0,4},{1,5},{2,6},{3,7},{4,0},{5,1},{6,2},{7,3},{8,12},{9,13},{10,... | collective-permute-start | bytes 21512 | tf_op jit(solution)/shard_map/ppermute | solution.py:55
  60.0 12.6 %collective-permute-start.11 = (bf16[512,512]{1,0:T(8,128)(2,1)}, bf16[512,512]{1,0:T(8,128)(2,1)}, u32[]{:S(2)}, u32[]{:S(2)}) collective-permute-start(bf16[512,512]{1,0:T(8,128)(2,1)} %collective-permute-done.6), channel_id=1, source_target_pairs={{0,16},{8,24},{16,0},{24,8},{32,48},{40,56},{48,32},{56,40},{64,80... | collective-permute-start | bytes 1572872 | tf_op jit(solution)/shard_map/ppermute | solution.py:59
  60.0 11.1 %collective-permute-start.12 = (f32[7,256]{1,0:T(8,128)S(1)}, f32[7,256]{1,0:T(8,128)S(1)}, u32[]{:S(2)}, u32[]{:S(2)}) collective-permute-start(f32[7,256]{1,0:T(8,128)S(1)} %add.210), channel_id=1, source_target_pairs={{0,1},{1,0},{2,3},{3,2},{4,5},{5,4},{6,7},{7,6},{8,9},{9,8},{10,11... | collective-permute-start | bytes 21512 | tf_op jit(solution)/shard_map/ppermute | solution.py:55
  60.5 14.4 %collective-permute-start.13 = (bf16[1024,256]{1,0:T(8,128)(2,1)}, bf16[1024,256]{1,0:T(8,128)(2,1)S(1)}, u32[]{:S(2)}, u32[]{:S(2)}) collective-permute-start(bf16[1024,256]{1,0:T(8,128)(2,1)} %pad_maximum_fusion.9), channel_id=1, source_target_pairs={{0,4},{1,5},{2,6},{3,7},{4,0},{5,1},{6,2},{7,3},{8,12},{9,13},{10,... | collective-permute-start | bytes 1572872 | tf_op jit(solution)/shard_map/ppermute | solution.py:51
  63.9 18.4 %collective-permute-start.10 = (bf16[256,1024]{1,0:T(8,128)(2,1)S(1)}, bf16[256,1024]{1,0:T(8,128)(2,1)S(1)}, u32[]{:S(2)}, u32[]{:S(2)}) collective-permute-start(bf16[256,1024]{1,0:T(8,128)(2,1)S(1)} %get-tuple-element.154), channel_id=1, source_target_pairs={{0,1},{1,0},{2,3},{3,2},{4,5},{5,4},{6,7},{7,6},{8,9},{9,8},{10,11... | collective-permute-start | bytes 1572872 | tf_op jit(solution)/shard_map/ppermute | solution.py:55
  71.1 12.1 %copy-start.18 = (bf16[1024,256]{1,0:T(8,128)(2,1)S(1)}, bf16[1024,256]{1,0:T(8,128)(2,1)}, u32[]{:S(2)}) copy-start(bf16[1024,256]{1,0:T(8,128)(2,1)} %pad_maximum_fusion.7) | copy-start | bytes 1572868
  71.1 12.1 %copy-start.21 = (bf16[1024,256]{1,0:T(8,128)(2,1)S(1)}, bf16[1024,256]{1,0:T(8,128)(2,1)}, u32[]{:S(2)}) copy-start(bf16[1024,256]{1,0:T(8,128)(2,1)} %copy-done.20) | copy-start | bytes 1572868
  71.1 12.1 %copy-start.23 = (bf16[1024,256]{1,0:T(8,128)(2,1)S(1)}, bf16[1024,256]{1,0:T(8,128)(2,1)}, u32[]{:S(2)}) copy-start(bf16[1024,256]{1,0:T(8,128)(2,1)} %copy-done.22) | copy-start | bytes 1572868
  84.8 44.6 %collective-permute-start.15 = (bf16[4,1024,256]{2,1,0:T(8,128)(2,1)}, bf16[4,1024,256]{2,1,0:T(8,128)(2,1)}, u32[]{:S(2)}, u32[]{:S(2)}) collective-permute-start(bf16[4,1024,256]{2,1,0:T(8,128)(2,1)} %pad_maximum_fusion.rest_0_.rest_2_.rest_4_), channel_id=1, source_target_pairs={{0,8},{8,0},{16,24},{24,16},{32,40},{40,32},{48,56},{56,48},{64,72... | collective-permute-start | bytes 6291464 | tf_op jit(solution)/shard_map/ppermute | solution.py:59
  87.5 26.6 %collective-permute-start.14 = (bf16[512,1024]{1,0:T(8,128)(2,1)}, bf16[512,1024]{1,0:T(8,128)(2,1)}, u32[]{:S(2)}, u32[]{:S(2)}) collective-permute-start(bf16[512,1024]{1,0:T(8,128)(2,1)} %pad_maximum_fusion.4), channel_id=1, source_target_pairs={{0,1},{1,0},{2,3},{3,2},{4,5},{5,4},{6,7},{7,6},{8,9},{9,8},{10,11... | collective-permute-start | bytes 3145736 | tf_op jit(solution)/shard_map/ppermute | solution.py:55
  90.0 4.5 %collective-permute-start.16 = (s32[4,6]{1,0:T(4,128)S(1)}, s32[4,6]{1,0:T(4,128)S(1)}, u32[]{:S(2)}, u32[]{:S(2)}) collective-permute-start(s32[4,6]{1,0:T(4,128)S(1)} %pad_add_fusion.2), channel_id=1, source_target_pairs={{0,32},{8,40},{16,48},{24,56},{32,0},{40,8},{48,16},{56,24},{64,96... | collective-permute-start | bytes 296 | tf_op jit(solution)/shard_map/ppermute | solution.py:59
  94.5 9.3 %collective-permute-start.17 = (s32[8,6]{1,0:T(8,128)S(1)}, s32[8,6]{1,0:T(8,128)S(1)}, u32[]{:S(2)}, u32[]{:S(2)}) collective-permute-start(s32[8,6]{1,0:T(8,128)S(1)} %pad_add_fusion), channel_id=1, source_target_pairs={{0,64},{8,72},{16,80},{24,88},{32,96},{40,104},{48,112},{56,120},{... | collective-permute-start | bytes 584 | tf_op jit(solution)/shard_map/ppermute | solution.py:59
  102.5 18.0 %collective-permute-start.20 = (bf16[1024,256]{1,0:T(8,128)(2,1)}, bf16[1024,256]{1,0:T(8,128)(2,1)}, u32[]{:S(2)}, u32[]{:S(2)}) collective-permute-start(bf16[1024,256]{1,0:T(8,128)(2,1)} %get-tuple-element.99), channel_id=1, source_target_pairs={{0,96},{8,104},{16,112},{24,120},{32,0},{40,8},{48,16},{56,24},{64... | collective-permute-start | bytes 1572872 | tf_op jit(solution)/shard_map/ppermute | solution.py:86
  102.5 18.0 %collective-permute-start.19 = (bf16[1024,256]{1,0:T(8,128)(2,1)}, bf16[1024,256]{1,0:T(8,128)(2,1)}, u32[]{:S(2)}, u32[]{:S(2)}) collective-permute-start(bf16[1024,256]{1,0:T(8,128)(2,1)} %get-tuple-element.99), channel_id=1, source_target_pairs={{0,64},{8,72},{16,80},{24,88},{32,96},{40,104},{48,112},{56,120},{... | collective-permute-start | bytes 1572872 | tf_op jit(solution)/shard_map/ppermute | solution.py:86
  103.7 25.7 %collective-permute-start.18 = (bf16[1024,256]{1,0:T(8,128)(2,1)}, bf16[1024,256]{1,0:T(8,128)(2,1)}, u32[]{:S(2)}, u32[]{:S(2)}) collective-permute-start(bf16[1024,256]{1,0:T(8,128)(2,1)} %get-tuple-element.99), channel_id=1, source_target_pairs={{0,32},{8,40},{16,48},{24,56},{32,64},{40,72},{48,80},{56,88},{64,... | collective-permute-start | bytes 1572872 | tf_op jit(solution)/shard_map/ppermute | solution.py:86
  131.2 8.0 %copy-start.1 = (bf16[4,1024,256]{2,1,0:T(8,128)(2,1)}, bf16[4,1024,256]{2,1,0:T(8,128)(2,1)S(1)}, u32[]{:S(2)}) copy-start(bf16[4,1024,256]{2,1,0:T(8,128)(2,1)S(1)} %pad_maximum_fusion.1.rest_0_.rest_2_.rest_4_) | copy-start | bytes 6291460
  131.2 8.0 %collective-permute-start.21 = (bf16[4,1024,256]{2,1,0:T(8,128)(2,1)S(1)}, bf16[4,1024,256]{2,1,0:T(8,128)(2,1)}, u32[]{:S(2)}, u32[]{:S(2)}) collective-permute-start(bf16[4,1024,256]{2,1,0:T(8,128)(2,1)S(1)} %pad_maximum_fusion.1.rest_0_.rest_2_.rest_4_), channel_id=1, source_target_pairs={{0,8},{8,0},{16,24},{24,16},{32,40},{40,32},{48,56},{56,48},{64,72... | collective-permute-start | bytes 6291464 | tf_op jit(solution)/shard_map/ppermute | solution.py:59
  131.9 7.3 %copy-start.28 = (s32[16]{0:T(128)S(1)}, s32[16]{0:T(128)}, u32[]{:S(2)}) copy-start(s32[16]{0:T(128)} %constant.481.clone) | copy-start | bytes 196
  137.3 19.2 %collective-permute-start.25 = (bf16[1792,256]{1,0:T(8,128)(2,1)S(1)}, bf16[1792,256]{1,0:T(8,128)(2,1)S(1)}, u32[]{:S(2)}, u32[]{:S(2)}) collective-permute-start(bf16[1792,256]{1,0:T(8,128)(2,1)S(1)} %part_rows.5.rest_2_), channel_id=1, source_target_pairs={{0,2},{1,3},{2,4},{3,5},{4,6},{5,7},{6,0},{7,1},{8,14},{9,15},{10,... | collective-permute-start | bytes 2752520 | tf_op jit(solution)/shard_map/ppermute | solution.py:82
  144.5 22.3 %collective-permute-start.24 = (bf16[1024,256]{1,0:T(8,128)(2,1)S(1)}, bf16[1024,256]{1,0:T(8,128)(2,1)S(1)}, u32[]{:S(2)}, u32[]{:S(2)}) collective-permute-start(bf16[1024,256]{1,0:T(8,128)(2,1)S(1)} %copy-done.19), channel_id=1, source_target_pairs={{0,96},{8,104},{16,112},{24,120},{32,0},{40,8},{48,16},{56,24},{64... | collective-permute-start | bytes 1572872 | tf_op jit(solution)/shard_map/ppermute | solution.py:86
  145.4 21.4 %collective-permute-start.23 = (bf16[1024,256]{1,0:T(8,128)(2,1)S(1)}, bf16[1024,256]{1,0:T(8,128)(2,1)S(1)}, u32[]{:S(2)}, u32[]{:S(2)}) collective-permute-start(bf16[1024,256]{1,0:T(8,128)(2,1)S(1)} %copy-done.19), channel_id=1, source_target_pairs={{0,64},{8,72},{16,80},{24,88},{32,96},{40,104},{48,112},{56,120},{... | collective-permute-start | bytes 1572872 | tf_op jit(solution)/shard_map/ppermute | solution.py:86
  146.0 26.0 %collective-permute-start.22 = (bf16[1024,256]{1,0:T(8,128)(2,1)S(1)}, bf16[1024,256]{1,0:T(8,128)(2,1)S(1)}, u32[]{:S(2)}, u32[]{:S(2)}) collective-permute-start(bf16[1024,256]{1,0:T(8,128)(2,1)S(1)} %copy-done.19), channel_id=1, source_target_pairs={{0,32},{8,40},{16,48},{24,56},{32,64},{40,72},{48,80},{56,88},{64,... | collective-permute-start | bytes 1572872 | tf_op jit(solution)/shard_map/ppermute | solution.py:86
  146.6 26.2 %collective-permute-start.30 = (bf16[1792,256]{1,0:T(8,128)(2,1)S(1)}, bf16[1792,256]{1,0:T(8,128)(2,1)S(1)}, u32[]{:S(2)}, u32[]{:S(2)}) collective-permute-start(bf16[1792,256]{1,0:T(8,128)(2,1)S(1)} %part_rows.6.rest_6_), channel_id=1, source_target_pairs={{0,2},{1,3},{2,4},{3,5},{4,6},{5,7},{6,0},{7,1},{8,14},{9,15},{10,... | collective-permute-start | bytes 2752520 | tf_op jit(solution)/shard_map/ppermute | solution.py:82
  156.7 17.6 %collective-permute-start.27 = (bf16[1792,256]{1,0:T(8,128)(2,1)S(1)}, bf16[1792,256]{1,0:T(8,128)(2,1)S(1)}, u32[]{:S(2)}, u32[]{:S(2)}) collective-permute-start(bf16[1792,256]{1,0:T(8,128)(2,1)S(1)} %add_convert_fusion.5.rest_6_), channel_id=1, source_target_pairs={{0,2},{1,3},{2,4},{3,5},{4,6},{5,7},{6,0},{7,1},{8,14},{9,15},{10,... | collective-permute-start | bytes 2752520 | tf_op jit(solution)/shard_map/ppermute | solution.py:82
  172.3 16.1 %collective-permute-start.26 = (bf16[4,1024,256]{2,1,0:T(8,128)(2,1)S(1)}, bf16[4,1024,256]{2,1,0:T(8,128)(2,1)}, u32[]{:S(2)}, u32[]{:S(2)}) collective-permute-start(bf16[4,1024,256]{2,1,0:T(8,128)(2,1)S(1)} %pad_maximum_fusion.2.rest_0_.rest_2_.rest_4_.rest_6_), channel_id=1, source_target_pairs={{0,8},{8,0},{16,24},{24,16},{32,40},{40,32},{48,56},{56,48},{64,72... | collective-permute-start | bytes 6291464 | tf_op jit(solution)/shard_map/ppermute | solution.py:59
  173.1 12.6 %collective-permute-start.31 = (bf16[1792,256]{1,0:T(8,128)(2,1)S(1)}, bf16[1792,256]{1,0:T(8,128)(2,1)S(1)}, u32[]{:S(2)}, u32[]{:S(2)}) collective-permute-start(bf16[1792,256]{1,0:T(8,128)(2,1)S(1)} %add_convert_fusion.3), channel_id=1, source_target_pairs={{0,2},{1,3},{2,4},{3,5},{4,6},{5,7},{6,0},{7,1},{8,14},{9,15},{10,... | collective-permute-start | bytes 2752520 | tf_op jit(solution)/shard_map/ppermute | solution.py:82
  174.6 26.8 %collective-permute-start.28 = (bf16[1792,256]{1,0:T(8,128)(2,1)S(1)}, bf16[1792,256]{1,0:T(8,128)(2,1)S(1)}, u32[]{:S(2)}, u32[]{:S(2)}) collective-permute-start(bf16[1792,256]{1,0:T(8,128)(2,1)S(1)} %add_convert_fusion.4), channel_id=1, source_target_pairs={{0,2},{1,3},{2,4},{3,5},{4,6},{5,7},{6,0},{7,1},{8,14},{9,15},{10,... | collective-permute-start | bytes 2752520 | tf_op jit(solution)/shard_map/ppermute | solution.py:82
  186.0 19.4 %collective-permute-start.32 = (bf16[1792,256]{1,0:T(8,128)(2,1)S(1)}, bf16[1792,256]{1,0:T(8,128)(2,1)S(1)}, u32[]{:S(2)}, u32[]{:S(2)}) collective-permute-start(bf16[1792,256]{1,0:T(8,128)(2,1)S(1)} %add_convert_fusion.2), channel_id=1, source_target_pairs={{0,2},{1,3},{2,4},{3,5},{4,6},{5,7},{6,0},{7,1},{8,14},{9,15},{10,... | collective-permute-start | bytes 2752520 | tf_op jit(solution)/shard_map/ppermute | solution.py:82
  188.4 17.0 %copy-start.2 = (f32[1792,128]{1,0:T(8,128)S(1)}, f32[1792,128]{1,0:T(8,128)}, u32[]{:S(2)}) copy-start(f32[1792,128]{1,0:T(8,128)} %pad_maximum_fusion.5.refs_3_.refs_6_) | copy-start | bytes 2752516
  188.4 17.0 %copy-start.5 = (f32[1792,128]{1,0:T(8,128)S(1)}, f32[1792,128]{1,0:T(8,128)}, u32[]{:S(2)}) copy-start(f32[1792,128]{1,0:T(8,128)} %pad_maximum_fusion.6.refs_4_.refs_7_) | copy-start | bytes 2752516
  188.4 17.0 %copy-start.14 = (f32[2,128]{1,0:T(2,128)S(1)}, f32[2,128]{1,0:T(2,128)}, u32[]{:S(2)}) copy-start(f32[2,128]{1,0:T(2,128)} %param.16) | copy-start | bytes 3076
  201.4 10.3 %copy-start.11 = (bf16[1792,256]{1,0:T(8,128)(2,1)}, bf16[1792,256]{1,0:T(8,128)(2,1)S(1)}, u32[]{:S(2)}) copy-start(bf16[1792,256]{1,0:T(8,128)(2,1)S(1)} %get-tuple-element.127) | copy-start | bytes 2752516
  201.4 10.3 %copy-start.15 = (bf16[1792,256]{1,0:T(8,128)(2,1)}, bf16[1792,256]{1,0:T(8,128)(2,1)S(1)}, u32[]{:S(2)}) copy-start(bf16[1792,256]{1,0:T(8,128)(2,1)S(1)} %get-tuple-element.121) | copy-start | bytes 2752516
  211.8 56.2 %all-to-all-start.1 = ((bf16[16,256,512]{2,1,0:T(8,128)(2,1)}), bf16[16,256,512]{2,1,0:T(8,128)(2,1)}, u32[]{:S(2)}, u32[]{:S(2)}) async-start(bf16[16,256,512]{2,1,0:T(8,128)(2,1)} %get-tuple-element.137), calls=%async_computation.1 | async-start | bytes 8388608 | tf_op jit(solution)/shard_map/all_to_all | solution.py:566
  218.2 12.9 %collective-permute-start.29 = (bf16[1792,256]{1,0:T(8,128)(2,1)}, bf16[1792,256]{1,0:T(8,128)(2,1)S(1)}, u32[]{:S(2)}, u32[]{:S(2)}) collective-permute-start(bf16[1792,256]{1,0:T(8,128)(2,1)} %copy-done.15), channel_id=1, source_target_pairs={{0,2},{1,3},{2,4},{3,5},{4,6},{5,7},{6,0},{7,1},{8,14},{9,15},{10,... | collective-permute-start | bytes 2752520 | tf_op jit(solution)/shard_map/ppermute | solution.py:82
  231.0 27.4 %copy-start.8 = (f32[1792,256]{1,0:T(8,128)S(1)}, f32[1792,256]{1,0:T(8,128)}, u32[]{:S(2)}) copy-start(f32[1792,256]{1,0:T(8,128)} %copy-done.7) | copy-start | bytes 5505028
  232.6 12.7 %collective-permute-start.33 = (bf16[1792,256]{1,0:T(8,128)(2,1)S(1)}, bf16[1792,256]{1,0:T(8,128)(2,1)S(1)}, u32[]{:S(2)}, u32[]{:S(2)}) collective-permute-start(bf16[1792,256]{1,0:T(8,128)(2,1)S(1)} %add_convert_fusion.1), channel_id=1, source_target_pairs={{0,2},{1,3},{2,4},{3,5},{4,6},{5,7},{6,0},{7,1},{8,14},{9,15},{10,... | collective-permute-start | bytes 2752520 | tf_op jit(solution)/shard_map/ppermute | solution.py:82
  245.5 12.8 %collective-permute-start.34 = (bf16[1792,256]{1,0:T(8,128)(2,1)S(1)}, bf16[1792,256]{1,0:T(8,128)(2,1)S(1)}, u32[]{:S(2)}, u32[]{:S(2)}) collective-permute-start(bf16[1792,256]{1,0:T(8,128)(2,1)S(1)} %add_convert_fusion), channel_id=1, source_target_pairs={{0,2},{1,3},{2,4},{3,5},{4,6},{5,7},{6,0},{7,1},{8,14},{9,15},{10,... | collective-permute-start | bytes 2752520 | tf_op jit(solution)/shard_map/ppermute | solution.py:82
  267.9 33.1 %all-to-all-start = ((bf16[16,256,256]{2,1,0:T(8,128)(2,1)}), bf16[16,256,256]{2,1,0:T(8,128)(2,1)S(1)}, u32[]{:S(2)}, u32[]{:S(2)}) async-start(bf16[16,256,256]{2,1,0:T(8,128)(2,1)} %get-tuple-element.133), calls=%async_computation | async-start | bytes 4194304 | tf_op jit(solution)/shard_map/all_to_all | solution.py:566
  (18 other events, 71.2 us)

commit v5 on v4

--- a/solution.py
+++ b/solution.py
@@ -182,20 +182,21 @@
 
 def parts_of(at, own, other, mine, theirs, half, dtypes, tokens):
     count = len(dtypes)
+    rows = 2 * ROWS if count == 1 else ROWS
 
     def weight_spec(turn):
         return pl.BlockSpec((1, PART, WIDE), lambda i, s: (s[turn], 0, half))
 
     grid_spec = pltpu.PrefetchScalarGridSpec(
         num_scalar_prefetch=1,
-        grid=(SEQ // ROWS,),
+        grid=(SEQ // rows,),
         in_specs=[
-            pl.BlockSpec((ROWS, PART), lambda i, s: (i, 0)),
-            pl.BlockSpec((ROWS, PART), lambda i, s: (i, 0)),
+            pl.BlockSpec((rows, PART), lambda i, s: (i, 0)),
+            pl.BlockSpec((rows, PART), lambda i, s: (i, 0)),
             *[weight_spec(turn) for turn in range(count) for _ in range(2)],
             *later(tokens),
         ],
-        out_specs=[pl.BlockSpec((ROWS, WIDE), lambda i, s: (i, 0))] * count,
+        out_specs=[pl.BlockSpec((rows, WIDE), lambda i, s: (i, 0))] * count,
     )
     return pl.pallas_call(
         functools.partial(part_kernel, count),

time: 314 us -> 313 us (level)
  transfers between devices with their start and end apart: 37 -> 37, of which waited for: 18 -> 18; matrix products, arithmetic and copies ran while one was open for 12% -> 12% of each run, Pallas kernels for 24% -> 23%
where the time goes in v5:
time: 313 us; the launch traced here: 312 us
  waiting for transfers between devices  104 us (33%)
  Pallas kernels  91.3 us (29%)
  starting transfers between devices  69.4 us (22%)
  other arithmetic  24.5 us (8%)
  local copies, waits for them, and re-layouts  21.1 us (7%)
    ppermute x9, waiting for transfers between devices, ring_x(): return lax.ppermute(value, ('dp', 'tensor'), pairs)  49.2 us
    pallas_call x5, Pallas kernels, parts_of(): pl.pallas_call(functools.partial(part_kernel, count), grid_spec=grid_spec...  39.9 us
    pallas_call x2, Pallas kernels, attend(): pl.pallas_call(body, grid_spec=grid_spec, out_shape=jax.ShapeDtypeStruct(...  25.1 us
    ppermute x7, waiting for transfers between devices, swap_tensor(): return lax.ppermute(value, 'tensor', [(t, t ^ bits) for t in range(8)])  21.3 us
    ppermute x8, starting transfers between devices, swap_dp(): return lax.ppermute(value, 'dp', [(d, d ^ bits) for d in range(16)])  16.4 us
    all_to_all x2, waiting for transfers between devices, local(): lax.all_to_all(slots, 'dp', split_axis=0, concat_axis=0, tiled=True)  15.5 us
    ppermute x6, waiting for transfers between devices, shift_z(): lax.ppermute(value, 'dp', [(d, (d + 4 * step) % 16) for d in range(16)])  14.1 us
    pallas_call x2, Pallas kernels, norm_rows(): pl.pallas_call(functools.partial(norm_kernel, bounds, begin), grid_spec=g...  12.3 us
  transfers between devices with their start and end apart: 37, of which 18 were waited for; matrix products, arithmetic and copies ran while one was open for 12% of the time, Pallas kernels for 23%

profile of v5, /device:TPU:1, one launch (start us, length us, event | category | flops | bytes accessed | tf_op | source)
XLA Modules:
  0.0 311.5 jit_solution(10603059394835862972)
XLA Ops:
  0.0 2.1 collective-permute-start.3
  2.1 2.3 slice.32
  4.4 2.6 collective-permute-start
  7.0 2.6 multiply_reduce_fusion
  10.8 1.9 multiply_reduce_fusion.1
  14.0 5.4 %collective-permute-start.1 = (bf16[512,512]{1,0:T(8,128)(2,1)}, bf16[512,512]{1,0:T(8,128)(2,1)}, u32[]{:S(2)}, u32[]{:S(2)}) collective-permute-start(bf16[512,512]{1,0:T(8,128)(2,1)} %param.13), channel_id=1, source_target_pairs={{0,0},{1,1},{2,34},{3,35},{4,68},{5,69},{6,102},{7,103},{8,8},{9,9... | collective-permute-start | bytes 1572872 | tf_op jit(solution)/shard_map/ppermute | solution.py:94
  19.4 7.6 %reshape.79 = bf16[4,2,2,512,256]{4,3,2,1,0:T(8,128)(2,1)} reshape(bf16[8192,2,128]{2,1,0:T(2,128)(2,1)} %param.14) | data formatting | bytes 8388608 | tf_op jit(solution)/shard_map/reshape | solution.py:445
  33.4 5.4 %collective-permute-start.6 = (bf16[512,512]{1,0:T(8,128)(2,1)}, bf16[512,512]{1,0:T(8,128)(2,1)}, u32[]{:S(2)}, u32[]{:S(2)}) collective-permute-start(bf16[512,512]{1,0:T(8,128)(2,1)} %collective-permute-done.1), channel_id=1, source_target_pairs={{0,0},{1,1},{2,2},{3,3},{4,4},{5,5},{6,6},{7,7},{8,8},{9,9},{10,10... | collective-permute-start | bytes 1572872 | tf_op jit(solution)/shard_map/ppermute | solution.py:102
  38.8 2.6 collective-permute-start.8
  41.3 3.4 %fusion.2 = (f32[1792,64]{1,0:T(8,128)S(1)}, f32[1792,64]{1,0:T(8,128)S(1)}, f32[1792,64]{1,0:T(8,128)S(1)}) fusion(f32[64]{0:T(128)S(1)} %multiply_power_fusion), kind=kLoop, calls=%fused_computation.24 | loop fusion | flops 229376 | bytes 1376512 | tf_op jit(solution)/shard_map/neg | solution.py:43
  46.0 1.9 collective-permute-start.7
  49.2 4.8 %collective-permute-done.7 = f32[7,256]{1,0:T(8,128)S(1)} collective-permute-done((f32[7,256]{1,0:T(8,128)S(1)}, f32[7,256]{1,0:T(8,128)S(1)}, u32[]{:S(2)}, u32[]{:S(2)}) %collective-permute-start.7) | collective-permute-done | bytes 7200 | tf_op jit(solution)/shard_map/ppermute | solution.py:55
  54.4 4.6 %collective-permute-done.5.refs_1_ = bf16[512,1024]{1,0:T(8,128)(2,1)S(1)} collective-permute-done((bf16[512,1024]{1,0:T(8,128)(2,1)S(1)}, bf16[512,1024]{1,0:T(8,128)(2,1)S(1)}, u32[]{:S(2)}, u32[]{:S(2)}) %collective-permute-start.5) | collective-permute-done | bytes 1048608 | tf_op jit(solution)/shard_map/ppermute | solution.py:55
  60.5 3.4 %collective-permute-start.13 = (bf16[1024,256]{1,0:T(8,128)(2,1)}, bf16[1024,256]{1,0:T(8,128)(2,1)S(1)}, u32[]{:S(2)}, u32[]{:S(2)}) collective-permute-start(bf16[1024,256]{1,0:T(8,128)(2,1)} %pad_maximum_fusion.9), channel_id=1, source_target_pairs={{0,4},{1,5},{2,6},{3,7},{4,0},{5,1},{6,2},{7,3},{8,12},{9,13},{10,... | collective-permute-start | bytes 1572872 | tf_op jit(solution)/shard_map/ppermute | solution.py:51
  63.9 2.2 collective-permute-start.10
  67.2 3.9 %collective-permute-done.12 = f32[7,256]{1,0:T(8,128)S(1)} collective-permute-done((f32[7,256]{1,0:T(8,128)S(1)}, f32[7,256]{1,0:T(8,128)S(1)}, u32[]{:S(2)}, u32[]{:S(2)}) %collective-permute-start.12) | collective-permute-done | bytes 7200 | tf_op jit(solution)/shard_map/ppermute | solution.py:55
  74.9 7.4 %collective-permute-done.10.refs_2_ = bf16[256,1024]{1,0:T(8,128)(2,1)S(1)} collective-permute-done((bf16[256,1024]{1,0:T(8,128)(2,1)S(1)}, bf16[256,1024]{1,0:T(8,128)(2,1)S(1)}, u32[]{:S(2)}, u32[]{:S(2)}) %collective-permute-start.10) | collective-permute-done | bytes 524320 | tf_op jit(solution)/shard_map/ppermute | solution.py:55
  84.8 2.7 collective-permute-start.15
  87.5 2.4 collective-permute-start.14
  90.0 3.1 collective-permute-start.16
  94.5 5.8 %collective-permute-start.17 = (s32[8,6]{1,0:T(8,128)S(1)}, s32[8,6]{1,0:T(8,128)S(1)}, u32[]{:S(2)}, u32[]{:S(2)}) collective-permute-start(s32[8,6]{1,0:T(8,128)S(1)} %pad_add_fusion), channel_id=1, source_target_pairs={{0,64},{8,72},{16,80},{24,88},{32,96},{40,104},{48,112},{56,120},{... | collective-permute-start | bytes 584 | tf_op jit(solution)/shard_map/ppermute | solution.py:59
  100.3 2.2 fusion.5
  107.6 5.8 %norm_rows.3.own = bf16[1792,1024]{1,0:T(8,128)(2,1)} custom-call(s32[2]{0:T(128)S(1)} %pad_add_fusion.6.picks, bf16[1536,1024]{1,0:T(8,128)(2,1)S(1)} %copy-done, bf16[1792,1024]{1,0:T(8,128)(2,1)} %refs_1_.1, f32[1792,1]{1,0:T(8,128)S(1)} %bitcast.53, f32[1,1024]{1,0:T(1,128)S(1)} %get-tuple-element.159.refs_3_), custom_call_target="tpu_custom_call" | custom-call | tf_op jit(solution)/shard_map/norm_rows/pallas_call | solution.py:155
  114.1 6.5 %norm_rows.2.other = bf16[1792,1024]{1,0:T(8,128)(2,1)} custom-call(s32[2]{0:T(128)S(1)} %pad_add_fusion.5.picks, bf16[512,1024]{1,0:T(8,128)(2,1)} %collective-permute-done.refs_0_, bf16[512,1024]{1,0:T(8,128)(2,1)S(1)} %copy-done.10, bf16[256,1024]{1,0:T(8,128)(2,1)S(1)} %copy-done.13, bf16[512,1024]{1,0:T(8,128)(2,1)} %collective-permute-done.14.refs_3_, ...), custom_call_target="tpu_custom_call" | custom-call | tf_op jit(solution)/shard_map/norm_rows/pallas_call | solution.py:155
  120.6 8.8 %collective-permute-done.18 = bf16[1024,256]{1,0:T(8,128)(2,1)} collective-permute-done((bf16[1024,256]{1,0:T(8,128)(2,1)}, bf16[1024,256]{1,0:T(8,128)(2,1)}, u32[]{:S(2)}, u32[]{:S(2)}) %collective-permute-start.18) | collective-permute-done | bytes 524320 | tf_op jit(solution)/shard_map/ppermute | solution.py:86
  129.4 1.8 pad_maximum_fusion.1.rest_0_.rest_2_.rest_4_
  131.9 4.7 %part_rows.5.rest_2_ = bf16[1792,256]{1,0:T(8,128)(2,1)S(1)} custom-call(s32[1]{0:T(128)} %bitcast.29.at, bf16[1792,1024]{1,0:T(8,128)(2,1)} %norm_rows.3.own, bf16[1792,1024]{1,0:T(8,128)(2,1)} %norm_rows.2.other, bf16[4,1024,256]{2,1,0:T(8,128)(2,1)} %pad_maximum_fusion.rest_0_.rest_2_.rest_4_, ...), custom_call_target="tpu_custom_call" | custom-call | flops 1879048192 | bytes 7340032 | tf_op jit(solution)/shard_map/part_rows/pallas_call | solution.py:201
  136.5 1.9 collective-permute-start.25
  138.5 4.5 %part_rows.6.rest_6_ = bf16[1792,256]{1,0:T(8,128)(2,1)S(1)} custom-call(s32[1]{0:T(128)} %bitcast.21.at, bf16[1792,1024]{1,0:T(8,128)(2,1)} %norm_rows.3.own, bf16[1792,1024]{1,0:T(8,128)(2,1)} %norm_rows.2.other, bf16[4,1024,256]{2,1,0:T(8,128)(2,1)S(1)} %pad_maximum_fusion.1.rest_0_.rest_2_.rest_4_, ...), custom_call_target="tpu_custom_call" | custom-call | flops 1879048192 | bytes 7340032 | tf_op jit(solution)/shard_map/part_rows/pallas_call | solution.py:201
  145.4 9.5 %part_rows.7 = (bf16[1792,256]{1,0:T(8,128)(2,1)S(1)}, bf16[1792,256]{1,0:T(8,128)(2,1)S(1)}, f32[1792,256]{1,0:T(8,128)S(1)}) custom-call(s32[3]{0:T(128)S(1)} %get-tuple-element.169.at, bf16[1792,1024]{1,0:T(8,128)(2,1)} %norm_rows.3.own, bf16[1792,1024]{1,0:T(8,128)(2,1)} %norm_rows.2.other, ...), custom_call_target="tpu_custom_call" | custom-call | flops 5637144576 | bytes 7340032 | tf_op jit(solution)/shard_map/part_rows/pallas_call | solution.py:201
  155.8 9.5 %part_rows.8 = (bf16[1792,256]{1,0:T(8,128)(2,1)S(1)}, bf16[1792,256]{1,0:T(8,128)(2,1)S(1)}, f32[1792,256]{1,0:T(8,128)S(1)}) custom-call(s32[3]{0:T(128)S(1)} %get-tuple-element.168.at, bf16[1792,1024]{1,0:T(8,128)(2,1)} %norm_rows.3.own, bf16[1792,1024]{1,0:T(8,128)(2,1)} %norm_rows.2.other, bf16[4,1024,256]{2,1,0:T(8,128)(2,1)} %copy-done.1, ...), custom_call_target="tpu_custom_call" | custom-call | flops 5637144576 | bytes 7340032 | tf_op jit(solution)/shard_map/part_rows/pallas_call | solution.py:201
  165.3 5.2 %collective-permute-done.22 = bf16[1024,256]{1,0:T(8,128)(2,1)S(1)} collective-permute-done((bf16[1024,256]{1,0:T(8,128)(2,1)S(1)}, bf16[1024,256]{1,0:T(8,128)(2,1)S(1)}, u32[]{:S(2)}, u32[]{:S(2)}) %collective-permute-start.22) | collective-permute-done | bytes 524320 | tf_op jit(solution)/shard_map/ppermute | solution.py:86
  173.7 10.6 %collective-permute-done.31 = bf16[1792,256]{1,0:T(8,128)(2,1)S(1)} collective-permute-done((bf16[1792,256]{1,0:T(8,128)(2,1)S(1)}, bf16[1792,256]{1,0:T(8,128)(2,1)S(1)}, u32[]{:S(2)}, u32[]{:S(2)}) %collective-permute-start.31) | collective-permute-done | bytes 917536 | tf_op jit(solution)/shard_map/ppermute | solution.py:82
  187.0 11.8 %part_rows.9 = (bf16[1792,256]{1,0:T(8,128)(2,1)S(1)}, bf16[1792,256]{1,0:T(8,128)(2,1)S(1)}, bf16[1792,256]{1,0:T(8,128)(2,1)S(1)}, f32[1792,256]{1,0:T(8,128)S(1)}) custom-call(s32[4]{0:T(128)S(1)} %pad_add_fusion.8.at, bf16[1792,1024]{1,0:T(8,128)(2,1)} %norm_rows.3.own, bf16[1792,1024]{1,0:T(8,128)(2,1)} %norm_rows.2.other, ...), custom_call_target="tpu_custom_call" | custom-call | flops 7516192768 | bytes 7340032 | tf_op jit(solution)/shard_map/part_rows/pallas_call | solution.py:201
  200.0 4.0 %collective-permute-done.32.refs_3_ = bf16[1792,256]{1,0:T(8,128)(2,1)S(1)} collective-permute-done((bf16[1792,256]{1,0:T(8,128)(2,1)S(1)}, bf16[1792,256]{1,0:T(8,128)(2,1)S(1)}, u32[]{:S(2)}, u32[]{:S(2)}) %collective-permute-start.32) | collective-permute-done | bytes 917536 | tf_op jit(solution)/shard_map/ppermute | solution.py:82
  203.9 6.3 %finish_rows.3 = (bf16[16,256,512]{2,1,0:T(8,128)(2,1)}, bf16[256,512]{1,0:T(8,128)(2,1)S(1)}) custom-call(s32[7]{0:T(128)S(1)} %get-tuple-element.166.dest, s32[7]{0:T(128)S(1)} %get-tuple-element.167.spots, f32[1792,256]{1,0:T(8,128)S(1)} %get-tuple-element.135.refs_0_, f32[1792,256]{1,0:T(8,128)} %copy-done.6, ...), custom_call_target="tpu_custom_call" | custom-call | flops 7340032 | bytes 9175040 | tf_op jit(solution)/shard_map/finish_rows/pallas_call | solution.py:262
  210.3 6.4 %all-to-all-start.1 = ((bf16[16,256,512]{2,1,0:T(8,128)(2,1)}), bf16[16,256,512]{2,1,0:T(8,128)(2,1)}, u32[]{:S(2)}, u32[]{:S(2)}) async-start(bf16[16,256,512]{2,1,0:T(8,128)(2,1)} %get-tuple-element.137), calls=%async_computation.1 | async-start | bytes 8388608 | tf_op jit(solution)/shard_map/all_to_all | solution.py:567
  216.7 12.8 %collective-permute-done.29 = bf16[1792,256]{1,0:T(8,128)(2,1)S(1)} collective-permute-done((bf16[1792,256]{1,0:T(8,128)(2,1)}, bf16[1792,256]{1,0:T(8,128)(2,1)S(1)}, u32[]{:S(2)}, u32[]{:S(2)}) %collective-permute-start.29) | collective-permute-done | bytes 917536 | tf_op jit(solution)/shard_map/ppermute | solution.py:82
  232.3 11.4 %collective-permute-done.33 = bf16[1792,256]{1,0:T(8,128)(2,1)S(1)} collective-permute-done((bf16[1792,256]{1,0:T(8,128)(2,1)S(1)}, bf16[1792,256]{1,0:T(8,128)(2,1)S(1)}, u32[]{:S(2)}, u32[]{:S(2)}) %collective-permute-start.33) | collective-permute-done | bytes 917536 | tf_op jit(solution)/shard_map/ppermute | solution.py:82
  244.0 2.5 collective-permute-start.34
  246.5 10.3 %collective-permute-done.34.refs_1_ = bf16[1792,256]{1,0:T(8,128)(2,1)S(1)} collective-permute-done((bf16[1792,256]{1,0:T(8,128)(2,1)S(1)}, bf16[1792,256]{1,0:T(8,128)(2,1)S(1)}, u32[]{:S(2)}, u32[]{:S(2)}) %collective-permute-start.34) | collective-permute-done | bytes 917536 | tf_op jit(solution)/shard_map/ppermute | solution.py:82
  256.9 3.8 %finish_rows.2 = (bf16[16,256,256]{2,1,0:T(8,128)(2,1)}, bf16[256,256]{1,0:T(8,128)(2,1)S(1)}) custom-call(s32[7]{0:T(128)S(1)} %get-tuple-element.166.dest, s32[7]{0:T(128)S(1)} %get-tuple-element.167.spots, f32[1792,256]{1,0:T(8,128)S(1)} %copy-done.8, bf16[1792,256]{1,0:T(8,128)(2,1)S(1)} %collective-permute-done.34.refs_1_, f32[1,256]{1,0:T(1,128)S(1)} %bitcast.56, ...), custom_call_target="tpu_custom_call" | custom-call | flops 3670016 | bytes 4587520 | tf_op jit(solution)/shard_map/finish_rows/pallas_call | solution.py:262
  260.7 5.8 %all-to-all-done.1.slots.refs_3_ = bf16[16,256,512]{2,1,0:T(8,128)(2,1)} async-done(((bf16[16,256,512]{2,1,0:T(8,128)(2,1)}), bf16[16,256,512]{2,1,0:T(8,128)(2,1)}, u32[]{:S(2)}, u32[]{:S(2)}) %all-to-all-start.1) | async-done | bytes 4194336 | tf_op jit(solution)/shard_map/all_to_all | solution.py:567
  266.4 5.9 %all-to-all-start = ((bf16[16,256,256]{2,1,0:T(8,128)(2,1)}), bf16[16,256,256]{2,1,0:T(8,128)(2,1)S(1)}, u32[]{:S(2)}, u32[]{:S(2)}) async-start(bf16[16,256,256]{2,1,0:T(8,128)(2,1)} %get-tuple-element.133), calls=%async_computation | async-start | bytes 4194304 | tf_op jit(solution)/shard_map/all_to_all | solution.py:567
  272.8 3.8 %gather_pair.1 = (bf16[1792,128]{1,0:T(8,128)(2,1)S(1)}, bf16[144,1792]{1,0:T(8,128)(2,1)S(1)}) custom-call(s32[7]{0:T(128)S(1)} %select_reduce_fusion.1.source.refs_0_, s32[1]{0:T(128)} %bitcast.1.text_at.refs_1_, bf16[16,256,512]{2,1,0:T(8,128)(2,1)} %all-to-all-done.1.slots.refs_3_, bf16[256,512]{1,0:T(8,128)(2,1)S(1)} %get-tuple-element.138.text.refs_4_), custom_call_target="tpu_custom_call" | custom-call | flops 458752 | bytes 1835008 | tf_op jit(solution)/shard_map/gather_pair/pallas_call | solution.py:305
  276.6 13.1 %attend.2.refs_7_ = bf16[1792,512]{1,0:T(8,128)(2,1)} custom-call(s32[7]{0:T(128)S(1)} %select_reduce_fusion.1.source.refs_0_, s32[1]{0:T(128)} %bitcast.1.text_at.refs_1_, s32[4]{0:T(128)S(1)} %bitcast.58, bf16[16,256,512]{2,1,0:T(8,128)(2,1)} %all-to-all-done.1.slots.refs_3_, bf16[256,512]{1,0:T(8,128)(2,1)S(1)} %get-tuple-element.138.text.refs_4_, ...), custom_call_target="tpu_custom_call" | custom-call | flops 3288334336 | bytes 2752512 | tf_op jit(solution)/shard_map/attend/pallas_call | solution.py:392
  289.7 9.8 %all-to-all-done.refs_3_ = bf16[16,256,256]{2,1,0:T(8,128)(2,1)S(1)} async-done(((bf16[16,256,256]{2,1,0:T(8,128)(2,1)}), bf16[16,256,256]{2,1,0:T(8,128)(2,1)S(1)}, u32[]{:S(2)}, u32[]{:S(2)}) %all-to-all-start) | async-done | bytes 2097184 | tf_op jit(solution)/shard_map/all_to_all | solution.py:567
  299.5 12.0 %attend.3 = bf16[1792,512]{1,0:T(8,128)(2,1)} custom-call(s32[7]{0:T(128)S(1)} %select_reduce_fusion.1.source.refs_0_, s32[1]{0:T(128)} %bitcast.1.text_at.refs_1_, s32[4]{0:T(128)S(1)} %bitcast.59, bf16[16,256,256]{2,1,0:T(8,128)(2,1)S(1)} %all-to-all-done.refs_3_, bf16[256,256]{1,0:T(8,128)(2,1)S(1)} %get-tuple-element.134.refs_4_, ...), custom_call_target="tpu_custom_call", output_to_operand_aliasing={{}: (7, {})} | custom-call | flops 3288334336 | bytes 2752512 | tf_op jit(solution)/shard_map/attend/pallas_call | solution.py:392
  (154 shorter events, 41.8 us)
Async XLA Ops:
  0.0 30.4 %collective-permute-start.3 = (s32[1,6]{1,0:T(1,128)}, s32[1,6]{1,0:T(1,128)S(1)}, u32[]{:S(2)}, u32[]{:S(2)}) collective-permute-start(s32[1,6]{1,0:T(1,128)} %param.19), channel_id=1, source_target_pairs={{0,16},{8,24},{16,0},{24,8},{32,48},{40,56},{48,32},{56,40},{64,80... | collective-permute-start | bytes 80 | tf_op jit(solution)/shard_map/ppermute | solution.py:59
  4.4 28.5 %collective-permute-start = (bf16[512,1024]{1,0:T(8,128)(2,1)}, bf16[512,1024]{1,0:T(8,128)(2,1)}, u32[]{:S(2)}, u32[]{:S(2)}) collective-permute-start(bf16[512,1024]{1,0:T(8,128)(2,1)} %slice.32), channel_id=1, source_target_pairs={{0,1},{1,0},{2,3},{3,2},{4,5},{5,4},{6,7},{7,6},{8,9},{9,8},{10,11... | collective-permute-start | bytes 3145736 | tf_op jit(solution)/shard_map/ppermute | solution.py:55
  12.7 20.1 %collective-permute-start.2 = (f32[7,256]{1,0:T(8,128)S(1)}, f32[7,256]{1,0:T(8,128)S(1)}, u32[]{:S(2)}, u32[]{:S(2)}) collective-permute-start(f32[7,256]{1,0:T(8,128)S(1)} %reshape.78), channel_id=1, source_target_pairs={{0,2},{1,3},{2,0},{3,1},{4,6},{5,7},{6,4},{7,5},{8,10},{9,11},{10,... | collective-permute-start | bytes 21512 | tf_op jit(solution)/shard_map/ppermute | solution.py:55
  14.0 18.8 %collective-permute-start.1 = (bf16[512,512]{1,0:T(8,128)(2,1)}, bf16[512,512]{1,0:T(8,128)(2,1)}, u32[]{:S(2)}, u32[]{:S(2)}) collective-permute-start(bf16[512,512]{1,0:T(8,128)(2,1)} %param.13), channel_id=1, source_target_pairs={{0,0},{1,1},{2,34},{3,35},{4,68},{5,69},{6,102},{7,103},{8,8},{9,9... | collective-permute-start | bytes 1572872 | tf_op jit(solution)/shard_map/ppermute | solution.py:94
  30.4 2.4 collective-permute-start.4
  33.0 26.0 %collective-permute-start.5 = (bf16[512,1024]{1,0:T(8,128)(2,1)S(1)}, bf16[512,1024]{1,0:T(8,128)(2,1)S(1)}, u32[]{:S(2)}, u32[]{:S(2)}) collective-permute-start(bf16[512,1024]{1,0:T(8,128)(2,1)S(1)} %slice.33), channel_id=1, source_target_pairs={{0,1},{1,0},{2,3},{3,2},{4,5},{5,4},{6,7},{7,6},{8,9},{9,8},{10,11... | collective-permute-start | bytes 3145736 | tf_op jit(solution)/shard_map/ppermute | solution.py:55
  33.4 20.5 %collective-permute-start.6 = (bf16[512,512]{1,0:T(8,128)(2,1)}, bf16[512,512]{1,0:T(8,128)(2,1)}, u32[]{:S(2)}, u32[]{:S(2)}) collective-permute-start(bf16[512,512]{1,0:T(8,128)(2,1)} %collective-permute-done.1), channel_id=1, source_target_pairs={{0,0},{1,1},{2,2},{3,3},{4,4},{5,5},{6,6},{7,7},{8,8},{9,9},{10,10... | collective-permute-start | bytes 1572872 | tf_op jit(solution)/shard_map/ppermute | solution.py:102
  38.8 15.2 %collective-permute-start.8 = (bf16[1024,256]{1,0:T(8,128)(2,1)S(1)}, bf16[1024,256]{1,0:T(8,128)(2,1)S(1)}, u32[]{:S(2)}, u32[]{:S(2)}) collective-permute-start(bf16[1024,256]{1,0:T(8,128)(2,1)S(1)} %pad_maximum_fusion.10), channel_id=1, source_target_pairs={{0,6},{1,7},{2,0},{3,1},{4,2},{5,3},{6,4},{7,5},{8,14},{9,15},{10,... | collective-permute-start | bytes 1572872 | tf_op jit(solution)/shard_map/ppermute | solution.py:51
  41.3 13.1 %collective-permute-start.9 = (bf16[1024,256]{1,0:T(8,128)(2,1)S(1)}, bf16[1024,256]{1,0:T(8,128)(2,1)S(1)}, u32[]{:S(2)}, u32[]{:S(2)}) collective-permute-start(bf16[1024,256]{1,0:T(8,128)(2,1)S(1)} %pad_maximum_fusion.8), channel_id=1, source_target_pairs={{0,2},{1,3},{2,4},{3,5},{4,6},{5,7},{6,0},{7,1},{8,10},{9,11},{10,... | collective-permute-start | bytes 1572872 | tf_op jit(solution)/shard_map/ppermute | solution.py:51
  46.0 7.9 %collective-permute-start.7 = (f32[7,256]{1,0:T(8,128)S(1)}, f32[7,256]{1,0:T(8,128)S(1)}, u32[]{:S(2)}, u32[]{:S(2)}) collective-permute-start(f32[7,256]{1,0:T(8,128)S(1)} %add.194), channel_id=1, source_target_pairs={{0,4},{1,5},{2,6},{3,7},{4,0},{5,1},{6,2},{7,3},{8,12},{9,13},{10,... | collective-permute-start | bytes 21512 | tf_op jit(solution)/shard_map/ppermute | solution.py:55
  60.0 12.6 %collective-permute-start.11 = (bf16[512,512]{1,0:T(8,128)(2,1)}, bf16[512,512]{1,0:T(8,128)(2,1)}, u32[]{:S(2)}, u32[]{:S(2)}) collective-permute-start(bf16[512,512]{1,0:T(8,128)(2,1)} %collective-permute-done.6), channel_id=1, source_target_pairs={{0,16},{8,24},{16,0},{24,8},{32,48},{40,56},{48,32},{56,40},{64,80... | collective-permute-start | bytes 1572872 | tf_op jit(solution)/shard_map/ppermute | solution.py:59
  60.0 11.1 %collective-permute-start.12 = (f32[7,256]{1,0:T(8,128)S(1)}, f32[7,256]{1,0:T(8,128)S(1)}, u32[]{:S(2)}, u32[]{:S(2)}) collective-permute-start(f32[7,256]{1,0:T(8,128)S(1)} %add.210), channel_id=1, source_target_pairs={{0,1},{1,0},{2,3},{3,2},{4,5},{5,4},{6,7},{7,6},{8,9},{9,8},{10,11... | collective-permute-start | bytes 21512 | tf_op jit(solution)/shard_map/ppermute | solution.py:55
  60.5 14.4 %collective-permute-start.13 = (bf16[1024,256]{1,0:T(8,128)(2,1)}, bf16[1024,256]{1,0:T(8,128)(2,1)S(1)}, u32[]{:S(2)}, u32[]{:S(2)}) collective-permute-start(bf16[1024,256]{1,0:T(8,128)(2,1)} %pad_maximum_fusion.9), channel_id=1, source_target_pairs={{0,4},{1,5},{2,6},{3,7},{4,0},{5,1},{6,2},{7,3},{8,12},{9,13},{10,... | collective-permute-start | bytes 1572872 | tf_op jit(solution)/shard_map/ppermute | solution.py:51
  63.9 18.4 %collective-permute-start.10 = (bf16[256,1024]{1,0:T(8,128)(2,1)S(1)}, bf16[256,1024]{1,0:T(8,128)(2,1)S(1)}, u32[]{:S(2)}, u32[]{:S(2)}) collective-permute-start(bf16[256,1024]{1,0:T(8,128)(2,1)S(1)} %get-tuple-element.154), channel_id=1, source_target_pairs={{0,1},{1,0},{2,3},{3,2},{4,5},{5,4},{6,7},{7,6},{8,9},{9,8},{10,11... | collective-permute-start | bytes 1572872 | tf_op jit(solution)/shard_map/ppermute | solution.py:55
  71.1 12.1 %copy-start.18 = (bf16[1024,256]{1,0:T(8,128)(2,1)S(1)}, bf16[1024,256]{1,0:T(8,128)(2,1)}, u32[]{:S(2)}) copy-start(bf16[1024,256]{1,0:T(8,128)(2,1)} %pad_maximum_fusion.7) | copy-start | bytes 1572868
  71.1 12.1 %copy-start.21 = (bf16[1024,256]{1,0:T(8,128)(2,1)S(1)}, bf16[1024,256]{1,0:T(8,128)(2,1)}, u32[]{:S(2)}) copy-start(bf16[1024,256]{1,0:T(8,128)(2,1)} %copy-done.20) | copy-start | bytes 1572868
  71.1 12.1 %copy-start.23 = (bf16[1024,256]{1,0:T(8,128)(2,1)S(1)}, bf16[1024,256]{1,0:T(8,128)(2,1)}, u32[]{:S(2)}) copy-start(bf16[1024,256]{1,0:T(8,128)(2,1)} %copy-done.22) | copy-start | bytes 1572868
  84.8 44.6 %collective-permute-start.15 = (bf16[4,1024,256]{2,1,0:T(8,128)(2,1)}, bf16[4,1024,256]{2,1,0:T(8,128)(2,1)}, u32[]{:S(2)}, u32[]{:S(2)}) collective-permute-start(bf16[4,1024,256]{2,1,0:T(8,128)(2,1)} %pad_maximum_fusion.rest_0_.rest_2_.rest_4_), channel_id=1, source_target_pairs={{0,8},{8,0},{16,24},{24,16},{32,40},{40,32},{48,56},{56,48},{64,72... | collective-permute-start | bytes 6291464 | tf_op jit(solution)/shard_map/ppermute | solution.py:59
  87.5 26.6 %collective-permute-start.14 = (bf16[512,1024]{1,0:T(8,128)(2,1)}, bf16[512,1024]{1,0:T(8,128)(2,1)}, u32[]{:S(2)}, u32[]{:S(2)}) collective-permute-start(bf16[512,1024]{1,0:T(8,128)(2,1)} %pad_maximum_fusion.4), channel_id=1, source_target_pairs={{0,1},{1,0},{2,3},{3,2},{4,5},{5,4},{6,7},{7,6},{8,9},{9,8},{10,11... | collective-permute-start | bytes 3145736 | tf_op jit(solution)/shard_map/ppermute | solution.py:55
  90.0 4.5 %collective-permute-start.16 = (s32[4,6]{1,0:T(4,128)S(1)}, s32[4,6]{1,0:T(4,128)S(1)}, u32[]{:S(2)}, u32[]{:S(2)}) collective-permute-start(s32[4,6]{1,0:T(4,128)S(1)} %pad_add_fusion.2), channel_id=1, source_target_pairs={{0,32},{8,40},{16,48},{24,56},{32,0},{40,8},{48,16},{56,24},{64,96... | collective-permute-start | bytes 296 | tf_op jit(solution)/shard_map/ppermute | solution.py:59
  94.5 9.3 %collective-permute-start.17 = (s32[8,6]{1,0:T(8,128)S(1)}, s32[8,6]{1,0:T(8,128)S(1)}, u32[]{:S(2)}, u32[]{:S(2)}) collective-permute-start(s32[8,6]{1,0:T(8,128)S(1)} %pad_add_fusion), channel_id=1, source_target_pairs={{0,64},{8,72},{16,80},{24,88},{32,96},{40,104},{48,112},{56,120},{... | collective-permute-start | bytes 584 | tf_op jit(solution)/shard_map/ppermute | solution.py:59
  102.5 18.0 %collective-permute-start.20 = (bf16[1024,256]{1,0:T(8,128)(2,1)}, bf16[1024,256]{1,0:T(8,128)(2,1)}, u32[]{:S(2)}, u32[]{:S(2)}) collective-permute-start(bf16[1024,256]{1,0:T(8,128)(2,1)} %get-tuple-element.99), channel_id=1, source_target_pairs={{0,96},{8,104},{16,112},{24,120},{32,0},{40,8},{48,16},{56,24},{64... | collective-permute-start | bytes 1572872 | tf_op jit(solution)/shard_map/ppermute | solution.py:86
  102.5 18.0 %collective-permute-start.19 = (bf16[1024,256]{1,0:T(8,128)(2,1)}, bf16[1024,256]{1,0:T(8,128)(2,1)}, u32[]{:S(2)}, u32[]{:S(2)}) collective-permute-start(bf16[1024,256]{1,0:T(8,128)(2,1)} %get-tuple-element.99), channel_id=1, source_target_pairs={{0,64},{8,72},{16,80},{24,88},{32,96},{40,104},{48,112},{56,120},{... | collective-permute-start | bytes 1572872 | tf_op jit(solution)/shard_map/ppermute | solution.py:86
  103.7 25.7 %collective-permute-start.18 = (bf16[1024,256]{1,0:T(8,128)(2,1)}, bf16[1024,256]{1,0:T(8,128)(2,1)}, u32[]{:S(2)}, u32[]{:S(2)}) collective-permute-start(bf16[1024,256]{1,0:T(8,128)(2,1)} %get-tuple-element.99), channel_id=1, source_target_pairs={{0,32},{8,40},{16,48},{24,56},{32,64},{40,72},{48,80},{56,88},{64,... | collective-permute-start | bytes 1572872 | tf_op jit(solution)/shard_map/ppermute | solution.py:86
  131.2 7.2 %copy-start.1 = (bf16[4,1024,256]{2,1,0:T(8,128)(2,1)}, bf16[4,1024,256]{2,1,0:T(8,128)(2,1)S(1)}, u32[]{:S(2)}) copy-start(bf16[4,1024,256]{2,1,0:T(8,128)(2,1)S(1)} %pad_maximum_fusion.1.rest_0_.rest_2_.rest_4_) | copy-start | bytes 6291460
  131.2 7.2 %collective-permute-start.21 = (bf16[4,1024,256]{2,1,0:T(8,128)(2,1)S(1)}, bf16[4,1024,256]{2,1,0:T(8,128)(2,1)}, u32[]{:S(2)}, u32[]{:S(2)}) collective-permute-start(bf16[4,1024,256]{2,1,0:T(8,128)(2,1)S(1)} %pad_maximum_fusion.1.rest_0_.rest_2_.rest_4_), channel_id=1, source_target_pairs={{0,8},{8,0},{16,24},{24,16},{32,40},{40,32},{48,56},{56,48},{64,72... | collective-permute-start | bytes 6291464 | tf_op jit(solution)/shard_map/ppermute | solution.py:59
  131.9 6.6 %copy-start.28 = (s32[16]{0:T(128)S(1)}, s32[16]{0:T(128)}, u32[]{:S(2)}) copy-start(s32[16]{0:T(128)} %constant.481.clone) | copy-start | bytes 196
  136.5 18.4 %collective-permute-start.25 = (bf16[1792,256]{1,0:T(8,128)(2,1)S(1)}, bf16[1792,256]{1,0:T(8,128)(2,1)S(1)}, u32[]{:S(2)}, u32[]{:S(2)}) collective-permute-start(bf16[1792,256]{1,0:T(8,128)(2,1)S(1)} %part_rows.5.rest_2_), channel_id=1, source_target_pairs={{0,2},{1,3},{2,4},{3,5},{4,6},{5,7},{6,0},{7,1},{8,14},{9,15},{10,... | collective-permute-start | bytes 2752520 | tf_op jit(solution)/shard_map/ppermute | solution.py:82
  143.0 22.3 %collective-permute-start.24 = (bf16[1024,256]{1,0:T(8,128)(2,1)S(1)}, bf16[1024,256]{1,0:T(8,128)(2,1)S(1)}, u32[]{:S(2)}, u32[]{:S(2)}) collective-permute-start(bf16[1024,256]{1,0:T(8,128)(2,1)S(1)} %copy-done.19), channel_id=1, source_target_pairs={{0,96},{8,104},{16,112},{24,120},{32,0},{40,8},{48,16},{56,24},{64... | collective-permute-start | bytes 1572872 | tf_op jit(solution)/shard_map/ppermute | solution.py:86
  143.9 21.4 %collective-permute-start.23 = (bf16[1024,256]{1,0:T(8,128)(2,1)S(1)}, bf16[1024,256]{1,0:T(8,128)(2,1)S(1)}, u32[]{:S(2)}, u32[]{:S(2)}) collective-permute-start(bf16[1024,256]{1,0:T(8,128)(2,1)S(1)} %copy-done.19), channel_id=1, source_target_pairs={{0,64},{8,72},{16,80},{24,88},{32,96},{40,104},{48,112},{56,120},{... | collective-permute-start | bytes 1572872 | tf_op jit(solution)/shard_map/ppermute | solution.py:86
  144.5 26.0 %collective-permute-start.22 = (bf16[1024,256]{1,0:T(8,128)(2,1)S(1)}, bf16[1024,256]{1,0:T(8,128)(2,1)S(1)}, u32[]{:S(2)}, u32[]{:S(2)}) collective-permute-start(bf16[1024,256]{1,0:T(8,128)(2,1)S(1)} %copy-done.19), channel_id=1, source_target_pairs={{0,32},{8,40},{16,48},{24,56},{32,64},{40,72},{48,80},{56,88},{64,... | collective-permute-start | bytes 1572872 | tf_op jit(solution)/shard_map/ppermute | solution.py:86
  145.1 26.2 %collective-permute-start.30 = (bf16[1792,256]{1,0:T(8,128)(2,1)S(1)}, bf16[1792,256]{1,0:T(8,128)(2,1)S(1)}, u32[]{:S(2)}, u32[]{:S(2)}) collective-permute-start(bf16[1792,256]{1,0:T(8,128)(2,1)S(1)} %part_rows.6.rest_6_), channel_id=1, source_target_pairs={{0,2},{1,3},{2,4},{3,5},{4,6},{5,7},{6,0},{7,1},{8,14},{9,15},{10,... | collective-permute-start | bytes 2752520 | tf_op jit(solution)/shard_map/ppermute | solution.py:82
  155.2 17.6 %collective-permute-start.27 = (bf16[1792,256]{1,0:T(8,128)(2,1)S(1)}, bf16[1792,256]{1,0:T(8,128)(2,1)S(1)}, u32[]{:S(2)}, u32[]{:S(2)}) collective-permute-start(bf16[1792,256]{1,0:T(8,128)(2,1)S(1)} %add_convert_fusion.5.rest_6_), channel_id=1, source_target_pairs={{0,2},{1,3},{2,4},{3,5},{4,6},{5,7},{6,0},{7,1},{8,14},{9,15},{10,... | collective-permute-start | bytes 2752520 | tf_op jit(solution)/shard_map/ppermute | solution.py:82
  170.8 16.1 %collective-permute-start.26 = (bf16[4,1024,256]{2,1,0:T(8,128)(2,1)S(1)}, bf16[4,1024,256]{2,1,0:T(8,128)(2,1)}, u32[]{:S(2)}, u32[]{:S(2)}) collective-permute-start(bf16[4,1024,256]{2,1,0:T(8,128)(2,1)S(1)} %pad_maximum_fusion.2.rest_0_.rest_2_.rest_4_.rest_6_), channel_id=1, source_target_pairs={{0,8},{8,0},{16,24},{24,16},{32,40},{40,32},{48,56},{56,48},{64,72... | collective-permute-start | bytes 6291464 | tf_op jit(solution)/shard_map/ppermute | solution.py:59
  171.7 12.6 %collective-permute-start.31 = (bf16[1792,256]{1,0:T(8,128)(2,1)S(1)}, bf16[1792,256]{1,0:T(8,128)(2,1)S(1)}, u32[]{:S(2)}, u32[]{:S(2)}) collective-permute-start(bf16[1792,256]{1,0:T(8,128)(2,1)S(1)} %add_convert_fusion.3), channel_id=1, source_target_pairs={{0,2},{1,3},{2,4},{3,5},{4,6},{5,7},{6,0},{7,1},{8,14},{9,15},{10,... | collective-permute-start | bytes 2752520 | tf_op jit(solution)/shard_map/ppermute | solution.py:82
  173.1 26.8 %collective-permute-start.28 = (bf16[1792,256]{1,0:T(8,128)(2,1)S(1)}, bf16[1792,256]{1,0:T(8,128)(2,1)S(1)}, u32[]{:S(2)}, u32[]{:S(2)}) collective-permute-start(bf16[1792,256]{1,0:T(8,128)(2,1)S(1)} %add_convert_fusion.4), channel_id=1, source_target_pairs={{0,2},{1,3},{2,4},{3,5},{4,6},{5,7},{6,0},{7,1},{8,14},{9,15},{10,... | collective-permute-start | bytes 2752520 | tf_op jit(solution)/shard_map/ppermute | solution.py:82
  184.5 19.4 %collective-permute-start.32 = (bf16[1792,256]{1,0:T(8,128)(2,1)S(1)}, bf16[1792,256]{1,0:T(8,128)(2,1)S(1)}, u32[]{:S(2)}, u32[]{:S(2)}) collective-permute-start(bf16[1792,256]{1,0:T(8,128)(2,1)S(1)} %add_convert_fusion.2), channel_id=1, source_target_pairs={{0,2},{1,3},{2,4},{3,5},{4,6},{5,7},{6,0},{7,1},{8,14},{9,15},{10,... | collective-permute-start | bytes 2752520 | tf_op jit(solution)/shard_map/ppermute | solution.py:82
  186.9 17.0 %copy-start.2 = (f32[1792,128]{1,0:T(8,128)S(1)}, f32[1792,128]{1,0:T(8,128)}, u32[]{:S(2)}) copy-start(f32[1792,128]{1,0:T(8,128)} %pad_maximum_fusion.5.refs_3_.refs_6_) | copy-start | bytes 2752516
  186.9 17.0 %copy-start.5 = (f32[1792,128]{1,0:T(8,128)S(1)}, f32[1792,128]{1,0:T(8,128)}, u32[]{:S(2)}) copy-start(f32[1792,128]{1,0:T(8,128)} %pad_maximum_fusion.6.refs_4_.refs_7_) | copy-start | bytes 2752516
  186.9 17.0 %copy-start.14 = (f32[2,128]{1,0:T(2,128)S(1)}, f32[2,128]{1,0:T(2,128)}, u32[]{:S(2)}) copy-start(f32[2,128]{1,0:T(2,128)} %param.16) | copy-start | bytes 3076
  200.0 10.3 %copy-start.11 = (bf16[1792,256]{1,0:T(8,128)(2,1)}, bf16[1792,256]{1,0:T(8,128)(2,1)S(1)}, u32[]{:S(2)}) copy-start(bf16[1792,256]{1,0:T(8,128)(2,1)S(1)} %get-tuple-element.127) | copy-start | bytes 2752516
  200.0 10.3 %copy-start.15 = (bf16[1792,256]{1,0:T(8,128)(2,1)}, bf16[1792,256]{1,0:T(8,128)(2,1)S(1)}, u32[]{:S(2)}) copy-start(bf16[1792,256]{1,0:T(8,128)(2,1)S(1)} %get-tuple-element.121) | copy-start | bytes 2752516
  210.3 56.2 %all-to-all-start.1 = ((bf16[16,256,512]{2,1,0:T(8,128)(2,1)}), bf16[16,256,512]{2,1,0:T(8,128)(2,1)}, u32[]{:S(2)}, u32[]{:S(2)}) async-start(bf16[16,256,512]{2,1,0:T(8,128)(2,1)} %get-tuple-element.137), calls=%async_computation.1 | async-start | bytes 8388608 | tf_op jit(solution)/shard_map/all_to_all | solution.py:567
  216.7 12.9 %collective-permute-start.29 = (bf16[1792,256]{1,0:T(8,128)(2,1)}, bf16[1792,256]{1,0:T(8,128)(2,1)S(1)}, u32[]{:S(2)}, u32[]{:S(2)}) collective-permute-start(bf16[1792,256]{1,0:T(8,128)(2,1)} %copy-done.15), channel_id=1, source_target_pairs={{0,2},{1,3},{2,4},{3,5},{4,6},{5,7},{6,0},{7,1},{8,14},{9,15},{10,... | collective-permute-start | bytes 2752520 | tf_op jit(solution)/shard_map/ppermute | solution.py:82
  229.5 27.4 %copy-start.8 = (f32[1792,256]{1,0:T(8,128)S(1)}, f32[1792,256]{1,0:T(8,128)}, u32[]{:S(2)}) copy-start(f32[1792,256]{1,0:T(8,128)} %copy-done.7) | copy-start | bytes 5505028
  231.1 12.7 %collective-permute-start.33 = (bf16[1792,256]{1,0:T(8,128)(2,1)S(1)}, bf16[1792,256]{1,0:T(8,128)(2,1)S(1)}, u32[]{:S(2)}, u32[]{:S(2)}) collective-permute-start(bf16[1792,256]{1,0:T(8,128)(2,1)S(1)} %add_convert_fusion.1), channel_id=1, source_target_pairs={{0,2},{1,3},{2,4},{3,5},{4,6},{5,7},{6,0},{7,1},{8,14},{9,15},{10,... | collective-permute-start | bytes 2752520 | tf_op jit(solution)/shard_map/ppermute | solution.py:82
  244.0 12.8 %collective-permute-start.34 = (bf16[1792,256]{1,0:T(8,128)(2,1)S(1)}, bf16[1792,256]{1,0:T(8,128)(2,1)S(1)}, u32[]{:S(2)}, u32[]{:S(2)}) collective-permute-start(bf16[1792,256]{1,0:T(8,128)(2,1)S(1)} %add_convert_fusion), channel_id=1, source_target_pairs={{0,2},{1,3},{2,4},{3,5},{4,6},{5,7},{6,0},{7,1},{8,14},{9,15},{10,... | collective-permute-start | bytes 2752520 | tf_op jit(solution)/shard_map/ppermute | solution.py:82
  266.4 33.0 %all-to-all-start = ((bf16[16,256,256]{2,1,0:T(8,128)(2,1)}), bf16[16,256,256]{2,1,0:T(8,128)(2,1)S(1)}, u32[]{:S(2)}, u32[]{:S(2)}) async-start(bf16[16,256,256]{2,1,0:T(8,128)(2,1)} %get-tuple-element.133), calls=%async_computation | async-start | bytes 4194304 | tf_op jit(solution)/shard_map/all_to_all | solution.py:567
  (18 other events, 70.5 us)
